TPU v7x, 512 devices: a whole 4x8x8 slice. The times are simulated.
512 devices in a mesh: row: 8 (over z), col: 16 (over y, core), rep: 4 (over x).
Axes of the slice: x: 4, y: 8, z: 8, core: 2. Of those that a mesh axis runs over, the one named last changes fastest.
Arguments:
- tile_values: bfloat16 [8, 16, 96, 128, 128], P('row', 'col'), may hold values from -0.078125 to 0.078125
- tile_rows: int32 [8, 16, 96], P('row', 'col'), may hold values from 0 to 31, as said below
- tile_cols: int32 [8, 16, 96], P('row', 'col'), may hold values from 0 to 15, as said below
- tile_count: int32 [8, 16], P('row', 'col'), may hold values from 24 to 96, as said below
- features: bfloat16 [32768, 512], P('col', 'rep'), may hold values from -6 to 6
- weight: bfloat16 [512, 512], P('rep'), may hold values from -0.25 to 0.25
- cotangent: bfloat16 [32768, 512], P(('row', 'col')), may hold values from -6 to 6
Outputs:
- activation: bfloat16 [32768, 512], P(('row', 'col'))
- weight_grad: float32 [512, 512], P('rep')
- input_grad: bfloat16 [32768, 512], P('col', 'rep')
Inputs may be any that keep to these rules, and one draw needn't show every extreme that they name: Row blocks lie below 32; within one grid block the slots hold distinct (tile_rows, tile_cols) pairs. `tile_cols`: column blocks lie below 16. `tile_count`: slots at or beyond a block's count hold no tile; some grid block uses all 96 slots.
All inputs are finite; a program needn't handle non-finite values.
Results may differ from a plain program's by a relative error of at most 0.006.
Values may be sent and summed in bfloat16 or wider, within the bound.
No kernel may reach another device: no remote copies, remote signals or barrier semaphores. Data moves between devices by JAX's collectives and lax.ppermute only.
A program may use at most 64 MiB of HBM per device.

v0:
```python
import math

import jax
import jax.numpy as jnp
from jax import lax
from jax.sharding import PartitionSpec as P


def block_sum(select, contrib):
    return jnp.einsum("bt,tif->bif", select, contrib, precision=lax.Precision.HIGHEST)


def body(tile_values, tile_rows, tile_cols, tile_count, features, weight, cotangent):
    values = tile_values[0, 0]
    row_ids = tile_rows[0, 0]
    col_ids = tile_cols[0, 0]
    used = tile_count[0, 0]
    side = values.shape[-1]
    slot_total = values.shape[0]
    width = features.shape[1]
    grains = cotangent.shape[0]
    row_blocks = lax.axis_size("col") * grains // side
    col_blocks = features.shape[0] // side
    live = jnp.arange(slot_total, dtype=jnp.int32) < used
    source = features.reshape(col_blocks, side, width)
    picked = jnp.take(source, col_ids, axis=0)
    contrib = jnp.einsum("tij,tjf->tif", values, picked, preferred_element_type=jnp.float32)
    select_rows = (
        (row_ids[None, :] == jnp.arange(row_blocks, dtype=jnp.int32)[:, None]) & live[None, :]
    ).astype(jnp.float32)
    partial_rows = block_sum(select_rows, contrib).reshape(row_blocks * side, width)
    aggregated = lax.psum_scatter(partial_rows, "col", scatter_dimension=0, tiled=True).astype(
        jnp.bfloat16
    )
    term = jnp.dot(aggregated, weight, preferred_element_type=jnp.float32)
    hidden = lax.psum(term, "rep")
    sigma = jax.nn.sigmoid(hidden)
    activation = (hidden * sigma).astype(jnp.bfloat16)
    slope = sigma * (1.0 + hidden * (1.0 - sigma))
    grad_hidden = (cotangent.astype(jnp.float32) * slope).astype(jnp.bfloat16)
    total_nodes = grains * lax.axis_size("row") * lax.axis_size("col")
    local_grad = lax.dot_general(
        aggregated, grad_hidden, (((0,), (0,)), ((), ())), preferred_element_type=jnp.float32
    ) * (1.0 / math.sqrt(total_nodes))
    weight_grad = lax.psum(local_grad, ("row", "col"))
    grad_agg = lax.dot_general(
        grad_hidden, weight, (((1,), (1,)), ((), ())), preferred_element_type=jnp.float32
    ).astype(jnp.bfloat16)
    grad_rowpart = lax.all_gather(grad_agg, "col", axis=0, tiled=True)
    grad_blocks = grad_rowpart.reshape(row_blocks, side, width)
    picked_back = jnp.take(grad_blocks, row_ids, axis=0)
    back = jnp.einsum("tji,tjf->tif", values, picked_back, preferred_element_type=jnp.float32)
    select_cols = (
        (col_ids[None, :] == jnp.arange(col_blocks, dtype=jnp.int32)[:, None]) & live[None, :]
    ).astype(jnp.float32)
    partial_cols = block_sum(select_cols, back).reshape(col_blocks * side, width)
    input_grad = lax.psum(partial_cols, "row").astype(jnp.bfloat16)
    return (activation, weight_grad, input_grad)


def solution(mesh):
    return jax.shard_map(
        body,
        mesh=mesh,
        in_specs=(
            P("row", "col", None, None, None),
            P("row", "col", None),
            P("row", "col", None),
            P("row", "col"),
            P("col", "rep"),
            P("rep", None),
            P(("row", "col"), None),
        ),
        out_specs=(P(("row", "col"), None), P("rep", None), P("col", "rep")),
        check_vma=False,
    )
```

profile of v0, /device:TPU:26, one launch (start us, length us, event | category | flops | bytes accessed | tf_op | source)
XLA Modules:
  0.0 402.4 jit_solution(14532733870149092276)
XLA Ops:
  7.2 0.0 copy-start
  7.2 0.0 reduce-scatter.2.cloned.1.call-start
  7.2 0.8 compare_and_fusion.1
  8.0 0.7 fusion.27
  9.5 3.8 gather_fusion
  13.2 0.0 copy-done
  13.3 7.0 %fusion.6 = f32[96,128,128]{2,1,0:T(8,128)} fusion(bf16[1,1,96,128,128]{4,3,2,1,0:T(8,128)(2,1)S(1)} %copy-done, bf16[96,128,128]{2,1,0:T(8,128)(2,1)} %gather_fusion, pred[96]{0:T(512)(128)(4,1)S(1)} %compare_and_fusion.1), kind=kOutput, calls=%fused_computation.8 | convolution fusion | flops 404226048 | bytes 12583008 | tf_op jit(solution)/shard_map/tij,tjf->tif/dot_general | solution.py:27
  20.3 0.0 copy-start.2
  20.3 6.7 %copy.12 = f32[96,128,128]{1,0,2:T(8,128)} copy(f32[96,128,128]{2,1,0:T(8,128)} %fusion.6) | data formatting | bytes 12582912 | tf_op jit(solution)/shard_map/tij,tjf->tif/dot_general | solution.py:27
  27.0 0.0 copy-done.2
  27.0 4.5 %fusion.2 = f32[32,128,128]{2,0,1:T(8,128)S(1)} fusion(f32[96,128,128]{1,0,2:T(8,128)} %copy.12, s32[96]{0:T(128)S(1)} %bitcast.43, pred[96]{0:T(512)(128)(4,1)S(1)} %iota_compare_fusion.2), kind=kOutput, calls=%fused_computation.4 | convolution fusion | flops 603985920 | bytes 8389088 | tf_op jit(solution)/shard_map/bt,tif->bif/dot_general | solution.py:10
  31.5 0.0 copy-start.1
  31.5 2.6 copy.10
  34.0 0.0 reduce-scatter.2.cloned.1.call-update
  34.0 0.0 all-reduce.4.cloned.1.call-start
  34.1 62.9 %reduce-scatter.2.cloned.1.call-done = f32[256,128]{1,0:T(8,128)} async-done(((f32[4096,128]{1,0:T(8,128)}), f32[256,128]{1,0:T(8,128)}) %reduce-scatter.2.cloned.1.call-update) | async-done | bytes 131088 | tf_op jit(solution)/shard_map/reduce_scatter | solution.py:32
  97.0 0.0 copy-done.1
  97.0 1.9 fusion.15
  98.9 0.0 all-reduce.4.cloned.1.call-update
  99.0 0.0 all-gather.2.cloned.1.call-start
  99.0 56.0 %all-reduce.4.cloned.1.call-done = f32[256,512]{1,0:T(8,128)} async-done(((f32[256,512]{1,0:T(8,128)}), f32[256,512]{1,0:T(8,128)}) %all-reduce.4.cloned.1.call-update) | async-done | bytes 524304 | tf_op jit(solution)/shard_map/psum | solution.py:36
  155.0 2.1 multiply_convert_fusion
  157.0 0.9 convolution_convert_fusion
  157.9 0.0 all-gather.2.cloned.1.call-update
  157.9 0.0 all-reduce.6.cloned.1.call-start
  158.0 1.8 convolution_multiply_fusion
  159.8 0.0 all-reduce.6.cloned.1.call-update
  159.8 40.6 %all-gather.2.cloned.1.call-done = bf16[4096,128]{1,0:T(8,128)(2,1)} async-done(((bf16[256,128]{1,0:T(8,128)(2,1)}), bf16[4096,128]{1,0:T(8,128)(2,1)}) %all-gather.2.cloned.1.call-update) | async-done | bytes 1048592 | tf_op jit(solution)/shard_map/all_gather | solution.py:49
  200.4 4.0 gather_fusion.1
  204.4 5.8 %fusion.4 = f32[96,128,128]{2,1,0:T(8,128)} fusion(bf16[1,1,96,128,128]{4,3,2,1,0:T(8,128)(2,1)S(1)} %copy-done, bf16[96,128,128]{2,1,0:T(8,128)(2,1)} %gather_fusion.1, pred[96]{0:T(512)(128)(4,1)S(1)} %compare_and_fusion), kind=kOutput, calls=%fused_computation.6 | convolution fusion | flops 404226048 | bytes 12583008 | tf_op jit(solution)/shard_map/tji,tjf->tif/dot_general | solution.py:52
  210.2 0.0 copy-start.3
  210.2 6.7 %copy.13 = f32[96,128,128]{1,0,2:T(8,128)} copy(f32[96,128,128]{2,1,0:T(8,128)} %fusion.4) | data formatting | bytes 12582912 | tf_op jit(solution)/shard_map/tji,tjf->tif/dot_general | solution.py:52
  216.9 0.0 copy-done.3
  216.9 4.2 %fusion = f32[16,128,128]{2,0,1:T(8,128)S(1)} fusion(f32[96,128,128]{1,0,2:T(8,128)} %copy.13, s32[96]{0:T(128)S(1)} %bitcast.44, pred[96]{0:T(512)(128)(4,1)S(1)} %iota_compare_fusion.2), kind=kOutput, calls=%fused_computation.2 | convolution fusion | flops 301992960 | bytes 7340512 | tf_op jit(solution)/shard_map/bt,tif->bif/dot_general | solution.py:10
  221.1 1.3 copy.11
  222.4 62.8 %all-reduce.7 = bf16[2048,128]{1,0:T(8,128)(2,1)} all-reduce(f32[2048,128]{1,0:T(8,128)} %bitcast.42), channel_id=1, replica_groups=mesh['row'=8,'col'=16,'rep'=4] {'row'}, use_global_device_ids=true, to_apply=%region_3.4 | all-reduce | flops 262144 | bytes 1572864 | tf_op jit(solution)/shard_map/psum | solution.py:57
  285.2 109.0 %all-reduce.6.cloned.1.call-done = f32[128,512]{1,0:T(8,128)} async-done(((f32[128,512]{1,0:T(8,128)}), f32[128,512]{1,0:T(8,128)}) %all-reduce.6.cloned.1.call-update) | async-done | bytes 262160 | tf_op jit(solution)/shard_map/psum | solution.py:45
  394.2 1.7 copy.19
  (5 shorter events, 0.0 us)
Async XLA Ops:
  7.2 6.1 %copy-start = (bf16[1,1,96,128,128]{4,3,2,1,0:T(8,128)(2,1)S(1)}, bf16[1,1,96,128,128]{4,3,2,1,0:T(8,128)(2,1)}, u32[]{:S(2)}) copy-start(bf16[1,1,96,128,128]{4,3,2,1,0:T(8,128)(2,1)} %param.7) | copy-start | bytes 9437188
  7.2 89.8 %reduce-scatter.2.cloned.1.call-start = ((), (), s32[]{:S(2)}) async-start(), calls=%async_computation.1 | async-start | bytes 2228224 | tf_op jit(solution)/shard_map/reduce_scatter | solution.py:32
  20.3 6.7 %copy-start.2 = (s32[1,1,96]{2,1,0:T(1,128)S(1)}, s32[1,1,96]{2,1,0:T(1,128)}, u32[]{:S(2)}) copy-start(s32[1,1,96]{2,1,0:T(1,128)} %param.8) | copy-start | bytes 1156
  31.5 65.6 %copy-start.1 = (bf16[128,512]{1,0:T(8,128)(2,1)S(1)}, bf16[128,512]{1,0:T(8,128)(2,1)}, u32[]{:S(2)}) copy-start(bf16[128,512]{1,0:T(8,128)(2,1)} %param.12) | copy-start | bytes 393220
  34.0 120.9 %all-reduce.4.cloned.1.call-start = ((), (), s32[]{:S(2)}) async-start(), calls=%async_computation.2 | async-start | bytes 1048576 | tf_op jit(solution)/shard_map/psum | solution.py:36
  99.0 101.4 %all-gather.2.cloned.1.call-start = ((), (), s32[]{:S(2)}) async-start(), calls=%async_computation.4 | async-start | bytes 1114112 | tf_op jit(solution)/shard_map/all_gather | solution.py:49
  157.9 236.3 %all-reduce.6.cloned.1.call-start = ((), (), s32[]{:S(2)}) async-start(), calls=%async_computation.3 | async-start | bytes 524288 | tf_op jit(solution)/shard_map/psum | solution.py:45
  210.2 6.7 %copy-start.3 = (s32[1,1,96]{2,1,0:T(1,128)S(1)}, s32[1,1,96]{2,1,0:T(1,128)}, u32[]{:S(2)}) copy-start(s32[1,1,96]{2,1,0:T(1,128)} %param.9) | copy-start | bytes 1156
Sparse Core Ops, SparseCore 0:
  34.2 62.8 reduce-scatter.1
  99.9 54.9 all-reduce.3
  158.0 42.3 all-gather.1
  204.0 190.1 all-reduce.5
where the time goes:
time: 403 us; the launch traced here: 402 us
  waiting for transfers between devices  269 us (67%)
  blocking collectives  62.8 us (16%)
  local copies, waits for them, and re-layouts  26.7 us (7%)
  matrix products  26.1 us (6%)
  between operations  14.5 us (4%)
    psum x1, waiting for transfers between devices, body(): weight_grad = lax.psum(local_grad, ('row', 'col'))  109 us
    reduce_scatter x1, waiting for transfers between devices, body(): lax.psum_scatter(partial_rows, 'col', scatter_dimension=0, tiled=True)  62.9 us
    psum x1, blocking collectives, body(): input_grad = lax.psum(partial_cols, 'row').astype(jnp.bfloat16)  62.8 us
    psum x1, waiting for transfers between devices, body(): hidden = lax.psum(term, 'rep')  56 us
    all_gather x1, waiting for transfers between devices, body(): grad_rowpart = lax.all_gather(grad_agg, 'col', axis=0, tiled=True)  40.6 us
    dot_general x2, matrix products, block_sum(): jnp.einsum('bt,tif->bif', select, contrib, precision=lax.Precision.HIGHEST)  8.67 us
  transfers between devices with their start and end apart: 4, of which 4 were waited for; matrix products, arithmetic and copies ran while one was open for 6% of the time, Pallas kernels for 0%

commit v1 on v0

v1 whole, which is shorter than its diff:
```python
import functools
import math

import jax
import jax.numpy as jnp
from jax import lax
from jax.experimental import pallas as pl
from jax.experimental.pallas import tpu as pltpu
from jax.sharding import Mesh
from jax.sharding import PartitionSpec as P

VMEM_LIMIT = 40 * 1024 * 1024
CHUNK = 16
GROUP = 4
BF = jnp.bfloat16
F4 = jnp.float32

VMEM = pl.BlockSpec(memory_space=pltpu.VMEM)
SMEM = pl.BlockSpec(memory_space=pltpu.SMEM)
HBM = pl.BlockSpec(memory_space=pl.ANY)


def dot(a, b, dims=(((1,), (0,)), ((), ()))):
    return lax.dot_general(a, b, dims, preferred_element_type=F4)


def tile_copies(values, tiles, sems):
    return [
        pltpu.make_async_copy(
            values.at[pl.ds(first, CHUNK)], tiles.at[pl.ds(first, CHUNK)], sems.at[first // CHUNK]
        )
        for first in range(0, tiles.shape[0], CHUNK)
    ]


def walk_tiles(used, copies, out_ids, dump, product, acc):
    for chunk, copy in enumerate(copies):
        copy.wait()
        first = chunk * CHUNK
        groups = jnp.clip((used - first + GROUP - 1) // GROUP, 0, CHUNK // GROUP)

        @pl.loop(0, groups)
        def _(g):
            slots = [first + g * GROUP + u for u in range(GROUP)]
            terms = [product(t) for t in slots]
            for t, term in zip(slots, terms):
                place = jnp.where(t < used, out_ids[t], dump)
                acc[place] += term


def forward_kernel(row_ids, col_ids, count, core, values, feats, own, other, tiles, acc, sems):
    copies = tile_copies(values, tiles, sems)
    for copy in copies:
        copy.start()
    acc[...] = jnp.zeros_like(acc)

    def product(t):
        return dot(tiles[t], feats[col_ids[t]])

    walk_tiles(count[0], copies, row_ids, acc.shape[0] - 1, product, acc)
    ys, grains, _ = own.shape
    blocks = grains // acc.shape[1]
    me = core[0]
    for y in range(ys):
        for b in range(blocks):
            rows = pl.ds(b * acc.shape[1], acc.shape[1])
            own[y, rows, :] = acc[(2 * y + me) * blocks + b]
            other[y, rows, :] = acc[(2 * y + 1 - me) * blocks + b].astype(BF)


def forward_tiles(row_ids, col_ids, count, core, values, feats, ys, grains):
    slots, side, _ = values.shape
    width = feats.shape[-1]
    row_blocks = 2 * ys * grains // side
    return pl.pallas_call(
        forward_kernel,
        out_shape=(
            jax.ShapeDtypeStruct((ys, grains, width), F4),
            jax.ShapeDtypeStruct((ys, grains, width), BF),
        ),
        in_specs=[SMEM, SMEM, SMEM, SMEM, HBM, VMEM],
        out_specs=(VMEM, VMEM),
        scratch_shapes=[
            pltpu.VMEM((slots, side, side), BF),
            pltpu.VMEM((row_blocks + 1, side, width), F4),
            pltpu.SemaphoreType.DMA((slots // CHUNK,)),
        ],
        compiler_params=pltpu.CompilerParams(vmem_limit_bytes=VMEM_LIMIT),
        name="forward_tiles",
    )(row_ids, col_ids, count, core, values, feats)


def dense_kernel(aggs, own_agg, w_all, w_own, cot, act, payload):
    reps, grains, width = aggs.shape
    ys, _, side = payload.shape
    hidden = dot(aggs[0], w_all[pl.ds(0, width), :])
    for q in range(1, reps):
        hidden += dot(aggs[q], w_all[pl.ds(q * width, width), :])
    sigma = jax.nn.sigmoid(hidden)
    act[...] = (hidden * sigma).astype(BF)
    slope = sigma * (1.0 + hidden * (1.0 - sigma))
    grad_hidden = (cot[...].astype(F4) * slope).astype(BF)
    back = dot(w_own[...], grad_hidden, (((1,), (1,)), ((), ()))).astype(BF)
    share = dot(own_agg[...], grad_hidden, (((0,), (0,)), ((), ()))).astype(BF)
    part = width // ys
    for y in range(ys):
        for b in range(grains // side):
            payload[y, pl.ds(b * width, width), :] = back[:, b * side : (b + 1) * side]
        base = grains // side * width
        for k in range(share.shape[1] // side):
            payload[y, pl.ds(base + k * part, part), :] = share[
                y * part : (y + 1) * part, k * side : (k + 1) * side
            ]


def dense(aggs, own_agg, w_all, w_own, cot, ys, side):
    reps, grains, width = aggs.shape
    total = w_own.shape[1]
    rows = grains // side * width + width // ys * (total // side)
    return pl.pallas_call(
        dense_kernel,
        out_shape=(
            jax.ShapeDtypeStruct((grains, total), BF),
            jax.ShapeDtypeStruct((ys, rows, side), BF),
        ),
        in_specs=[VMEM] * 5,
        out_specs=(VMEM, VMEM),
        compiler_params=pltpu.CompilerParams(vmem_limit_bytes=VMEM_LIMIT),
        name="dense",
    )(aggs, own_agg, w_all, w_own, cot)


def backward_kernel(
    row_ids, col_ids, count, core, values, mine, theirs, payload, tiles, grads, acc, sems, gsems
):
    me = core[0]
    copies = tile_copies(values, tiles, sems)
    take = [
        pltpu.make_async_copy(mine, grads.at[me], gsems.at[0]),
        pltpu.make_async_copy(theirs, grads.at[1 - me], gsems.at[1]),
    ]
    for copy in take + copies:
        copy.start()
    acc[...] = jnp.zeros_like(acc)
    side = tiles.shape[1]
    width = acc.shape[1]
    rows, _, _ = payload.shape
    ys = grads.shape[1]
    col_blocks = acc.shape[0] - 1
    per_row = col_blocks // rows
    blocks = per_row
    base = blocks * width
    for copy in take:
        copy.wait()

    def product(t):
        b = row_ids[t]
        device = b // blocks
        start = pl.multiple_of((b % blocks) * width, width)
        return dot(grads[device % 2, device // 2, pl.ds(start, width), :], tiles[t])

    share = jnp.zeros((payload.shape[1] - base, side), F4)
    for c in range(2):
        for y in range(ys):
            share += grads[c, y, base:, :].astype(F4)
    share = share.astype(BF)
    walk_tiles(count[0], copies, col_ids, col_blocks, product, acc)
    for r in range(rows):
        for b in range(per_row):
            payload[r, pl.ds(b * width, width), :] = acc[r * per_row + b].astype(BF)
        payload[r, base:, :] = share


def backward_tiles(row_ids, col_ids, count, core, values, mine, theirs, rows, col_blocks):
    slots, side, _ = values.shape
    ys, length, _ = mine.shape
    width = side
    return pl.pallas_call(
        backward_kernel,
        out_shape=jax.ShapeDtypeStruct((rows, length, side), BF),
        in_specs=[SMEM, SMEM, SMEM, SMEM, HBM, HBM, HBM],
        out_specs=VMEM,
        scratch_shapes=[
            pltpu.VMEM((slots, side, side), BF),
            pltpu.VMEM((2, ys, length, side), BF),
            pltpu.VMEM((col_blocks + 1, width, side), F4),
            pltpu.SemaphoreType.DMA((slots // CHUNK,)),
            pltpu.SemaphoreType.DMA((2,)),
        ],
        compiler_params=pltpu.CompilerParams(vmem_limit_bytes=VMEM_LIMIT),
        name="backward_tiles",
    )(row_ids, col_ids, count, core, values, mine, theirs)


def finish_kernel(scale, parts, grad, share):
    rows, length, side = parts.shape
    copies, grains, width = grad.shape
    base = grains // side * width
    total = parts[0].astype(F4)
    for r in range(1, rows):
        total += parts[r].astype(F4)
    for b in range(grains // side):
        block = total[b * width : (b + 1) * width].T.astype(BF)
        for r in range(copies):
            grad[r, pl.ds(b * side, side), :] = block
    ys, part, _ = share.shape
    for k in range(share.shape[2] // side):
        piece = total[base + k * part : base + (k + 1) * part] * scale
        for y in range(ys):
            share[y, :, k * side : (k + 1) * side] = piece


def finish(parts, scale, grains, width, ys, total):
    rows, length, side = parts.shape
    return pl.pallas_call(
        functools.partial(finish_kernel, scale),
        out_shape=(
            jax.ShapeDtypeStruct((rows, grains, width), BF),
            jax.ShapeDtypeStruct((ys, width // ys, total), F4),
        ),
        in_specs=[VMEM],
        out_specs=(VMEM, VMEM),
        compiler_params=pltpu.CompilerParams(vmem_limit_bytes=VMEM_LIMIT),
        name="finish",
    )(parts)


def swap_cores(x):
    return lax.ppermute(x, "core", [(0, 1), (1, 0)])


def exchange(x, axis):
    return lax.all_to_all(x, axis, 0, 0, tiled=True)


def body(tile_values, tile_rows, tile_cols, tile_count, features, weight, cotangent):
    values = tile_values[0, 0]
    row_ids = tile_rows[0, 0]
    col_ids = tile_cols[0, 0]
    count = tile_count[0]
    core = lax.axis_index("core").astype(jnp.int32).reshape(1)
    side = values.shape[-1]
    width = features.shape[1]
    grains, total = cotangent.shape
    ys, rows, reps = (lax.axis_size(a) for a in ("y", "row", "rep"))
    col_blocks = features.shape[0] // side
    nodes = grains * rows * ys * 2

    w_all = lax.all_gather(weight, "rep", axis=0, tiled=True)
    feats = features.reshape(col_blocks, side, width)
    own, other = forward_tiles(row_ids, col_ids, count, core, values, feats, ys, grains)
    pair = (own + swap_cores(other).astype(F4)).astype(BF)
    parts = exchange(pair, "y")
    agg = jnp.sum(parts.astype(F4), axis=0).astype(BF)
    aggs = lax.all_gather(agg, "rep", axis=0)
    activation, payload = dense(aggs, agg, w_all, weight, cotangent, ys, side)
    mine = exchange(payload, "y")
    theirs = swap_cores(mine)
    back = backward_tiles(row_ids, col_ids, count, core, values, mine, theirs, rows, col_blocks)
    sums = exchange(back, "row")
    grad, share = finish(sums, 1.0 / math.sqrt(nodes), grains, width, ys, total)
    input_grad = exchange(grad, "row").reshape(rows * grains, width)
    weight_grad = exchange(share, "y").reshape(width, total)
    return (activation, weight_grad, input_grad)


def solution(mesh):
    rows, cols, reps = mesh.devices.shape
    split = Mesh(
        mesh.devices.reshape(rows, cols // 2, 2, reps), ("row", "y", "core", "rep")
    )
    col = ("y", "core")
    return jax.shard_map(
        body,
        mesh=split,
        in_specs=(
            P("row", col, None, None, None),
            P("row", col, None),
            P("row", col, None),
            P("row", col),
            P(col, "rep"),
            P("rep", None),
            P(("row",) + col, None),
        ),
        out_specs=(P(("row",) + col, None), P("rep", None), P(col, "rep")),
        check_vma=False,
    )
```

time: 403 us -> 155 us (0.38)
  the two profiles are of different devices: /device:TPU:26 before, /device:TPU:2 now
where the time goes in v1:
time: 155 us; the launch traced here: 154 us
  blocking collectives  92.6 us (60%)
  waiting for transfers between devices  24 us (15%)
  starting transfers between devices  15.7 us (10%)
  Pallas kernels  10.5 us (7%)
  local copies, waits for them, and re-layouts  7.74 us (5%)
  other arithmetic  2.02 us (1%)
    all_to_all x3, blocking collectives, exchange(): return lax.all_to_all(x, axis, 0, 0, tiled=True)  66.7 us
    all_to_all x2, waiting for transfers between devices, exchange(): return lax.all_to_all(x, axis, 0, 0, tiled=True)  20 us
    all_gather x1, blocking collectives, body(): w_all = lax.all_gather(weight, 'rep', axis=0, tiled=True)  13.6 us
    all_gather x1, blocking collectives, body(): aggs = lax.all_gather(agg, 'rep', axis=0)  12.3 us
    all_to_all x2, starting transfers between devices, exchange(): return lax.all_to_all(x, axis, 0, 0, tiled=True)  11.8 us
    unnamed x22, local copies, waits for them, and re-layouts  7.74 us
    pallas_call x1, Pallas kernels, backward_tiles(): pl.pallas_call(backward_kernel, out_shape=jax.ShapeDtypeStruct((rows, len...  4.38 us
    ppermute x2, waiting for transfers between devices, swap_cores(): return lax.ppermute(x, 'core', [(0, 1), (1, 0)])  3.94 us
  transfers between devices with their start and end apart: 4, of which 4 were waited for; matrix products, arithmetic and copies ran while one was open for 0% of the time, Pallas kernels for 0%

profile of v1, /device:TPU:2, one launch (start us, length us, event | category | flops | bytes accessed | tf_op | source)
XLA Modules:
  0.0 153.9 jit_solution(12119100924072199660)
XLA Ops:
  1.3 0.0 copy-start
  1.3 1.9 %copy-done = bf16[1,1,96,128,128]{4,3,2,1,0:T(8,128)(2,1)S(1)} copy-done((bf16[1,1,96,128,128]{4,3,2,1,0:T(8,128)(2,1)S(1)}, bf16[1,1,96,128,128]{4,3,2,1,0:T(8,128)(2,1)}, u32[]{:S(2)}) %copy-start) | copy-done | bytes 3145752
  3.2 0.0 copy-start.3
  3.2 1.0 copy-done.3
  4.2 0.0 copy-start.6
  4.2 0.7 copy-done.6
  4.9 0.0 copy-start.8
  4.9 0.7 copy-done.8
  5.5 0.0 copy-start.4
  5.5 3.9 %forward_tiles.1 = (f32[8,256,128]{2,1,0:T(8,128)S(1)}, bf16[8,256,128]{2,1,0:T(8,128)(2,1)S(1)}) custom-call(s32[96]{0:T(128)S(1)} %bitcast.15, s32[96]{0:T(128)S(1)} %bitcast.17, s32[1]{0:T(128)} %bitcast.9.count, s32[1]{0:T(128)} %bitcast.3.core, bf16[96,128,128]{2,1,0:T(8,128)(2,1)S(1)} %bitcast.11, bf16[16,128,128]{2,1,0:T(8,128)(2,1)S(1)} %bitcast.14), custom_call_target="tpu_custom_call" | custom-call | tf_op jit(solution)/shard_map/forward_tiles/pallas_call | solution.py:75
  9.5 1.9 %collective-permute-start = (bf16[8,256,128]{2,1,0:T(8,128)(2,1)S(1)}, bf16[8,256,128]{2,1,0:T(8,128)(2,1)S(1)}, u32[]{:S(2)}, u32[]{:S(2)}) collective-permute-start(bf16[8,256,128]{2,1,0:T(8,128)(2,1)S(1)} %get-tuple-element.10), channel_id=1, source_target_pairs={{0,4},{4,0},{1,5},{5,1},{2,6},{6,2},{3,7},{7,3},{8,12},{12,8},{9,1... | collective-permute-start | bytes 1572872 | tf_op jit(solution)/shard_map/ppermute | solution.py:229
  11.4 1.9 %collective-permute-done = bf16[8,256,128]{2,1,0:T(8,128)(2,1)S(1)} collective-permute-done((bf16[8,256,128]{2,1,0:T(8,128)(2,1)S(1)}, bf16[8,256,128]{2,1,0:T(8,128)(2,1)S(1)}, u32[]{:S(2)}, u32[]{:S(2)}) %collective-permute-start) | collective-permute-done | bytes 524320 | tf_op jit(solution)/shard_map/ppermute | solution.py:229
  13.3 0.0 copy-start.1
  13.3 0.0 copy-start.7
  13.3 0.0 copy-start.9
  13.3 0.9 add_convert_fusion
  14.2 8.3 %all-to-all-start = ((bf16[8,256,128]{2,1,0:T(8,128)(2,1)}), bf16[8,256,128]{2,1,0:T(8,128)(2,1)}, u32[]{:S(2)}, u32[]{:S(2)}) async-start(bf16[8,256,128]{2,1,0:T(8,128)(2,1)} %add_convert_fusion), calls=%async_computation | async-start | bytes 1048576 | tf_op jit(solution)/shard_map/all_to_all | solution.py:233
  22.5 0.0 copy-done.4
  22.5 13.6 %all_gather.11.w_all = bf16[512,512]{1,0:T(8,128)(2,1)} all-gather(bf16[128,512]{1,0:T(8,128)(2,1)S(1)} %copy-done.4), channel_id=1, replica_groups=mesh['row'=8,'y'=8,'core'=2,'rep'=4] {'rep'}, dimensions={0}, use_global_device_ids=true | all-gather | bytes 655360 | tf_op jit(solution)/shard_map/all_gather | solution.py:249
  36.1 4.4 %all-to-all-done = bf16[8,256,128]{2,1,0:T(8,128)(2,1)} async-done(((bf16[8,256,128]{2,1,0:T(8,128)(2,1)}), bf16[8,256,128]{2,1,0:T(8,128)(2,1)}, u32[]{:S(2)}, u32[]{:S(2)}) %all-to-all-start) | async-done | bytes 524320 | tf_op jit(solution)/shard_map/all_to_all | solution.py:233
  40.5 1.1 reduce_sum.12.own_agg
  41.6 12.3 %all-gather = bf16[1024,128]{1,0:T(8,128)(2,1)S(1)} all-gather(bf16[256,128]{1,0:T(8,128)(2,1)S(1)} %reduce_sum.12.own_agg), channel_id=2, replica_groups=mesh['row'=8,'y'=8,'core'=2,'rep'=4] {'rep'}, dimensions={0}, use_global_device_ids=true | all-gather | bytes 327680 | tf_op jit(solution)/shard_map/all_gather | solution.py:255
  53.9 0.0 copy-start.2
  53.9 1.0 copy-done.2
  55.0 0.0 copy-start.5
  55.0 0.9 copy-done.5
  55.9 1.3 dense.1
  57.2 20.5 %all_to_all.25.mine = bf16[8,320,128]{2,1,0:T(8,128)(2,1)S(1)} all-to-all(bf16[8,320,128]{2,1,0:T(8,128)(2,1)S(1)} %get-tuple-element.12), channel_id=1, replica_groups=mesh['row'=8,'y'=8,'core'=2,'rep'=4] {'y'}, dimensions={0} | all-to-all | bytes 1310720 | tf_op jit(solution)/shard_map/all_to_all | solution.py:233
  77.7 1.9 %collective-permute-start.1 = (bf16[8,320,128]{2,1,0:T(8,128)(2,1)S(1)}, bf16[8,320,128]{2,1,0:T(8,128)(2,1)S(1)}, u32[]{:S(2)}, u32[]{:S(2)}) collective-permute-start(bf16[8,320,128]{2,1,0:T(8,128)(2,1)S(1)} %all_to_all.25.mine), channel_id=1, source_target_pairs={{0,4},{4,0},{1,5},{5,1},{2,6},{6,2},{3,7},{7,3},{8,12},{12,8},{9,1... | collective-permute-start | bytes 1966088 | tf_op jit(solution)/shard_map/ppermute | solution.py:229
  79.6 2.1 %collective-permute-done.1.theirs = bf16[8,320,128]{2,1,0:T(8,128)(2,1)S(1)} collective-permute-done((bf16[8,320,128]{2,1,0:T(8,128)(2,1)S(1)}, bf16[8,320,128]{2,1,0:T(8,128)(2,1)S(1)}, u32[]{:S(2)}, u32[]{:S(2)}) %collective-permute-start.1) | collective-permute-done | bytes 655392 | tf_op jit(solution)/shard_map/ppermute | solution.py:229
  81.6 0.0 copy-done.1
  81.6 0.0 copy-done.7
  81.6 0.0 copy-done.9
  81.6 4.4 %backward_tiles.1 = bf16[8,320,128]{2,1,0:T(8,128)(2,1)S(1)} custom-call(s32[96]{0:T(128)S(1)} %bitcast.16, s32[96]{0:T(128)S(1)} %bitcast.18, s32[1]{0:T(128)} %bitcast.10.count, s32[1]{0:T(128)} %bitcast.3.core, bf16[96,128,128]{2,1,0:T(8,128)(2,1)S(1)} %bitcast.12, bf16[8,320,128]{2,1,0:T(8,128)(2,1)S(1)} %all_to_all.25.mine, ...), custom_call_target="tpu_custom_call" | custom-call | tf_op jit(solution)/shard_map/backward_tiles/pallas_call | solution.py:178
  86.0 32.3 %all_to_all.26.parts = bf16[8,320,128]{2,1,0:T(8,128)(2,1)S(1)} all-to-all(bf16[8,320,128]{2,1,0:T(8,128)(2,1)S(1)} %backward_tiles.1), channel_id=1, replica_groups=mesh['row'=8,'y'=8,'core'=2,'rep'=4] {'row'}, dimensions={0} | all-to-all | bytes 1310720 | tf_op jit(solution)/shard_map/all_to_all | solution.py:233
  118.4 1.0 finish.1
  119.3 13.9 %all_to_all.27 = f32[8,16,512]{2,1,0:T(8,128)S(1)} all-to-all(f32[8,16,512]{2,1,0:T(8,128)S(1)} %get-tuple-element.13), channel_id=1, replica_groups=mesh['row'=8,'y'=8,'core'=2,'rep'=4] {'y'}, dimensions={0} | all-to-all | bytes 524288 | tf_op jit(solution)/shard_map/all_to_all | solution.py:233
  133.3 3.5 %all-to-all-start.4 = ((bf16[8,256,128]{2,1,0:T(8,128)(2,1)}), bf16[8,256,128]{2,1,0:T(8,128)(2,1)S(1)}, u32[]{:S(2)}, u32[]{:S(2)}) async-start(bf16[8,256,128]{2,1,0:T(8,128)(2,1)} %get-tuple-element.14), calls=%async_computation.4 | async-start | bytes 1048576 | tf_op jit(solution)/shard_map/all_to_all | solution.py:233
  136.8 15.6 %all-to-all-done.4 = bf16[8,256,128]{2,1,0:T(8,128)(2,1)S(1)} async-done(((bf16[8,256,128]{2,1,0:T(8,128)(2,1)}), bf16[8,256,128]{2,1,0:T(8,128)(2,1)S(1)}, u32[]{:S(2)}, u32[]{:S(2)}) %all-to-all-start.4) | async-done | bytes 524320 | tf_op jit(solution)/shard_map/all_to_all | solution.py:233
  152.4 0.7 copy.13
  153.1 0.8 copy.14
Async XLA Ops:
  1.3 1.9 %copy-start = (bf16[1,1,96,128,128]{4,3,2,1,0:T(8,128)(2,1)S(1)}, bf16[1,1,96,128,128]{4,3,2,1,0:T(8,128)(2,1)}, u32[]{:S(2)}) copy-start(bf16[1,1,96,128,128]{4,3,2,1,0:T(8,128)(2,1)} %param.7) | copy-start | bytes 9437188
  3.2 1.0 copy-start.3
  4.2 0.7 copy-start.6
  4.9 0.7 copy-start.8
  5.5 17.0 %copy-start.4 = (bf16[128,512]{1,0:T(8,128)(2,1)S(1)}, bf16[128,512]{1,0:T(8,128)(2,1)}, u32[]{:S(2)}) copy-start(bf16[128,512]{1,0:T(8,128)(2,1)} %w_own.1) | copy-start | bytes 393220
  9.5 3.8 %collective-permute-start = (bf16[8,256,128]{2,1,0:T(8,128)(2,1)S(1)}, bf16[8,256,128]{2,1,0:T(8,128)(2,1)S(1)}, u32[]{:S(2)}, u32[]{:S(2)}) collective-permute-start(bf16[8,256,128]{2,1,0:T(8,128)(2,1)S(1)} %get-tuple-element.10), channel_id=1, source_target_pairs={{0,4},{4,0},{1,5},{5,1},{2,6},{6,2},{3,7},{7,3},{8,12},{12,8},{9,1... | collective-permute-start | bytes 1572872 | tf_op jit(solution)/shard_map/ppermute | solution.py:229
  13.3 68.4 %copy-start.1 = (bf16[1,1,96,128,128]{4,3,2,1,0:T(8,128)(2,1)S(1)}, bf16[1,1,96,128,128]{4,3,2,1,0:T(8,128)(2,1)}, u32[]{:S(2)}) copy-start(bf16[1,1,96,128,128]{4,3,2,1,0:T(8,128)(2,1)} %param.7) | copy-start | bytes 9437188
  13.3 68.4 %copy-start.7 = (s32[1,1,96]{2,1,0:T(1,128)S(1)}, s32[1,1,96]{2,1,0:T(1,128)}, u32[]{:S(2)}) copy-start(s32[1,1,96]{2,1,0:T(1,128)} %param.8) | copy-start | bytes 1156
  13.3 68.4 %copy-start.9 = (s32[1,1,96]{2,1,0:T(1,128)S(1)}, s32[1,1,96]{2,1,0:T(1,128)}, u32[]{:S(2)}) copy-start(s32[1,1,96]{2,1,0:T(1,128)} %param.9) | copy-start | bytes 1156
  14.2 26.3 %all-to-all-start = ((bf16[8,256,128]{2,1,0:T(8,128)(2,1)}), bf16[8,256,128]{2,1,0:T(8,128)(2,1)}, u32[]{:S(2)}, u32[]{:S(2)}) async-start(bf16[8,256,128]{2,1,0:T(8,128)(2,1)} %add_convert_fusion), calls=%async_computation | async-start | bytes 1048576 | tf_op jit(solution)/shard_map/all_to_all | solution.py:233
  53.9 1.0 copy-start.2
  55.0 0.9 copy-start.5
  77.7 4.0 %collective-permute-start.1 = (bf16[8,320,128]{2,1,0:T(8,128)(2,1)S(1)}, bf16[8,320,128]{2,1,0:T(8,128)(2,1)S(1)}, u32[]{:S(2)}, u32[]{:S(2)}) collective-permute-start(bf16[8,320,128]{2,1,0:T(8,128)(2,1)S(1)} %all_to_all.25.mine), channel_id=1, source_target_pairs={{0,4},{4,0},{1,5},{5,1},{2,6},{6,2},{3,7},{7,3},{8,12},{12,8},{9,1... | collective-permute-start | bytes 1966088 | tf_op jit(solution)/shard_map/ppermute | solution.py:229
  133.3 19.1 %all-to-all-start.4 = ((bf16[8,256,128]{2,1,0:T(8,128)(2,1)}), bf16[8,256,128]{2,1,0:T(8,128)(2,1)S(1)}, u32[]{:S(2)}, u32[]{:S(2)}) async-start(bf16[8,256,128]{2,1,0:T(8,128)(2,1)} %get-tuple-element.14), calls=%async_computation.4 | async-start | bytes 1048576 | tf_op jit(solution)/shard_map/all_to_all | solution.py:233

commit v2 on v1

v2 whole, which is shorter than its diff:
```python
import functools
import math

import jax
import jax.numpy as jnp
from jax import lax
from jax.experimental import pallas as pl
from jax.experimental.pallas import tpu as pltpu
from jax.sharding import Mesh
from jax.sharding import PartitionSpec as P

VMEM_LIMIT = 40 * 1024 * 1024
FORWARD_VMEM = 51 * 1024 * 1024
CHUNK = 16
BF = jnp.bfloat16
F4 = jnp.float32

VMEM = pl.BlockSpec(memory_space=pltpu.VMEM)
SMEM = pl.BlockSpec(memory_space=pltpu.SMEM)
ANY = pl.BlockSpec(memory_space=pl.ANY)
HOLDERS = 4


def dot(a, b, dims=(((1,), (0,)), ((), ()))):
    return lax.dot_general(a, b, dims, preferred_element_type=F4)


def tile_copies(values, tiles, sems):
    return [
        pltpu.make_async_copy(
            values.at[pl.ds(first, CHUNK)], tiles.at[pl.ds(first, CHUNK)], sems.at[first // CHUNK]
        )
        for first in range(0, tiles.shape[0], CHUNK)
    ]


def pack_ids(row_ids, col_ids, used, row_blocks, col_blocks):
    live = jnp.arange(row_ids.shape[0], dtype=jnp.int32) < used
    span = 2 * col_blocks
    return jnp.where(live, row_ids * span + col_ids, row_blocks * span + col_blocks)


def forward_kernel(
    core, ids_any, values, feats_any, own, other, ids, feats, tiles, acc, sems, more_sems
):
    first = [
        pltpu.make_async_copy(ids_any, ids, more_sems.at[0]),
        pltpu.make_async_copy(feats_any, feats, more_sems.at[1]),
    ]
    copies = tile_copies(values, tiles, sems)
    for copy in first + copies:
        copy.start()
    acc[...] = jnp.zeros_like(acc)
    for copy in first:
        copy.wait()
    col_blocks, side, _ = feats.shape
    for chunk, copy in enumerate(copies):
        copy.wait()
        for t in range(chunk * CHUNK, (chunk + 1) * CHUNK):
            acc[ids[t] // (2 * col_blocks)] += dot(tiles[t], feats[ids[t] % col_blocks])
    ys, grains, _ = own.shape
    blocks = grains // side
    me = core[0]
    for y in range(ys):
        for b in range(blocks):
            rows = pl.ds(b * side, side)
            own[y, rows, :] = acc[(2 * y + me) * blocks + b]
            other[y, rows, :] = acc[(2 * y + 1 - me) * blocks + b].astype(BF)


def forward_tiles(core, ids, values, feats, ys, grains):
    slots, side, _ = values.shape
    width = feats.shape[-1]
    row_blocks = 2 * ys * grains // side
    return pl.pallas_call(
        forward_kernel,
        out_shape=(
            jax.ShapeDtypeStruct((ys, grains, width), F4),
            jax.ShapeDtypeStruct((ys, grains, width), BF),
        ),
        in_specs=[SMEM, ANY, ANY, ANY],
        out_specs=(VMEM, VMEM),
        scratch_shapes=[
            pltpu.SMEM(ids.shape, jnp.int32),
            pltpu.VMEM(feats.shape, BF),
            pltpu.VMEM((slots, side, side), BF),
            pltpu.VMEM((row_blocks + 1, side, width), F4),
            pltpu.SemaphoreType.DMA((slots // CHUNK,)),
            pltpu.SemaphoreType.DMA((2,)),
        ],
        compiler_params=pltpu.CompilerParams(vmem_limit_bytes=FORWARD_VMEM),
        name="forward_tiles",
    )(core, ids, values, feats)


def pair_kernel(own, theirs, weight, pair, lent):
    pair[...] = (own[...] + theirs[...].astype(F4)).astype(BF)
    lent[...] = weight[...]


def add_pair(own, theirs, weight):
    return pl.pallas_call(
        pair_kernel,
        out_shape=(
            jax.ShapeDtypeStruct(own.shape, BF),
            jax.ShapeDtypeStruct(weight.shape, BF),
        ),
        in_specs=[VMEM] * 3,
        out_specs=(VMEM, VMEM),
        compiler_params=pltpu.CompilerParams(vmem_limit_bytes=VMEM_LIMIT),
        name="add_pair",
    )(own, theirs, weight)


def fold_kernel(parts, *refs):
    copies = refs[-1]
    total = parts[0].astype(F4)
    for y in range(1, parts.shape[0]):
        total += parts[y].astype(F4)
    total = total.astype(BF)
    for q in range(copies.shape[0]):
        copies[q] = total


def fold(parts, copies, before):
    return pl.pallas_call(
        fold_kernel,
        out_shape=jax.ShapeDtypeStruct((copies,) + parts.shape[1:], BF),
        in_specs=[VMEM] + [ANY] * len(before),
        out_specs=VMEM,
        compiler_params=pltpu.CompilerParams(vmem_limit_bytes=VMEM_LIMIT),
        name="fold",
    )(parts, *before)


def dense_kernel(rep, aggs, own_weight, *refs):
    reps, grains, width = aggs.shape
    others, (cot, act, payload) = refs[: reps - 1], refs[reps - 1 :]
    me = rep[0]
    ys, _, side = payload.shape
    own_agg = aggs[me]
    hidden = dot(own_agg, own_weight[...])
    for k, weight in enumerate(others):
        hidden += dot(aggs[(me + k + 1) % reps], weight[...])
    sigma = jax.nn.sigmoid(hidden)
    act[...] = (hidden * sigma).astype(BF)
    slope = sigma * (1.0 + hidden * (1.0 - sigma))
    grad_hidden = (cot[...].astype(F4) * slope).astype(BF)
    back = dot(own_weight[...], grad_hidden, (((1,), (1,)), ((), ()))).astype(BF)
    share = dot(own_agg, grad_hidden, (((0,), (0,)), ((), ()))).astype(BF)
    holders = min(HOLDERS, ys)
    part = width // holders
    base = grains // side * width
    for y in range(ys):
        for b in range(grains // side):
            payload[y, pl.ds(b * width, width), :] = back[:, b * side : (b + 1) * side]
        chunk = y % holders
        for k in range(share.shape[1] // side):
            payload[y, pl.ds(base + k * part, part), :] = share[
                chunk * part : (chunk + 1) * part, k * side : (k + 1) * side
            ]


def dense(rep, aggs, weights, cot, ys, side):
    reps, grains, width = aggs.shape
    total = cot.shape[1]
    rows = grains // side * width + width // min(HOLDERS, ys) * (total // side)
    return pl.pallas_call(
        dense_kernel,
        out_shape=(
            jax.ShapeDtypeStruct((grains, total), BF),
            jax.ShapeDtypeStruct((ys, rows, side), BF),
        ),
        in_specs=[SMEM] + [VMEM] * (reps + 2),
        out_specs=(VMEM, VMEM),
        compiler_params=pltpu.CompilerParams(vmem_limit_bytes=VMEM_LIMIT),
        name="dense",
    )(rep, aggs, *weights, cot)


def backward_kernel(ids, core, tiles, mine, theirs, payload, acc):
    acc[...] = jnp.zeros_like(acc)
    side = tiles.shape[1]
    width = acc.shape[1]
    rows = payload.shape[0]
    ys = mine.shape[0]
    col_blocks = acc.shape[0] - 1
    per_row = col_blocks // rows
    base = per_row * width

    for t in range(tiles.shape[0]):
        b = ids[t] // (2 * col_blocks) % (2 * ys * per_row)
        device = b // per_row
        block = pl.ds(pl.multiple_of((b % per_row) * width, width), width)
        grad = jnp.where(device % 2 == core[0], mine[device // 2, block], theirs[device // 2, block])
        acc[ids[t] % (2 * col_blocks)] += dot(grad, tiles[t])
    share = jnp.zeros((payload.shape[1] - base, side), F4)
    for grads in (mine, theirs):
        for y in range(ys):
            share += grads[y, base:, :].astype(F4)
    share = share.astype(BF)
    for r in range(rows):
        for b in range(per_row):
            payload[r, pl.ds(b * width, width), :] = acc[r * per_row + b].astype(BF)
        payload[r, base:, :] = share


def backward_tiles(ids, core, values, mine, theirs, rows, col_blocks):
    side = values.shape[1]
    length = mine.shape[1]
    return pl.pallas_call(
        backward_kernel,
        out_shape=jax.ShapeDtypeStruct((rows, length, side), BF),
        in_specs=[SMEM] * 2 + [VMEM] * 3,
        out_specs=VMEM,
        scratch_shapes=[pltpu.VMEM((col_blocks + 1, side, side), F4)],
        compiler_params=pltpu.CompilerParams(vmem_limit_bytes=VMEM_LIMIT),
        name="backward_tiles",
    )(ids, core, values, mine, theirs)


def finish_kernel(scale, parts, grad, share):
    rows, length, side = parts.shape
    width = side
    grains = grad.shape[0] // rows
    base = grains // side * width
    total = parts[0].astype(F4)
    for r in range(1, rows):
        total += parts[r].astype(F4)
    for b in range(grains // side):
        block = total[b * width : (b + 1) * width].T.astype(BF)
        for r in range(rows):
            grad[pl.ds(r * grains + b * side, side), :] = block
    part = share.shape[0]
    for k in range(share.shape[1] // side):
        share[:, k * side : (k + 1) * side] = total[base + k * part : base + (k + 1) * part] * scale


def finish(parts, scale, grains, part, total):
    rows, length, side = parts.shape
    return pl.pallas_call(
        functools.partial(finish_kernel, scale),
        out_shape=(
            jax.ShapeDtypeStruct((rows * grains, side), BF),
            jax.ShapeDtypeStruct((part, total), F4),
        ),
        in_specs=[VMEM],
        out_specs=(VMEM, VMEM),
        compiler_params=pltpu.CompilerParams(vmem_limit_bytes=VMEM_LIMIT),
        name="finish",
    )(parts)


def fetch_others(weight):
    reps = lax.axis_size("rep")
    if reps != 4:
        return [
            lax.ppermute(weight, "rep", [((i + k) % reps, i) for i in range(reps)])
            for k in range(1, reps)
        ]
    steps = [(0, 1), (1, -1)]
    sides = lax.ppermute(
        weight,
        ("core", "rep"),
        [(c * reps + (i + k) % reps, c * reps + i) for c, k in steps for i in range(reps)],
    )
    across = lax.ppermute(weight, "rep", [((i + 2) % reps, i) for i in range(reps)])
    sides = lax.all_gather(sides, "core", axis=0)
    return [sides[0], across, sides[1]]


def swap_cores(x):
    return lax.ppermute(x, "core", [(0, 1), (1, 0)])


def exchange(x, axis):
    return lax.all_to_all(x, axis, 0, 0, tiled=True)


def body(tile_values, tile_rows, tile_cols, tile_count, features, weight, cotangent):
    values = tile_values[0, 0]
    core = lax.axis_index("core").astype(jnp.int32).reshape(1)
    rep = lax.axis_index("rep").astype(jnp.int32).reshape(1)
    side = values.shape[-1]
    width = features.shape[1]
    grains, total = cotangent.shape
    ys, rows, reps = (lax.axis_size(a) for a in ("y", "row", "rep"))
    col_blocks = features.shape[0] // side
    row_blocks = 2 * ys * grains // side
    nodes = grains * rows * ys * 2
    holders = min(HOLDERS, ys)

    ids = pack_ids(tile_rows[0, 0], tile_cols[0, 0], tile_count[0, 0], row_blocks, col_blocks)
    feats = features.reshape(col_blocks, side, width)
    own, other = forward_tiles(core, ids, values, feats, ys, grains)
    pair, lent = add_pair(own, swap_cores(other), weight)
    parts = exchange(pair, "y")
    others = fetch_others(lent)
    aggs = exchange(fold(parts, reps, others), "rep")
    activation, payload = dense(rep, aggs, [weight, *others], cotangent, ys, side)
    mine = exchange(payload, "y")
    theirs = swap_cores(mine)
    back = backward_tiles(ids, core, values, mine, theirs, rows, col_blocks)
    sums = exchange(back, "row")
    grad, share = finish(sums, 1.0 / math.sqrt(nodes), grains, width // holders, total)
    input_grad = exchange(grad, "row")
    groups = [list(range(y, y + holders)) for y in range(0, ys, holders)]
    weight_grad = lax.all_gather(share, "y", axis_index_groups=groups, tiled=True)
    return (activation, weight_grad, input_grad)


def solution(mesh):
    rows, cols, reps = mesh.devices.shape
    split = Mesh(
        mesh.devices.reshape(rows, cols // 2, 2, reps), ("row", "y", "core", "rep")
    )
    col = ("y", "core")
    return jax.shard_map(
        body,
        mesh=split,
        in_specs=(
            P("row", col, None, None, None),
            P("row", col, None),
            P("row", col, None),
            P("row", col),
            P(col, "rep"),
            P("rep", None),
            P(("row",) + col, None),
        ),
        out_specs=(P(("row",) + col, None), P("rep", None), P(col, "rep")),
        check_vma=False,
    )
```

time: 155 us -> 142 us (0.916)
  blocking collectives: 92.6 us -> 71.6 us
  starting transfers between devices: 15.7 us -> 28.7 us
  waiting for transfers between devices: 24 us -> 21.4 us
  local copies, waits for them, and re-layouts: 7.74 us -> 5.9 us
    all_to_all x3 -> x2, blocking collectives: 66.7 us -> 55.4 us  [exchange(): return lax.all_to_all(x, axis, 0, 0, tiled=True)]
    all_gather x2, blocking collectives: 25.9 us -> 16.2 us  [the longest x1 13.8 us: body(): lax.all_gather(share, 'y', axis_index_groups=groups, tiled=True)]
    all_to_all x2 -> x3, waiting for transfers between devices: 20 us -> 13 us  [exchange(): return lax.all_to_all(x, axis, 0, 0, tiled=True)]
    ppermute x0 -> x2, starting transfers between devices: none -> 6.84 us  [the longest x1 4.92 us: fetch_others(): lax.ppermute(weight, ('core', 'rep'), [(c * reps + (i + k) % reps, c * re...]
    all_to_all x2 -> x3, starting transfers between devices: 11.8 us -> 18 us  [exchange(): return lax.all_to_all(x, axis, 0, 0, tiled=True)]
    ppermute x0 -> x2, waiting for transfers between devices: none -> 4.24 us  [the longest x1 3.35 us: fetch_others(): lax.ppermute(weight, 'rep', [((i + 2) % reps, i) for i in range(reps)])]
    unnamed x22 -> x16, local copies, waits for them, and re-layouts: 7.74 us -> 5.89 us
    pallas_call x0 -> x2, Pallas kernels: none -> 1.84 us  [the longest x1 1.11 us: fold(): pl.pallas_call(fold_kernel, out_shape=jax.ShapeDtypeStruct((copies,) + pa...]
  transfers between devices with their start and end apart: 4 -> 7, of which waited for: 4 -> 7; matrix products, arithmetic and copies ran while one was open for 0% -> 0% of each run, Pallas kernels for 0% -> 0%
where the time goes in v2:
time: 142 us; the launch traced here: 141 us
  blocking collectives  71.6 us (50%)
  starting transfers between devices  28.7 us (20%)
  waiting for transfers between devices  21.4 us (15%)
  Pallas kernels  11.4 us (8%)
  local copies, waits for them, and re-layouts  5.9 us (4%)
    all_to_all x2, blocking collectives, exchange(): return lax.all_to_all(x, axis, 0, 0, tiled=True)  55.4 us
    all_to_all x3, starting transfers between devices, exchange(): return lax.all_to_all(x, axis, 0, 0, tiled=True)  18 us
    all_gather x1, blocking collectives, body(): lax.all_gather(share, 'y', axis_index_groups=groups, tiled=True)  13.8 us
    all_to_all x3, waiting for transfers between devices, exchange(): return lax.all_to_all(x, axis, 0, 0, tiled=True)  13 us
    unnamed x16, local copies, waits for them, and re-layouts  5.89 us
    ppermute x1, starting transfers between devices, fetch_others(): lax.ppermute(weight, ('core', 'rep'), [(c * reps + (i + k) % reps, c * re...  4.92 us
    ppermute x2, waiting for transfers between devices, swap_cores(): return lax.ppermute(x, 'core', [(0, 1), (1, 0)])  4.13 us
    ppermute x2, starting transfers between devices, swap_cores(): return lax.ppermute(x, 'core', [(0, 1), (1, 0)])  3.83 us
  transfers between devices with their start and end apart: 7, of which 7 were waited for; matrix products, arithmetic and copies ran while one was open for 0% of the time, Pallas kernels for 0%

profile of v2, /device:TPU:2, one launch (start us, length us, event | category | flops | bytes accessed | tf_op | source)
XLA Modules:
  0.0 141.0 jit_solution(10944242196074103123)
XLA Ops:
  1.3 0.7 compare_select_fusion.ids_any.ids
  2.0 0.0 copy-start.3
  2.0 1.0 copy-done.3
  3.0 0.0 copy-start.4
  3.0 3.2 %forward_tiles.1 = (f32[8,256,128]{2,1,0:T(8,128)S(1)}, bf16[8,256,128]{2,1,0:T(8,128)(2,1)S(1)}) custom-call(s32[1]{0:T(128)} %bitcast.1.core, s32[96]{0:T(128)S(1)} %compare_select_fusion.ids_any.ids, bf16[96,128,128]{2,1,0:T(8,128)(2,1)} %bitcast.10, bf16[16,128,128]{2,1,0:T(8,128)(2,1)S(1)} %bitcast.12), custom_call_target="tpu_custom_call" | custom-call | tf_op jit(solution)/shard_map/forward_tiles/pallas_call | solution.py:75
  6.2 1.9 %collective-permute-start = (bf16[8,256,128]{2,1,0:T(8,128)(2,1)S(1)}, bf16[8,256,128]{2,1,0:T(8,128)(2,1)S(1)}, u32[]{:S(2)}, u32[]{:S(2)}) collective-permute-start(bf16[8,256,128]{2,1,0:T(8,128)(2,1)S(1)} %get-tuple-element.12), channel_id=1, source_target_pairs={{0,4},{4,0},{1,5},{5,1},{2,6},{6,2},{3,7},{7,3},{8,12},{12,8},{9,1... | collective-permute-start | bytes 1572872 | tf_op jit(solution)/shard_map/ppermute | solution.py:273
  8.2 1.9 %collective-permute-done.theirs = bf16[8,256,128]{2,1,0:T(8,128)(2,1)S(1)} collective-permute-done((bf16[8,256,128]{2,1,0:T(8,128)(2,1)S(1)}, bf16[8,256,128]{2,1,0:T(8,128)(2,1)S(1)}, u32[]{:S(2)}, u32[]{:S(2)}) %collective-permute-start) | collective-permute-done | bytes 524320 | tf_op jit(solution)/shard_map/ppermute | solution.py:273
  10.0 0.0 copy-done.4
  10.0 0.7 add_pair.1
  10.8 0.0 copy-start.2
  10.8 0.8 copy-done.2
  11.6 0.0 copy-start
  11.6 7.3 %all-to-all-start = ((bf16[8,256,128]{2,1,0:T(8,128)(2,1)}), bf16[8,256,128]{2,1,0:T(8,128)(2,1)}, u32[]{:S(2)}, u32[]{:S(2)}) async-start(bf16[8,256,128]{2,1,0:T(8,128)(2,1)} %copy-done.2), calls=%async_computation | async-start | bytes 1048576 | tf_op jit(solution)/shard_map/all_to_all | solution.py:277
  18.9 4.9 %collective-permute-start.1 = (bf16[128,512]{1,0:T(8,128)(2,1)}, bf16[128,512]{1,0:T(8,128)(2,1)S(1)}, u32[]{:S(2)}, u32[]{:S(2)}) collective-permute-start(bf16[128,512]{1,0:T(8,128)(2,1)} %get-tuple-element.14), channel_id=1, source_target_pairs={{1,0},{2,1},{3,2},{0,3},{7,4},{4,5},{5,6},{6,7},{9,8},{10,9},{11,1... | collective-permute-start | bytes 393224 | tf_op jit(solution)/shard_map/ppermute | solution.py:262
  23.8 1.9 %collective-permute-start.2 = (bf16[128,512]{1,0:T(8,128)(2,1)}, bf16[128,512]{1,0:T(8,128)(2,1)S(1)}, u32[]{:S(2)}, u32[]{:S(2)}) collective-permute-start(bf16[128,512]{1,0:T(8,128)(2,1)} %get-tuple-element.14), channel_id=1, source_target_pairs={{2,0},{3,1},{0,2},{1,3},{6,4},{7,5},{4,6},{5,7},{10,8},{11,9},{8,1... | collective-permute-start | bytes 393224 | tf_op jit(solution)/shard_map/ppermute | solution.py:267
  25.7 0.9 collective-permute-done.1
  26.6 2.4 %all-gather = bf16[256,512]{1,0:T(8,128)(2,1)S(1)} all-gather(bf16[128,512]{1,0:T(8,128)(2,1)S(1)} %collective-permute-done.1), channel_id=2, replica_groups=mesh['row'=8,'y'=8,'core'=2,'rep'=4] {'core'}, dimensions={0}, use_global_device_ids=true | all-gather | bytes 393216 | tf_op jit(solution)/shard_map/all_gather | solution.py:268
  29.0 3.4 %collective-permute-done.2.refs_1_ = bf16[128,512]{1,0:T(8,128)(2,1)S(1)} collective-permute-done((bf16[128,512]{1,0:T(8,128)(2,1)}, bf16[128,512]{1,0:T(8,128)(2,1)S(1)}, u32[]{:S(2)}, u32[]{:S(2)}) %collective-permute-start.2) | collective-permute-done | bytes 131104 | tf_op jit(solution)/shard_map/ppermute | solution.py:267
  32.4 4.4 %all-to-all-done.parts = bf16[8,256,128]{2,1,0:T(8,128)(2,1)} async-done(((bf16[8,256,128]{2,1,0:T(8,128)(2,1)}), bf16[8,256,128]{2,1,0:T(8,128)(2,1)}, u32[]{:S(2)}, u32[]{:S(2)}) %all-to-all-start) | async-done | bytes 524320 | tf_op jit(solution)/shard_map/all_to_all | solution.py:277
  36.8 1.1 fold.1
  37.9 0.0 copy-start.1
  37.9 0.7 copy-done.1
  38.6 7.2 %all-to-all-start.1 = ((bf16[4,256,128]{2,1,0:T(8,128)(2,1)}), bf16[4,256,128]{2,1,0:T(8,128)(2,1)}, u32[]{:S(2)}, u32[]{:S(2)}) async-start(bf16[4,256,128]{2,1,0:T(8,128)(2,1)} %copy-done.1), calls=%async_computation.1 | async-start | bytes 524288 | tf_op jit(solution)/shard_map/all_to_all | solution.py:277
  45.8 5.8 %all-to-all-done.1.aggs = bf16[4,256,128]{2,1,0:T(8,128)(2,1)} async-done(((bf16[4,256,128]{2,1,0:T(8,128)(2,1)}), bf16[4,256,128]{2,1,0:T(8,128)(2,1)}, u32[]{:S(2)}, u32[]{:S(2)}) %all-to-all-start.1) | async-done | bytes 262176 | tf_op jit(solution)/shard_map/all_to_all | solution.py:277
  51.6 0.0 copy-start.5
  51.6 0.9 copy-done.5
  52.5 0.0 copy-start.6
  52.5 0.9 copy-done.6
  53.5 2.2 %dense.1 = (bf16[256,512]{1,0:T(8,128)(2,1)}, bf16[8,384,128]{2,1,0:T(8,128)(2,1)S(1)}) custom-call(s32[1]{0:T(128)} %bitcast.rep, bf16[4,256,128]{2,1,0:T(8,128)(2,1)} %all-to-all-done.1.aggs, bf16[128,512]{1,0:T(8,128)(2,1)S(1)} %copy-done.5, bf16[128,512]{1,0:T(8,128)(2,1)S(1)} %get-tuple-element.20.refs_0_, ...), custom_call_target="tpu_custom_call" | custom-call | tf_op jit(solution)/shard_map/dense/pallas_call | solution.py:168
  55.7 24.8 %all_to_all.32.mine = bf16[8,384,128]{2,1,0:T(8,128)(2,1)S(1)} all-to-all(bf16[8,384,128]{2,1,0:T(8,128)(2,1)S(1)} %get-tuple-element.16), channel_id=1, replica_groups=mesh['row'=8,'y'=8,'core'=2,'rep'=4] {'y'}, dimensions={0} | all-to-all | bytes 1572864 | tf_op jit(solution)/shard_map/all_to_all | solution.py:277
  80.6 1.9 %collective-permute-start.3 = (bf16[8,384,128]{2,1,0:T(8,128)(2,1)S(1)}, bf16[8,384,128]{2,1,0:T(8,128)(2,1)S(1)}, u32[]{:S(2)}, u32[]{:S(2)}) collective-permute-start(bf16[8,384,128]{2,1,0:T(8,128)(2,1)S(1)} %all_to_all.32.mine), channel_id=1, source_target_pairs={{0,4},{4,0},{1,5},{5,1},{2,6},{6,2},{3,7},{7,3},{8,12},{12,8},{9,1... | collective-permute-start | bytes 2359304 | tf_op jit(solution)/shard_map/ppermute | solution.py:273
  82.5 2.3 %collective-permute-done.3.theirs = bf16[8,384,128]{2,1,0:T(8,128)(2,1)S(1)} collective-permute-done((bf16[8,384,128]{2,1,0:T(8,128)(2,1)S(1)}, bf16[8,384,128]{2,1,0:T(8,128)(2,1)S(1)}, u32[]{:S(2)}, u32[]{:S(2)}) %collective-permute-start.3) | collective-permute-done | bytes 786464 | tf_op jit(solution)/shard_map/ppermute | solution.py:273
  84.7 0.0 copy-done
  84.7 3.1 %backward_tiles.1 = bf16[8,384,128]{2,1,0:T(8,128)(2,1)S(1)} custom-call(s32[96]{0:T(128)S(1)} %compare_select_fusion.ids_any.ids, s32[1]{0:T(128)} %bitcast.1.core, bf16[96,128,128]{2,1,0:T(8,128)(2,1)S(1)} %bitcast.11, bf16[8,384,128]{2,1,0:T(8,128)(2,1)S(1)} %all_to_all.32.mine, bf16[8,384,128]{2,1,0:T(8,128)(2,1)S(1)} %collective-permute-done.3.theirs), custom_call_target="tpu_custom_call" | custom-call | tf_op jit(solution)/shard_map/backward_tiles/pallas_call | solution.py:211
  87.8 30.6 %all_to_all.33.parts = bf16[8,384,128]{2,1,0:T(8,128)(2,1)S(1)} all-to-all(bf16[8,384,128]{2,1,0:T(8,128)(2,1)S(1)} %backward_tiles.1), channel_id=1, replica_groups=mesh['row'=8,'y'=8,'core'=2,'rep'=4] {'row'}, dimensions={0} | all-to-all | bytes 1572864 | tf_op jit(solution)/shard_map/all_to_all | solution.py:277
  118.4 1.0 finish.1
  119.4 3.5 %all-to-all-start.4 = ((bf16[8,256,128]{2,1,0:T(8,128)(2,1)}), bf16[8,256,128]{2,1,0:T(8,128)(2,1)S(1)}, u32[]{:S(2)}, u32[]{:S(2)}) async-start(bf16[8,256,128]{2,1,0:T(8,128)(2,1)} %bitcast.6), calls=%async_computation.4 | async-start | bytes 1048576 | tf_op jit(solution)/shard_map/all_to_all | solution.py:277
  122.9 13.8 %all_gather.11 = f32[128,512]{1,0:T(8,128)S(1)} all-gather(f32[32,512]{1,0:T(8,128)S(1)} %get-tuple-element.17), channel_id=1, replica_groups={{0,8,16,24},{32,40,48,56},{1,9,17,25},{33,41,49,57},{2,10,18,26},{34,42..., dimensions={0}, use_global_device_ids=true | all-gather | bytes 327680 | tf_op jit(solution)/shard_map/all_gather | solution.py:308
  136.7 2.8 %all-to-all-done.4 = bf16[8,256,128]{2,1,0:T(8,128)(2,1)S(1)} async-done(((bf16[8,256,128]{2,1,0:T(8,128)(2,1)}), bf16[8,256,128]{2,1,0:T(8,128)(2,1)S(1)}, u32[]{:S(2)}, u32[]{:S(2)}) %all-to-all-start.4) | async-done | bytes 524320 | tf_op jit(solution)/shard_map/all_to_all | solution.py:277
  139.5 0.7 copy.13
  140.2 0.8 copy.14
  (1 shorter events, 0.0 us)
Async XLA Ops:
  2.0 1.0 copy-start.3
  3.0 7.0 %copy-start.4 = (bf16[128,512]{1,0:T(8,128)(2,1)S(1)}, bf16[128,512]{1,0:T(8,128)(2,1)}, u32[]{:S(2)}) copy-start(bf16[128,512]{1,0:T(8,128)(2,1)} %own_weight.1) | copy-start | bytes 393220
  6.2 3.8 %collective-permute-start = (bf16[8,256,128]{2,1,0:T(8,128)(2,1)S(1)}, bf16[8,256,128]{2,1,0:T(8,128)(2,1)S(1)}, u32[]{:S(2)}, u32[]{:S(2)}) collective-permute-start(bf16[8,256,128]{2,1,0:T(8,128)(2,1)S(1)} %get-tuple-element.12), channel_id=1, source_target_pairs={{0,4},{4,0},{1,5},{5,1},{2,6},{6,2},{3,7},{7,3},{8,12},{12,8},{9,1... | collective-permute-start | bytes 1572872 | tf_op jit(solution)/shard_map/ppermute | solution.py:273
  10.8 0.8 copy-start.2
  11.6 73.2 %copy-start = (bf16[1,1,96,128,128]{4,3,2,1,0:T(8,128)(2,1)S(1)}, bf16[1,1,96,128,128]{4,3,2,1,0:T(8,128)(2,1)}, u32[]{:S(2)}) copy-start(bf16[1,1,96,128,128]{4,3,2,1,0:T(8,128)(2,1)} %param.7) | copy-start | bytes 9437188
  11.6 25.2 %all-to-all-start = ((bf16[8,256,128]{2,1,0:T(8,128)(2,1)}), bf16[8,256,128]{2,1,0:T(8,128)(2,1)}, u32[]{:S(2)}, u32[]{:S(2)}) async-start(bf16[8,256,128]{2,1,0:T(8,128)(2,1)} %copy-done.2), calls=%async_computation | async-start | bytes 1048576 | tf_op jit(solution)/shard_map/all_to_all | solution.py:277
  18.9 7.7 %collective-permute-start.1 = (bf16[128,512]{1,0:T(8,128)(2,1)}, bf16[128,512]{1,0:T(8,128)(2,1)S(1)}, u32[]{:S(2)}, u32[]{:S(2)}) collective-permute-start(bf16[128,512]{1,0:T(8,128)(2,1)} %get-tuple-element.14), channel_id=1, source_target_pairs={{1,0},{2,1},{3,2},{0,3},{7,4},{4,5},{5,6},{6,7},{9,8},{10,9},{11,1... | collective-permute-start | bytes 393224 | tf_op jit(solution)/shard_map/ppermute | solution.py:262
  23.8 8.6 %collective-permute-start.2 = (bf16[128,512]{1,0:T(8,128)(2,1)}, bf16[128,512]{1,0:T(8,128)(2,1)S(1)}, u32[]{:S(2)}, u32[]{:S(2)}) collective-permute-start(bf16[128,512]{1,0:T(8,128)(2,1)} %get-tuple-element.14), channel_id=1, source_target_pairs={{2,0},{3,1},{0,2},{1,3},{6,4},{7,5},{4,6},{5,7},{10,8},{11,9},{8,1... | collective-permute-start | bytes 393224 | tf_op jit(solution)/shard_map/ppermute | solution.py:267
  37.9 0.7 copy-start.1
  38.6 13.0 %all-to-all-start.1 = ((bf16[4,256,128]{2,1,0:T(8,128)(2,1)}), bf16[4,256,128]{2,1,0:T(8,128)(2,1)}, u32[]{:S(2)}, u32[]{:S(2)}) async-start(bf16[4,256,128]{2,1,0:T(8,128)(2,1)} %copy-done.1), calls=%async_computation.1 | async-start | bytes 524288 | tf_op jit(solution)/shard_map/all_to_all | solution.py:277
  51.6 0.9 copy-start.5
  52.5 0.9 copy-start.6
  80.6 4.2 %collective-permute-start.3 = (bf16[8,384,128]{2,1,0:T(8,128)(2,1)S(1)}, bf16[8,384,128]{2,1,0:T(8,128)(2,1)S(1)}, u32[]{:S(2)}, u32[]{:S(2)}) collective-permute-start(bf16[8,384,128]{2,1,0:T(8,128)(2,1)S(1)} %all_to_all.32.mine), channel_id=1, source_target_pairs={{0,4},{4,0},{1,5},{5,1},{2,6},{6,2},{3,7},{7,3},{8,12},{12,8},{9,1... | collective-permute-start | bytes 2359304 | tf_op jit(solution)/shard_map/ppermute | solution.py:273
  119.4 20.1 %all-to-all-start.4 = ((bf16[8,256,128]{2,1,0:T(8,128)(2,1)}), bf16[8,256,128]{2,1,0:T(8,128)(2,1)S(1)}, u32[]{:S(2)}, u32[]{:S(2)}) async-start(bf16[8,256,128]{2,1,0:T(8,128)(2,1)} %bitcast.6), calls=%async_computation.4 | async-start | bytes 1048576 | tf_op jit(solution)/shard_map/all_to_all | solution.py:277

commit v3 on v2

--- a/solution.py
+++ b/solution.py
@@ -34,15 +34,18 @@
     ]
 
 
-def pack_ids(row_ids, col_ids, used, row_blocks, col_blocks):
-    live = jnp.arange(row_ids.shape[0], dtype=jnp.int32) < used
+def pack_ids(row_ids, col_ids, used, row_blocks, col_blocks, *extra):
+    slots = row_ids.shape[0]
+    at = jnp.arange(slots + len(extra), dtype=jnp.int32)
     span = 2 * col_blocks
-    return jnp.where(live, row_ids * span + col_ids, row_blocks * span + col_blocks)
-
-
-def forward_kernel(
-    core, ids_any, values, feats_any, own, other, ids, feats, tiles, acc, sems, more_sems
-):
+    words = jnp.pad(row_ids * span + col_ids, (0, len(extra)))
+    words = jnp.where(at < used, words, row_blocks * span + col_blocks)
+    for k, word in enumerate(extra):
+        words = jnp.where(at == slots + k, word, words)
+    return words
+
+
+def forward_kernel(ids_any, values, feats_any, own, other, ids, feats, tiles, acc, sems, more_sems):
     first = [
         pltpu.make_async_copy(ids_any, ids, more_sems.at[0]),
         pltpu.make_async_copy(feats_any, feats, more_sems.at[1]),
@@ -53,14 +56,16 @@
     acc[...] = jnp.zeros_like(acc)
     for copy in first:
         copy.wait()
+    slots = tiles.shape[0]
     col_blocks, side, _ = feats.shape
+    row_shift = col_blocks.bit_length()
     for chunk, copy in enumerate(copies):
         copy.wait()
         for t in range(chunk * CHUNK, (chunk + 1) * CHUNK):
-            acc[ids[t] // (2 * col_blocks)] += dot(tiles[t], feats[ids[t] % col_blocks])
+            acc[ids[t] >> row_shift] += dot(tiles[t], feats[ids[t] & (col_blocks - 1)])
     ys, grains, _ = own.shape
     blocks = grains // side
-    me = core[0]
+    me = ids[slots]
     for y in range(ys):
         for b in range(blocks):
             rows = pl.ds(b * side, side)
@@ -68,7 +73,7 @@
             other[y, rows, :] = acc[(2 * y + 1 - me) * blocks + b].astype(BF)
 
 
-def forward_tiles(core, ids, values, feats, ys, grains):
+def forward_tiles(ids, values, feats, ys, grains):
     slots, side, _ = values.shape
     width = feats.shape[-1]
     row_blocks = 2 * ys * grains // side
@@ -78,7 +83,7 @@
             jax.ShapeDtypeStruct((ys, grains, width), F4),
             jax.ShapeDtypeStruct((ys, grains, width), BF),
         ),
-        in_specs=[SMEM, ANY, ANY, ANY],
+        in_specs=[ANY, ANY, ANY],
         out_specs=(VMEM, VMEM),
         scratch_shapes=[
             pltpu.SMEM(ids.shape, jnp.int32),
@@ -90,26 +95,7 @@
         ],
         compiler_params=pltpu.CompilerParams(vmem_limit_bytes=FORWARD_VMEM),
         name="forward_tiles",
-    )(core, ids, values, feats)
-
-
-def pair_kernel(own, theirs, weight, pair, lent):
-    pair[...] = (own[...] + theirs[...].astype(F4)).astype(BF)
-    lent[...] = weight[...]
-
-
-def add_pair(own, theirs, weight):
-    return pl.pallas_call(
-        pair_kernel,
-        out_shape=(
-            jax.ShapeDtypeStruct(own.shape, BF),
-            jax.ShapeDtypeStruct(weight.shape, BF),
-        ),
-        in_specs=[VMEM] * 3,
-        out_specs=(VMEM, VMEM),
-        compiler_params=pltpu.CompilerParams(vmem_limit_bytes=VMEM_LIMIT),
-        name="add_pair",
-    )(own, theirs, weight)
+    )(ids, values, feats)
 
 
 def fold_kernel(parts, *refs):
@@ -133,10 +119,10 @@
     )(parts, *before)
 
 
-def dense_kernel(rep, aggs, own_weight, *refs):
+def dense_kernel(rep_at, ids, aggs, own_weight, *refs):
     reps, grains, width = aggs.shape
     others, (cot, act, payload) = refs[: reps - 1], refs[reps - 1 :]
-    me = rep[0]
+    me = ids[rep_at]
     ys, _, side = payload.shape
     own_agg = aggs[me]
     hidden = dot(own_agg, own_weight[...])
@@ -161,12 +147,12 @@
             ]
 
 
-def dense(rep, aggs, weights, cot, ys, side):
+def dense(ids, aggs, weights, cot, ys, side):
     reps, grains, width = aggs.shape
     total = cot.shape[1]
     rows = grains // side * width + width // min(HOLDERS, ys) * (total // side)
     return pl.pallas_call(
-        dense_kernel,
+        functools.partial(dense_kernel, ids.shape[0] - 1),
         out_shape=(
             jax.ShapeDtypeStruct((grains, total), BF),
             jax.ShapeDtypeStruct((ys, rows, side), BF),
@@ -175,10 +161,10 @@
         out_specs=(VMEM, VMEM),
         compiler_params=pltpu.CompilerParams(vmem_limit_bytes=VMEM_LIMIT),
         name="dense",
-    )(rep, aggs, *weights, cot)
-
-
-def backward_kernel(ids, core, tiles, mine, theirs, payload, acc):
+    )(ids, aggs, *weights, cot)
+
+
+def backward_kernel(ids, tiles, mine, theirs, payload, acc):
     acc[...] = jnp.zeros_like(acc)
     side = tiles.shape[1]
     width = acc.shape[1]
@@ -188,12 +174,18 @@
     per_row = col_blocks // rows
     base = per_row * width
 
-    for t in range(tiles.shape[0]):
-        b = ids[t] // (2 * col_blocks) % (2 * ys * per_row)
-        device = b // per_row
-        block = pl.ds(pl.multiple_of((b % per_row) * width, width), width)
-        grad = jnp.where(device % 2 == core[0], mine[device // 2, block], theirs[device // 2, block])
-        acc[ids[t] % (2 * col_blocks)] += dot(grad, tiles[t])
+    slots = tiles.shape[0]
+    row_shift = col_blocks.bit_length()
+    core_shift = row_shift + per_row.bit_length() - 1
+    me = ids[slots]
+    for t in range(slots):
+        word = ids[t]
+        start = ((word >> row_shift) & (per_row - 1)) * width
+        block = pl.ds(pl.multiple_of(start, width), width)
+        y = (word >> (core_shift + 1)) & (ys - 1)
+        local = ((word >> core_shift) & 1) == me
+        grad = jnp.where(local, mine[y, block], theirs[y, block])
+        acc[word & (2 * col_blocks - 1)] += dot(grad, tiles[t])
     share = jnp.zeros((payload.shape[1] - base, side), F4)
     for grads in (mine, theirs):
         for y in range(ys):
@@ -205,18 +197,18 @@
         payload[r, base:, :] = share
 
 
-def backward_tiles(ids, core, values, mine, theirs, rows, col_blocks):
+def backward_tiles(ids, values, mine, theirs, rows, col_blocks):
     side = values.shape[1]
     length = mine.shape[1]
     return pl.pallas_call(
         backward_kernel,
         out_shape=jax.ShapeDtypeStruct((rows, length, side), BF),
-        in_specs=[SMEM] * 2 + [VMEM] * 3,
+        in_specs=[SMEM] + [VMEM] * 3,
         out_specs=VMEM,
         scratch_shapes=[pltpu.VMEM((col_blocks + 1, side, side), F4)],
         compiler_params=pltpu.CompilerParams(vmem_limit_bytes=VMEM_LIMIT),
         name="backward_tiles",
-    )(ids, core, values, mine, theirs)
+    )(ids, values, mine, theirs)
 
 
 def finish_kernel(scale, parts, grad, share):
@@ -251,20 +243,55 @@
     )(parts)
 
 
-def fetch_others(weight):
-    reps = lax.axis_size("rep")
-    if reps != 4:
+def deliver_kernel(holders, chunk_at, ids, grad, *refs):
+    pieces, (grad_out, weight_out, sems) = refs[:holders], refs[holders:]
+    part = weight_out.shape[0] // holders
+    copies = [pltpu.make_async_copy(grad, grad_out, sems.at[holders])]
+    for k, piece in enumerate(pieces):
+        start = ((ids[chunk_at] + k) & (holders - 1)) * part
+        place = weight_out.at[pl.ds(pl.multiple_of(start, part), part)]
+        copies.append(pltpu.make_async_copy(piece, place, sems.at[k]))
+    for copy in copies:
+        copy.start()
+    for copy in copies:
+        copy.wait()
+
+
+def deliver(ids, chunk_at, grad, pieces):
+    holders = len(pieces)
+    part, total = pieces[0].shape
+    return pl.pallas_call(
+        functools.partial(deliver_kernel, holders, chunk_at),
+        out_shape=(
+            jax.ShapeDtypeStruct(grad.shape, BF),
+            jax.ShapeDtypeStruct((part * holders, total), F4),
+        ),
+        in_specs=[SMEM] + [ANY] * (1 + holders),
+        out_specs=(ANY, ANY),
+        scratch_shapes=[pltpu.SemaphoreType.DMA((holders + 1,))],
+        compiler_params=pltpu.CompilerParams(vmem_limit_bytes=VMEM_LIMIT),
+        name="deliver",
+    )(ids, grad, *pieces)
+
+
+def around(x, axis, count):
+    n = lax.axis_size(axis)
+    if count != 4:
         return [
-            lax.ppermute(weight, "rep", [((i + k) % reps, i) for i in range(reps)])
-            for k in range(1, reps)
+            lax.ppermute(x, axis, [((i + k) % n, i) for i in range(n)]) for k in range(1, count)
         ]
-    steps = [(0, 1), (1, -1)]
+    names, place = (("y", "core"), (2, 1)) if axis == "y" else (("core", axis), (1, n))
+    step, core = place
     sides = lax.ppermute(
-        weight,
-        ("core", "rep"),
-        [(c * reps + (i + k) % reps, c * reps + i) for c, k in steps for i in range(reps)],
-    )
-    across = lax.ppermute(weight, "rep", [((i + 2) % reps, i) for i in range(reps)])
+        x,
+        names,
+        [
+            ((i + k) % n * step + c * core, i * step + c * core)
+            for c, k in ((0, 1), (1, -1))
+            for i in range(n)
+        ],
+    )
+    across = lax.ppermute(x, axis, [((i + 2) % n, i) for i in range(n)])
     sides = lax.all_gather(sides, "core", axis=0)
     return [sides[0], across, sides[1]]
 
@@ -279,8 +306,6 @@
 
 def body(tile_values, tile_rows, tile_cols, tile_count, features, weight, cotangent):
     values = tile_values[0, 0]
-    core = lax.axis_index("core").astype(jnp.int32).reshape(1)
-    rep = lax.axis_index("rep").astype(jnp.int32).reshape(1)
     side = values.shape[-1]
     width = features.shape[1]
     grains, total = cotangent.shape
@@ -290,22 +315,28 @@
     nodes = grains * rows * ys * 2
     holders = min(HOLDERS, ys)
 
-    ids = pack_ids(tile_rows[0, 0], tile_cols[0, 0], tile_count[0, 0], row_blocks, col_blocks)
+    slots = values.shape[0]
+    where = [lax.axis_index(a).astype(jnp.int32) for a in ("core", "y", "rep")]
+    ids = pack_ids(
+        tile_rows[0, 0], tile_cols[0, 0], tile_count[0, 0], row_blocks, col_blocks, *where
+    )
     feats = features.reshape(col_blocks, side, width)
-    own, other = forward_tiles(core, ids, values, feats, ys, grains)
-    pair, lent = add_pair(own, swap_cores(other), weight)
+    own, other = forward_tiles(ids, values, feats, ys, grains)
+    pair = (own + swap_cores(other).astype(F4)).astype(BF)
+    pair, lent = lax.optimization_barrier((pair, weight))
     parts = exchange(pair, "y")
-    others = fetch_others(lent)
+    others = around(lent, "rep", reps)
     aggs = exchange(fold(parts, reps, others), "rep")
-    activation, payload = dense(rep, aggs, [weight, *others], cotangent, ys, side)
+    activation, payload = dense(ids, aggs, [weight, *others], cotangent, ys, side)
     mine = exchange(payload, "y")
     theirs = swap_cores(mine)
-    back = backward_tiles(ids, core, values, mine, theirs, rows, col_blocks)
+    back = backward_tiles(ids, values, mine, theirs, rows, col_blocks)
     sums = exchange(back, "row")
     grad, share = finish(sums, 1.0 / math.sqrt(nodes), grains, width // holders, total)
     input_grad = exchange(grad, "row")
-    groups = [list(range(y, y + holders)) for y in range(0, ys, holders)]
-    weight_grad = lax.all_gather(share, "y", axis_index_groups=groups, tiled=True)
+    input_grad, weight_grad = deliver(
+        ids, slots + 1, input_grad, [share, *around(share, "y", holders)]
+    )
     return (activation, weight_grad, input_grad)
 
 

time: 142 us -> 138 us (0.972)
  local copies, waits for them, and re-layouts: 5.9 us -> 2.02 us
  starting transfers between devices: 28.7 us -> 26.4 us
    all_to_all x2 -> x3, blocking collectives: 55.4 us -> 68.1 us  [exchange(): return lax.all_to_all(x, axis, 0, 0, tiled=True)]
    all_gather x2, blocking collectives: 16.2 us -> 4.28 us  [around(): sides = lax.all_gather(sides, 'core', axis=0)]
    all_to_all x3 -> x2, starting transfers between devices: 18 us -> 10.9 us  [exchange(): return lax.all_to_all(x, axis, 0, 0, tiled=True)]
    ppermute x2 -> x4, starting transfers between devices: 6.84 us -> 11.7 us  [the longest x2 6.8 us: around(): lax.ppermute(x, names, [((i + k) % n * step + c * core, i * step + c * co...]
    unnamed x16 -> x6, local copies, waits for them, and re-layouts: 5.89 us -> 1.99 us
    ppermute x2 -> x4, waiting for transfers between devices: 4.24 us -> 6.47 us  [the longest x2 4.38 us: around(): across = lax.ppermute(x, axis, [((i + 2) % n, i) for i in range(n)])]
    all_to_all x3 -> x2, waiting for transfers between devices: 13 us -> 11.9 us  [exchange(): return lax.all_to_all(x, axis, 0, 0, tiled=True)]
  transfers between devices with their start and end apart: 7 -> 8, of which waited for: 7 -> 8; matrix products, arithmetic and copies ran while one was open for 0% -> 0% of each run, Pallas kernels for 0% -> 0%
where the time goes in v3:
time: 138 us; the launch traced here: 137 us
  blocking collectives  72.3 us (52%)
  starting transfers between devices  26.4 us (19%)
  waiting for transfers between devices  22.5 us (16%)
  Pallas kernels  10.8 us (8%)
  local copies, waits for them, and re-layouts  2.02 us (1%)
  other arithmetic  1.58 us (1%)
    all_to_all x3, blocking collectives, exchange(): return lax.all_to_all(x, axis, 0, 0, tiled=True)  68.1 us
    all_to_all x2, waiting for transfers between devices, exchange(): return lax.all_to_all(x, axis, 0, 0, tiled=True)  11.9 us
    all_to_all x2, starting transfers between devices, exchange(): return lax.all_to_all(x, axis, 0, 0, tiled=True)  10.9 us
    ppermute x2, starting transfers between devices, around(): lax.ppermute(x, names, [((i + k) % n * step + c * core, i * step + c * co...  6.8 us
    ppermute x2, starting transfers between devices, around(): across = lax.ppermute(x, axis, [((i + 2) % n, i) for i in range(n)])  4.94 us
    ppermute x2, waiting for transfers between devices, around(): across = lax.ppermute(x, axis, [((i + 2) % n, i) for i in range(n)])  4.38 us
    all_gather x2, blocking collectives, around(): sides = lax.all_gather(sides, 'core', axis=0)  4.28 us
    ppermute x2, waiting for transfers between devices, swap_cores(): return lax.ppermute(x, 'core', [(0, 1), (1, 0)])  4.13 us
  transfers between devices with their start and end apart: 8, of which 8 were waited for; matrix products, arithmetic and copies ran while one was open for 0% of the time, Pallas kernels for 0%

profile of v3, /device:TPU:2, one launch (start us, length us, event | category | flops | bytes accessed | tf_op | source)
XLA Modules:
  0.0 137.1 jit_solution(4214235904439355037)
XLA Ops:
  1.3 0.7 add_bitcast_fusion
  2.0 0.0 copy-start.1
  2.0 1.0 copy-done.1
  3.0 3.1 %forward_tiles.1 = (f32[8,256,128]{2,1,0:T(8,128)S(1)}, bf16[8,256,128]{2,1,0:T(8,128)(2,1)S(1)}) custom-call(s32[99]{0:T(128)S(1)} %compare_select_fusion.3.ids_any.ids, bf16[96,128,128]{2,1,0:T(8,128)(2,1)} %bitcast.8, bf16[16,128,128]{2,1,0:T(8,128)(2,1)S(1)} %bitcast.11), custom_call_target="tpu_custom_call" | custom-call | tf_op jit(solution)/shard_map/forward_tiles/pallas_call | solution.py:80
  6.2 1.9 %collective-permute-start = (bf16[8,256,128]{2,1,0:T(8,128)(2,1)S(1)}, bf16[8,256,128]{2,1,0:T(8,128)(2,1)S(1)}, u32[]{:S(2)}, u32[]{:S(2)}) collective-permute-start(bf16[8,256,128]{2,1,0:T(8,128)(2,1)S(1)} %get-tuple-element.14), channel_id=1, source_target_pairs={{0,4},{4,0},{1,5},{5,1},{2,6},{6,2},{3,7},{7,3},{8,12},{12,8},{9,1... | collective-permute-start | bytes 1572872 | tf_op jit(solution)/shard_map/ppermute | solution.py:300
  8.1 1.9 %collective-permute-done = bf16[8,256,128]{2,1,0:T(8,128)(2,1)S(1)} collective-permute-done((bf16[8,256,128]{2,1,0:T(8,128)(2,1)S(1)}, bf16[8,256,128]{2,1,0:T(8,128)(2,1)S(1)}, u32[]{:S(2)}, u32[]{:S(2)}) %collective-permute-start) | collective-permute-done | bytes 524320 | tf_op jit(solution)/shard_map/ppermute | solution.py:300
  10.0 0.9 add_convert_fusion
  10.9 0.0 copy-start
  10.9 7.4 %all-to-all-start = ((bf16[8,256,128]{2,1,0:T(8,128)(2,1)}), bf16[8,256,128]{2,1,0:T(8,128)(2,1)}, u32[]{:S(2)}, u32[]{:S(2)}) async-start(bf16[8,256,128]{2,1,0:T(8,128)(2,1)} %add_convert_fusion), calls=%async_computation | async-start | bytes 1048576 | tf_op jit(solution)/shard_map/all_to_all | solution.py:304
  18.2 4.9 %collective-permute-start.1 = (bf16[128,512]{1,0:T(8,128)(2,1)}, bf16[128,512]{1,0:T(8,128)(2,1)S(1)}, u32[]{:S(2)}, u32[]{:S(2)}) collective-permute-start(bf16[128,512]{1,0:T(8,128)(2,1)} %own_weight.1), channel_id=1, source_target_pairs={{1,0},{2,1},{3,2},{0,3},{7,4},{4,5},{5,6},{6,7},{9,8},{10,9},{11,1... | collective-permute-start | bytes 393224 | tf_op jit(solution)/shard_map/ppermute | solution.py:285
  23.1 1.9 %collective-permute-start.2 = (bf16[128,512]{1,0:T(8,128)(2,1)}, bf16[128,512]{1,0:T(8,128)(2,1)S(1)}, u32[]{:S(2)}, u32[]{:S(2)}) collective-permute-start(bf16[128,512]{1,0:T(8,128)(2,1)} %own_weight.1), channel_id=1, source_target_pairs={{2,0},{3,1},{0,2},{1,3},{6,4},{7,5},{4,6},{5,7},{10,8},{11,9},{8,1... | collective-permute-start | bytes 393224 | tf_op jit(solution)/shard_map/ppermute | solution.py:294
  25.1 0.9 collective-permute-done.1
  25.9 2.4 %all-gather = bf16[256,512]{1,0:T(8,128)(2,1)S(1)} all-gather(bf16[128,512]{1,0:T(8,128)(2,1)S(1)} %collective-permute-done.1), channel_id=2, replica_groups=mesh['row'=8,'y'=8,'core'=2,'rep'=4] {'core'}, dimensions={0}, use_global_device_ids=true | all-gather | bytes 393216 | tf_op jit(solution)/shard_map/all_gather | solution.py:295
  28.3 3.4 %collective-permute-done.2.refs_1_ = bf16[128,512]{1,0:T(8,128)(2,1)S(1)} collective-permute-done((bf16[128,512]{1,0:T(8,128)(2,1)}, bf16[128,512]{1,0:T(8,128)(2,1)S(1)}, u32[]{:S(2)}, u32[]{:S(2)}) %collective-permute-start.2) | collective-permute-done | bytes 131104 | tf_op jit(solution)/shard_map/ppermute | solution.py:294
  31.7 4.4 %all-to-all-done.parts = bf16[8,256,128]{2,1,0:T(8,128)(2,1)} async-done(((bf16[8,256,128]{2,1,0:T(8,128)(2,1)}), bf16[8,256,128]{2,1,0:T(8,128)(2,1)}, u32[]{:S(2)}, u32[]{:S(2)}) %all-to-all-start) | async-done | bytes 524320 | tf_op jit(solution)/shard_map/all_to_all | solution.py:304
  36.1 1.1 fold.1
  37.2 11.3 %all_to_all.31.aggs = bf16[4,256,128]{2,1,0:T(8,128)(2,1)S(1)} all-to-all(bf16[4,256,128]{2,1,0:T(8,128)(2,1)S(1)} %fold.1), channel_id=1, replica_groups=mesh['row'=8,'y'=8,'core'=2,'rep'=4] {'rep'}, dimensions={0} | all-to-all | bytes 524288 | tf_op jit(solution)/shard_map/all_to_all | solution.py:304
  48.5 0.0 copy-start.2
  48.5 0.9 copy-done.2
  49.5 2.2 %dense.1 = (bf16[256,512]{1,0:T(8,128)(2,1)}, bf16[8,384,128]{2,1,0:T(8,128)(2,1)S(1)}) custom-call(s32[99]{0:T(128)S(1)} %compare_select_fusion.3.ids_any.ids, bf16[4,256,128]{2,1,0:T(8,128)(2,1)S(1)} %all_to_all.31.aggs, bf16[128,512]{1,0:T(8,128)(2,1)} %own_weight.1, bf16[128,512]{1,0:T(8,128)(2,1)S(1)} %get-tuple-element.24.refs_0_, ...), custom_call_target="tpu_custom_call" | custom-call | tf_op jit(solution)/shard_map/dense/pallas_call | solution.py:154
  51.6 25.1 %all_to_all.32.mine = bf16[8,384,128]{2,1,0:T(8,128)(2,1)S(1)} all-to-all(bf16[8,384,128]{2,1,0:T(8,128)(2,1)S(1)} %get-tuple-element.18), channel_id=1, replica_groups=mesh['row'=8,'y'=8,'core'=2,'rep'=4] {'y'}, dimensions={0} | all-to-all | bytes 1572864 | tf_op jit(solution)/shard_map/all_to_all | solution.py:304
  76.8 1.9 %collective-permute-start.3 = (bf16[8,384,128]{2,1,0:T(8,128)(2,1)S(1)}, bf16[8,384,128]{2,1,0:T(8,128)(2,1)S(1)}, u32[]{:S(2)}, u32[]{:S(2)}) collective-permute-start(bf16[8,384,128]{2,1,0:T(8,128)(2,1)S(1)} %all_to_all.32.mine), channel_id=1, source_target_pairs={{0,4},{4,0},{1,5},{5,1},{2,6},{6,2},{3,7},{7,3},{8,12},{12,8},{9,1... | collective-permute-start | bytes 2359304 | tf_op jit(solution)/shard_map/ppermute | solution.py:300
  78.7 2.3 %collective-permute-done.3.theirs = bf16[8,384,128]{2,1,0:T(8,128)(2,1)S(1)} collective-permute-done((bf16[8,384,128]{2,1,0:T(8,128)(2,1)S(1)}, bf16[8,384,128]{2,1,0:T(8,128)(2,1)S(1)}, u32[]{:S(2)}, u32[]{:S(2)}) %collective-permute-start.3) | collective-permute-done | bytes 786464 | tf_op jit(solution)/shard_map/ppermute | solution.py:300
  80.9 0.0 copy-done
  80.9 2.0 %backward_tiles.1 = bf16[8,384,128]{2,1,0:T(8,128)(2,1)S(1)} custom-call(s32[99]{0:T(128)S(1)} %compare_select_fusion.3.ids_any.ids, bf16[96,128,128]{2,1,0:T(8,128)(2,1)S(1)} %bitcast.9, bf16[8,384,128]{2,1,0:T(8,128)(2,1)S(1)} %all_to_all.32.mine, bf16[8,384,128]{2,1,0:T(8,128)(2,1)S(1)} %collective-permute-done.3.theirs), custom_call_target="tpu_custom_call" | custom-call | tf_op jit(solution)/shard_map/backward_tiles/pallas_call | solution.py:203
  83.0 31.6 %all_to_all.33.parts = bf16[8,384,128]{2,1,0:T(8,128)(2,1)S(1)} all-to-all(bf16[8,384,128]{2,1,0:T(8,128)(2,1)S(1)} %backward_tiles.1), channel_id=1, replica_groups=mesh['row'=8,'y'=8,'core'=2,'rep'=4] {'row'}, dimensions={0} | all-to-all | bytes 1572864 | tf_op jit(solution)/shard_map/all_to_all | solution.py:304
  114.6 1.0 finish.1
  115.6 3.5 %all-to-all-start.4 = ((bf16[8,256,128]{2,1,0:T(8,128)(2,1)}), bf16[8,256,128]{2,1,0:T(8,128)(2,1)S(1)}, u32[]{:S(2)}, u32[]{:S(2)}) async-start(bf16[8,256,128]{2,1,0:T(8,128)(2,1)} %bitcast.4), calls=%async_computation.4 | async-start | bytes 1048576 | tf_op jit(solution)/shard_map/all_to_all | solution.py:304
  119.1 1.9 %collective-permute-start.4 = (f32[32,512]{1,0:T(8,128)S(1)}, f32[32,512]{1,0:T(8,128)S(1)}, u32[]{:S(2)}, u32[]{:S(2)}) collective-permute-start(f32[32,512]{1,0:T(8,128)S(1)} %get-tuple-element.20.refs_0_), channel_id=1, source_target_pairs={{8,0},{16,8},{24,16},{32,24},{40,32},{48,40},{56,48},{0,56},{60,4}... | collective-permute-start | bytes 196616 | tf_op jit(solution)/shard_map/ppermute | solution.py:285
  121.0 3.0 %collective-permute-start.5 = (f32[32,512]{1,0:T(8,128)S(1)}, f32[32,512]{1,0:T(8,128)S(1)}, u32[]{:S(2)}, u32[]{:S(2)}) collective-permute-start(f32[32,512]{1,0:T(8,128)S(1)} %get-tuple-element.20.refs_0_), channel_id=1, source_target_pairs={{16,0},{24,8},{32,16},{40,24},{48,32},{56,40},{0,48},{8,56},{17,1}... | collective-permute-start | bytes 196616 | tf_op jit(solution)/shard_map/ppermute | solution.py:294
  124.0 1.2 collective-permute-done.4
  125.2 1.9 %all-gather.1 = f32[64,512]{1,0:T(8,128)S(1)} all-gather(f32[32,512]{1,0:T(8,128)S(1)} %collective-permute-done.4), channel_id=3, replica_groups=mesh['row'=8,'y'=8,'core'=2,'rep'=4] {'core'}, dimensions={0}, use_global_device_ids=true | all-gather | bytes 196608 | tf_op jit(solution)/shard_map/all_gather | solution.py:295
  127.1 1.0 collective-permute-done.5.refs_2_
  128.2 7.5 %all-to-all-done.4 = bf16[8,256,128]{2,1,0:T(8,128)(2,1)S(1)} async-done(((bf16[8,256,128]{2,1,0:T(8,128)(2,1)}), bf16[8,256,128]{2,1,0:T(8,128)(2,1)S(1)}, u32[]{:S(2)}, u32[]{:S(2)}) %all-to-all-start.4) | async-done | bytes 524320 | tf_op jit(solution)/shard_map/all_to_all | solution.py:304
  135.6 1.4 %deliver.1 = (bf16[2048,128]{1,0:T(8,128)(2,1)}, f32[128,512]{1,0:T(8,128)}) custom-call(s32[99]{0:T(128)S(1)} %compare_select_fusion.3.ids_any.ids, bf16[2048,128]{1,0:T(8,128)(2,1)S(1)} %bitcast.10, f32[32,512]{1,0:T(8,128)S(1)} %get-tuple-element.20.refs_0_, f32[32,512]{1,0:T(8,128)S(1)} %get-tuple-element.26.refs_1_, ...), custom_call_target="tpu_custom_call" | custom-call | tf_op jit(solution)/shard_map/deliver/pallas_call | solution.py:263
  (3 shorter events, 0.0 us)
Async XLA Ops:
  2.0 1.0 copy-start.1
  6.2 3.8 %collective-permute-start = (bf16[8,256,128]{2,1,0:T(8,128)(2,1)S(1)}, bf16[8,256,128]{2,1,0:T(8,128)(2,1)S(1)}, u32[]{:S(2)}, u32[]{:S(2)}) collective-permute-start(bf16[8,256,128]{2,1,0:T(8,128)(2,1)S(1)} %get-tuple-element.14), channel_id=1, source_target_pairs={{0,4},{4,0},{1,5},{5,1},{2,6},{6,2},{3,7},{7,3},{8,12},{12,8},{9,1... | collective-permute-start | bytes 1572872 | tf_op jit(solution)/shard_map/ppermute | solution.py:300
  10.9 70.1 %copy-start = (bf16[1,1,96,128,128]{4,3,2,1,0:T(8,128)(2,1)S(1)}, bf16[1,1,96,128,128]{4,3,2,1,0:T(8,128)(2,1)}, u32[]{:S(2)}) copy-start(bf16[1,1,96,128,128]{4,3,2,1,0:T(8,128)(2,1)} %param.7) | copy-start | bytes 9437188
  10.9 25.3 %all-to-all-start = ((bf16[8,256,128]{2,1,0:T(8,128)(2,1)}), bf16[8,256,128]{2,1,0:T(8,128)(2,1)}, u32[]{:S(2)}, u32[]{:S(2)}) async-start(bf16[8,256,128]{2,1,0:T(8,128)(2,1)} %add_convert_fusion), calls=%async_computation | async-start | bytes 1048576 | tf_op jit(solution)/shard_map/all_to_all | solution.py:304
  18.2 7.7 %collective-permute-start.1 = (bf16[128,512]{1,0:T(8,128)(2,1)}, bf16[128,512]{1,0:T(8,128)(2,1)S(1)}, u32[]{:S(2)}, u32[]{:S(2)}) collective-permute-start(bf16[128,512]{1,0:T(8,128)(2,1)} %own_weight.1), channel_id=1, source_target_pairs={{1,0},{2,1},{3,2},{0,3},{7,4},{4,5},{5,6},{6,7},{9,8},{10,9},{11,1... | collective-permute-start | bytes 393224 | tf_op jit(solution)/shard_map/ppermute | solution.py:285
  23.1 8.6 %collective-permute-start.2 = (bf16[128,512]{1,0:T(8,128)(2,1)}, bf16[128,512]{1,0:T(8,128)(2,1)S(1)}, u32[]{:S(2)}, u32[]{:S(2)}) collective-permute-start(bf16[128,512]{1,0:T(8,128)(2,1)} %own_weight.1), channel_id=1, source_target_pairs={{2,0},{3,1},{0,2},{1,3},{6,4},{7,5},{4,6},{5,7},{10,8},{11,9},{8,1... | collective-permute-start | bytes 393224 | tf_op jit(solution)/shard_map/ppermute | solution.py:294
  48.5 1.0 copy-start.2
  76.8 4.2 %collective-permute-start.3 = (bf16[8,384,128]{2,1,0:T(8,128)(2,1)S(1)}, bf16[8,384,128]{2,1,0:T(8,128)(2,1)S(1)}, u32[]{:S(2)}, u32[]{:S(2)}) collective-permute-start(bf16[8,384,128]{2,1,0:T(8,128)(2,1)S(1)} %all_to_all.32.mine), channel_id=1, source_target_pairs={{0,4},{4,0},{1,5},{5,1},{2,6},{6,2},{3,7},{7,3},{8,12},{12,8},{9,1... | collective-permute-start | bytes 2359304 | tf_op jit(solution)/shard_map/ppermute | solution.py:300
  115.6 20.1 %all-to-all-start.4 = ((bf16[8,256,128]{2,1,0:T(8,128)(2,1)}), bf16[8,256,128]{2,1,0:T(8,128)(2,1)S(1)}, u32[]{:S(2)}, u32[]{:S(2)}) async-start(bf16[8,256,128]{2,1,0:T(8,128)(2,1)} %bitcast.4), calls=%async_computation.4 | async-start | bytes 1048576 | tf_op jit(solution)/shard_map/all_to_all | solution.py:304
  119.1 6.2 %collective-permute-start.4 = (f32[32,512]{1,0:T(8,128)S(1)}, f32[32,512]{1,0:T(8,128)S(1)}, u32[]{:S(2)}, u32[]{:S(2)}) collective-permute-start(f32[32,512]{1,0:T(8,128)S(1)} %get-tuple-element.20.refs_0_), channel_id=1, source_target_pairs={{8,0},{16,8},{24,16},{32,24},{40,32},{48,40},{56,48},{0,56},{60,4}... | collective-permute-start | bytes 196616 | tf_op jit(solution)/shard_map/ppermute | solution.py:285
  121.0 7.2 %collective-permute-start.5 = (f32[32,512]{1,0:T(8,128)S(1)}, f32[32,512]{1,0:T(8,128)S(1)}, u32[]{:S(2)}, u32[]{:S(2)}) collective-permute-start(f32[32,512]{1,0:T(8,128)S(1)} %get-tuple-element.20.refs_0_), channel_id=1, source_target_pairs={{16,0},{24,8},{32,16},{40,24},{48,32},{56,40},{0,48},{8,56},{17,1}... | collective-permute-start | bytes 196616 | tf_op jit(solution)/shard_map/ppermute | solution.py:294

commit v4 on v3

--- a/solution.py
+++ b/solution.py
@@ -10,8 +10,7 @@
 from jax.sharding import PartitionSpec as P
 
 VMEM_LIMIT = 40 * 1024 * 1024
-FORWARD_VMEM = 51 * 1024 * 1024
-CHUNK = 16
+PIECES = 2
 BF = jnp.bfloat16
 F4 = jnp.float32
 
@@ -21,25 +20,30 @@
 HOLDERS = 4
 
 
+def in_hbm(x):
+    return pltpu.with_memory_space_constraint(x, pltpu.HBM)
+
+
 def dot(a, b, dims=(((1,), (0,)), ((), ()))):
     return lax.dot_general(a, b, dims, preferred_element_type=F4)
 
 
 def tile_copies(values, tiles, sems):
+    piece = tiles.shape[0] // PIECES
+    spans = [pl.ds(k * piece, piece) for k in range(PIECES)]
     return [
-        pltpu.make_async_copy(
-            values.at[pl.ds(first, CHUNK)], tiles.at[pl.ds(first, CHUNK)], sems.at[first // CHUNK]
-        )
-        for first in range(0, tiles.shape[0], CHUNK)
+        pltpu.make_async_copy(values.at[span], tiles.at[span], sems.at[k])
+        for k, span in enumerate(spans)
     ]
 
 
 def pack_ids(row_ids, col_ids, used, row_blocks, col_blocks, *extra):
     slots = row_ids.shape[0]
+    at = jnp.arange(slots, dtype=jnp.int32)
+    span = 2 * col_blocks
+    words = jnp.where(at < used, row_ids * span + col_ids, row_blocks * span + col_blocks)
     at = jnp.arange(slots + len(extra), dtype=jnp.int32)
-    span = 2 * col_blocks
-    words = jnp.pad(row_ids * span + col_ids, (0, len(extra)))
-    words = jnp.where(at < used, words, row_blocks * span + col_blocks)
+    words = jnp.pad(words, (0, len(extra)))
     for k, word in enumerate(extra):
         words = jnp.where(at == slots + k, word, words)
     return words
@@ -59,9 +63,10 @@
     slots = tiles.shape[0]
     col_blocks, side, _ = feats.shape
     row_shift = col_blocks.bit_length()
-    for chunk, copy in enumerate(copies):
+    piece = slots // PIECES
+    for k, copy in enumerate(copies):
         copy.wait()
-        for t in range(chunk * CHUNK, (chunk + 1) * CHUNK):
+        for t in range(k * piece, (k + 1) * piece):
             acc[ids[t] >> row_shift] += dot(tiles[t], feats[ids[t] & (col_blocks - 1)])
     ys, grains, _ = own.shape
     blocks = grains // side
@@ -90,38 +95,62 @@
             pltpu.VMEM(feats.shape, BF),
             pltpu.VMEM((slots, side, side), BF),
             pltpu.VMEM((row_blocks + 1, side, width), F4),
-            pltpu.SemaphoreType.DMA((slots // CHUNK,)),
+            pltpu.SemaphoreType.DMA((PIECES,)),
             pltpu.SemaphoreType.DMA((2,)),
         ],
-        compiler_params=pltpu.CompilerParams(vmem_limit_bytes=FORWARD_VMEM),
+        compiler_params=pltpu.CompilerParams(vmem_limit_bytes=VMEM_LIMIT),
         name="forward_tiles",
-    )(ids, values, feats)
-
-
-def fold_kernel(parts, *refs):
-    copies = refs[-1]
+    )(ids, in_hbm(values), in_hbm(feats))
+
+
+def fold_kernel(parts_hbm, weight_hbm, cot_hbm, *refs):
+    copies, weight, cot, parts, sems, more_sems = refs[-6:]
+    bring = [
+        pltpu.make_async_copy(parts_hbm.at[y], parts.at[y], sems.at[y])
+        for y in range(parts.shape[0])
+    ]
+    more = [
+        pltpu.make_async_copy(weight_hbm, weight, more_sems.at[0]),
+        pltpu.make_async_copy(cot_hbm, cot, more_sems.at[1]),
+    ]
+    for copy in bring + more:
+        copy.start()
+    bring[0].wait()
     total = parts[0].astype(F4)
     for y in range(1, parts.shape[0]):
+        bring[y].wait()
         total += parts[y].astype(F4)
     total = total.astype(BF)
     for q in range(copies.shape[0]):
         copies[q] = total
-
-
-def fold(parts, copies, before):
+    for copy in more:
+        copy.wait()
+
+
+def fold(parts, weight, cot, copies, before):
     return pl.pallas_call(
         fold_kernel,
-        out_shape=jax.ShapeDtypeStruct((copies,) + parts.shape[1:], BF),
-        in_specs=[VMEM] + [ANY] * len(before),
-        out_specs=VMEM,
+        out_shape=(
+            jax.ShapeDtypeStruct((copies,) + parts.shape[1:], BF),
+            pltpu.VMEM(weight.shape, BF),
+            pltpu.VMEM(cot.shape, BF),
+        ),
+        in_specs=[ANY] * (3 + len(before)),
+        out_specs=(VMEM,) * 3,
+        scratch_shapes=[
+            pltpu.VMEM(parts.shape, BF),
+            pltpu.SemaphoreType.DMA(parts.shape[:1]),
+            pltpu.SemaphoreType.DMA((2,)),
+        ],
         compiler_params=pltpu.CompilerParams(vmem_limit_bytes=VMEM_LIMIT),
         name="fold",
-    )(parts, *before)
+    )(in_hbm(parts), in_hbm(weight), in_hbm(cot), *before)
 
 
 def dense_kernel(rep_at, ids, aggs, own_weight, *refs):
     reps, grains, width = aggs.shape
-    others, (cot, act, payload) = refs[: reps - 1], refs[reps - 1 :]
+    others, (cot, act_hbm, payload, act, sem) = refs[: reps - 1], refs[reps - 1 :]
+    take_act = pltpu.make_async_copy(act, act_hbm, sem)
     me = ids[rep_at]
     ys, _, side = payload.shape
     own_agg = aggs[me]
@@ -130,6 +159,7 @@
         hidden += dot(aggs[(me + k + 1) % reps], weight[...])
     sigma = jax.nn.sigmoid(hidden)
     act[...] = (hidden * sigma).astype(BF)
+    take_act.start()
     slope = sigma * (1.0 + hidden * (1.0 - sigma))
     grad_hidden = (cot[...].astype(F4) * slope).astype(BF)
     back = dot(own_weight[...], grad_hidden, (((1,), (1,)), ((), ()))).astype(BF)
@@ -145,9 +175,10 @@
             payload[y, pl.ds(base + k * part, part), :] = share[
                 chunk * part : (chunk + 1) * part, k * side : (k + 1) * side
             ]
-
-
-def dense(ids, aggs, weights, cot, ys, side):
+    take_act.wait()
+
+
+def dense(ids, aggs, weight, others, cot, ys, side):
     reps, grains, width = aggs.shape
     total = cot.shape[1]
     rows = grains // side * width + width // min(HOLDERS, ys) * (total // side)
@@ -157,11 +188,12 @@
             jax.ShapeDtypeStruct((grains, total), BF),
             jax.ShapeDtypeStruct((ys, rows, side), BF),
         ),
-        in_specs=[SMEM] + [VMEM] * (reps + 2),
-        out_specs=(VMEM, VMEM),
+        in_specs=[SMEM] + [VMEM] * (2 + reps),
+        out_specs=(ANY, VMEM),
+        scratch_shapes=[pltpu.VMEM((grains, total), BF), pltpu.SemaphoreType.DMA],
         compiler_params=pltpu.CompilerParams(vmem_limit_bytes=VMEM_LIMIT),
         name="dense",
-    )(ids, aggs, *weights, cot)
+    )(ids, aggs, weight, *others, cot)
 
 
 def backward_kernel(ids, tiles, mine, theirs, payload, acc):
@@ -243,35 +275,24 @@
     )(parts)
 
 
-def deliver_kernel(holders, chunk_at, ids, grad, *refs):
-    pieces, (grad_out, weight_out, sems) = refs[:holders], refs[holders:]
-    part = weight_out.shape[0] // holders
-    copies = [pltpu.make_async_copy(grad, grad_out, sems.at[holders])]
+def place_kernel(chunk_at, ids, *refs):
+    pieces, out = refs[:-1], refs[-1]
+    part = pieces[0].shape[0]
     for k, piece in enumerate(pieces):
-        start = ((ids[chunk_at] + k) & (holders - 1)) * part
-        place = weight_out.at[pl.ds(pl.multiple_of(start, part), part)]
-        copies.append(pltpu.make_async_copy(piece, place, sems.at[k]))
-    for copy in copies:
-        copy.start()
-    for copy in copies:
-        copy.wait()
-
-
-def deliver(ids, chunk_at, grad, pieces):
-    holders = len(pieces)
+        start = ((ids[chunk_at] + k) & (len(pieces) - 1)) * part
+        out[pl.ds(pl.multiple_of(start, part), part), :] = piece[...]
+
+
+def place(ids, chunk_at, pieces):
     part, total = pieces[0].shape
     return pl.pallas_call(
-        functools.partial(deliver_kernel, holders, chunk_at),
-        out_shape=(
-            jax.ShapeDtypeStruct(grad.shape, BF),
-            jax.ShapeDtypeStruct((part * holders, total), F4),
-        ),
-        in_specs=[SMEM] + [ANY] * (1 + holders),
-        out_specs=(ANY, ANY),
-        scratch_shapes=[pltpu.SemaphoreType.DMA((holders + 1,))],
-        compiler_params=pltpu.CompilerParams(vmem_limit_bytes=VMEM_LIMIT),
-        name="deliver",
-    )(ids, grad, *pieces)
+        functools.partial(place_kernel, chunk_at),
+        out_shape=jax.ShapeDtypeStruct((part * len(pieces), total), F4),
+        in_specs=[SMEM] + [VMEM] * len(pieces),
+        out_specs=VMEM,
+        compiler_params=pltpu.CompilerParams(vmem_limit_bytes=VMEM_LIMIT),
+        name="place",
+    )(ids, *pieces)
 
 
 def around(x, axis, count):
@@ -326,17 +347,16 @@
     pair, lent = lax.optimization_barrier((pair, weight))
     parts = exchange(pair, "y")
     others = around(lent, "rep", reps)
-    aggs = exchange(fold(parts, reps, others), "rep")
-    activation, payload = dense(ids, aggs, [weight, *others], cotangent, ys, side)
+    copies, near, cot = fold(parts, weight, cotangent, reps, others)
+    aggs = exchange(copies, "rep")
+    activation, payload = dense(ids, aggs, near, others, cot, ys, side)
     mine = exchange(payload, "y")
     theirs = swap_cores(mine)
     back = backward_tiles(ids, values, mine, theirs, rows, col_blocks)
     sums = exchange(back, "row")
     grad, share = finish(sums, 1.0 / math.sqrt(nodes), grains, width // holders, total)
     input_grad = exchange(grad, "row")
-    input_grad, weight_grad = deliver(
-        ids, slots + 1, input_grad, [share, *around(share, "y", holders)]
-    )
+    weight_grad = place(ids, slots + 1, [share, *around(share, "y", holders)])
     return (activation, weight_grad, input_grad)
 
 

time: 138 us -> 135 us (0.978)
  transfers between devices with their start and end apart: 8 -> 8, of which waited for: 8 -> 8; matrix products, arithmetic and copies ran while one was open for 0% -> 0% of each run, Pallas kernels for 0% -> 1%
where the time goes in v4:
time: 135 us; the launch traced here: 134 us
  blocking collectives  72.3 us (54%)
  starting transfers between devices  26.4 us (20%)
  waiting for transfers between devices  21.3 us (16%)
  Pallas kernels  10.5 us (8%)
  other arithmetic  1.58 us (1%)
  between operations  1.39 us (1%)
    all_to_all x3, blocking collectives, exchange(): return lax.all_to_all(x, axis, 0, 0, tiled=True)  68.1 us
    all_to_all x2, starting transfers between devices, exchange(): return lax.all_to_all(x, axis, 0, 0, tiled=True)  10.9 us
    all_to_all x2, waiting for transfers between devices, exchange(): return lax.all_to_all(x, axis, 0, 0, tiled=True)  10.7 us
    ppermute x2, starting transfers between devices, around(): lax.ppermute(x, names, [((i + k) % n * step + c * core, i * step + c * co...  6.8 us
    ppermute x2, starting transfers between devices, around(): across = lax.ppermute(x, axis, [((i + 2) % n, i) for i in range(n)])  4.94 us
    ppermute x2, waiting for transfers between devices, around(): across = lax.ppermute(x, axis, [((i + 2) % n, i) for i in range(n)])  4.38 us
    all_gather x2, blocking collectives, around(): sides = lax.all_gather(sides, 'core', axis=0)  4.28 us
    ppermute x2, waiting for transfers between devices, swap_cores(): return lax.ppermute(x, 'core', [(0, 1), (1, 0)])  4.13 us
  transfers between devices with their start and end apart: 8, of which 8 were waited for; matrix products, arithmetic and copies ran while one was open for 0% of the time, Pallas kernels for 1%

profile of v4, /device:TPU:2, one launch (start us, length us, event | category | flops | bytes accessed | tf_op | source)
XLA Modules:
  0.0 134.3 jit_solution(10721723436818079472)
XLA Ops:
  1.3 0.7 compare_select_fusion
  2.0 3.1 %forward_tiles.1 = (f32[8,256,128]{2,1,0:T(8,128)S(1)}, bf16[8,256,128]{2,1,0:T(8,128)(2,1)S(1)}) custom-call(s32[99]{0:T(128)S(1)} %compare_select_fusion.3.ids_any.ids, bf16[96,128,128]{2,1,0:T(8,128)(2,1)} %bitcast.8, bf16[16,128,128]{2,1,0:T(8,128)(2,1)} %bitcast.11), custom_call_target="tpu_custom_call" | custom-call | tf_op jit(solution)/shard_map/forward_tiles/pallas_call | solution.py:85
  5.0 1.9 %collective-permute-start = (bf16[8,256,128]{2,1,0:T(8,128)(2,1)S(1)}, bf16[8,256,128]{2,1,0:T(8,128)(2,1)S(1)}, u32[]{:S(2)}, u32[]{:S(2)}) collective-permute-start(bf16[8,256,128]{2,1,0:T(8,128)(2,1)S(1)} %get-tuple-element.15), channel_id=1, source_target_pairs={{0,4},{4,0},{1,5},{5,1},{2,6},{6,2},{3,7},{7,3},{8,12},{12,8},{9,1... | collective-permute-start | bytes 1572872 | tf_op jit(solution)/shard_map/ppermute | solution.py:321
  7.0 1.9 %collective-permute-done = bf16[8,256,128]{2,1,0:T(8,128)(2,1)S(1)} collective-permute-done((bf16[8,256,128]{2,1,0:T(8,128)(2,1)S(1)}, bf16[8,256,128]{2,1,0:T(8,128)(2,1)S(1)}, u32[]{:S(2)}, u32[]{:S(2)}) %collective-permute-start) | collective-permute-done | bytes 524320 | tf_op jit(solution)/shard_map/ppermute | solution.py:321
  8.8 0.9 add_convert_fusion
  9.7 0.0 copy-start
  9.7 7.4 %all-to-all-start = ((bf16[8,256,128]{2,1,0:T(8,128)(2,1)}), bf16[8,256,128]{2,1,0:T(8,128)(2,1)}, u32[]{:S(2)}, u32[]{:S(2)}) async-start(bf16[8,256,128]{2,1,0:T(8,128)(2,1)} %add_convert_fusion), calls=%async_computation | async-start | bytes 1048576 | tf_op jit(solution)/shard_map/all_to_all | solution.py:325
  17.1 4.9 %collective-permute-start.1 = (bf16[128,512]{1,0:T(8,128)(2,1)}, bf16[128,512]{1,0:T(8,128)(2,1)S(1)}, u32[]{:S(2)}, u32[]{:S(2)}) collective-permute-start(bf16[128,512]{1,0:T(8,128)(2,1)} %weight_hbm.1), channel_id=1, source_target_pairs={{1,0},{2,1},{3,2},{0,3},{7,4},{4,5},{5,6},{6,7},{9,8},{10,9},{11,1... | collective-permute-start | bytes 393224 | tf_op jit(solution)/shard_map/ppermute | solution.py:306
  22.0 1.9 %collective-permute-start.2 = (bf16[128,512]{1,0:T(8,128)(2,1)}, bf16[128,512]{1,0:T(8,128)(2,1)S(1)}, u32[]{:S(2)}, u32[]{:S(2)}) collective-permute-start(bf16[128,512]{1,0:T(8,128)(2,1)} %weight_hbm.1), channel_id=1, source_target_pairs={{2,0},{3,1},{0,2},{1,3},{6,4},{7,5},{4,6},{5,7},{10,8},{11,9},{8,1... | collective-permute-start | bytes 393224 | tf_op jit(solution)/shard_map/ppermute | solution.py:315
  23.9 0.9 collective-permute-done.1
  24.8 2.4 %all-gather = bf16[256,512]{1,0:T(8,128)(2,1)S(1)} all-gather(bf16[128,512]{1,0:T(8,128)(2,1)S(1)} %collective-permute-done.1), channel_id=2, replica_groups=mesh['row'=8,'y'=8,'core'=2,'rep'=4] {'core'}, dimensions={0}, use_global_device_ids=true | all-gather | bytes 393216 | tf_op jit(solution)/shard_map/all_gather | solution.py:316
  27.2 3.4 %collective-permute-done.2.refs_1_ = bf16[128,512]{1,0:T(8,128)(2,1)S(1)} collective-permute-done((bf16[128,512]{1,0:T(8,128)(2,1)}, bf16[128,512]{1,0:T(8,128)(2,1)S(1)}, u32[]{:S(2)}, u32[]{:S(2)}) %collective-permute-start.2) | collective-permute-done | bytes 131104 | tf_op jit(solution)/shard_map/ppermute | solution.py:315
  30.6 4.4 %all-to-all-done.parts_hbm = bf16[8,256,128]{2,1,0:T(8,128)(2,1)} async-done(((bf16[8,256,128]{2,1,0:T(8,128)(2,1)}), bf16[8,256,128]{2,1,0:T(8,128)(2,1)}, u32[]{:S(2)}, u32[]{:S(2)}) %all-to-all-start) | async-done | bytes 524320 | tf_op jit(solution)/shard_map/all_to_all | solution.py:325
  35.0 1.4 %fold.1 = (bf16[4,256,128]{2,1,0:T(8,128)(2,1)S(1)}, bf16[128,512]{1,0:T(8,128)(2,1)S(1)}, bf16[256,512]{1,0:T(8,128)(2,1)S(1)}) custom-call(bf16[8,256,128]{2,1,0:T(8,128)(2,1)} %all-to-all-done.parts_hbm, bf16[128,512]{1,0:T(8,128)(2,1)} %weight_hbm.1, bf16[256,512]{1,0:T(8,128)(2,1)} %cot_hbm.1, bf16[128,512]{1,0:T(8,128)(2,1)S(1)} %get-tuple-element.26.refs_0_, ...), custom_call_target="tpu_custom_call" | custom-call | tf_op jit(solution)/shard_map/fold/pallas_call | solution.py:131
  36.4 11.3 %all_to_all.32.aggs = bf16[4,256,128]{2,1,0:T(8,128)(2,1)S(1)} all-to-all(bf16[4,256,128]{2,1,0:T(8,128)(2,1)S(1)} %get-tuple-element.18), channel_id=1, replica_groups=mesh['row'=8,'y'=8,'core'=2,'rep'=4] {'rep'}, dimensions={0} | all-to-all | bytes 524288 | tf_op jit(solution)/shard_map/all_to_all | solution.py:325
  47.6 1.8 %dense.1 = (bf16[256,512]{1,0:T(8,128)(2,1)}, bf16[8,384,128]{2,1,0:T(8,128)(2,1)S(1)}) custom-call(s32[99]{0:T(128)S(1)} %compare_select_fusion.3.ids_any.ids, bf16[4,256,128]{2,1,0:T(8,128)(2,1)S(1)} %all_to_all.32.aggs, bf16[128,512]{1,0:T(8,128)(2,1)S(1)} %get-tuple-element.19.own_weight, bf16[128,512]{1,0:T(8,128)(2,1)S(1)} %get-tuple-element.26.refs_0_, ...), custom_call_target="tpu_custom_call" | custom-call | tf_op jit(solution)/shard_map/dense/pallas_call | solution.py:185
  49.5 25.2 %all_to_all.33.mine = bf16[8,384,128]{2,1,0:T(8,128)(2,1)S(1)} all-to-all(bf16[8,384,128]{2,1,0:T(8,128)(2,1)S(1)} %get-tuple-element.22), channel_id=1, replica_groups=mesh['row'=8,'y'=8,'core'=2,'rep'=4] {'y'}, dimensions={0} | all-to-all | bytes 1572864 | tf_op jit(solution)/shard_map/all_to_all | solution.py:325
  74.6 1.9 %collective-permute-start.3 = (bf16[8,384,128]{2,1,0:T(8,128)(2,1)S(1)}, bf16[8,384,128]{2,1,0:T(8,128)(2,1)S(1)}, u32[]{:S(2)}, u32[]{:S(2)}) collective-permute-start(bf16[8,384,128]{2,1,0:T(8,128)(2,1)S(1)} %all_to_all.33.mine), channel_id=1, source_target_pairs={{0,4},{4,0},{1,5},{5,1},{2,6},{6,2},{3,7},{7,3},{8,12},{12,8},{9,1... | collective-permute-start | bytes 2359304 | tf_op jit(solution)/shard_map/ppermute | solution.py:321
  76.5 2.3 %collective-permute-done.3.theirs = bf16[8,384,128]{2,1,0:T(8,128)(2,1)S(1)} collective-permute-done((bf16[8,384,128]{2,1,0:T(8,128)(2,1)S(1)}, bf16[8,384,128]{2,1,0:T(8,128)(2,1)S(1)}, u32[]{:S(2)}, u32[]{:S(2)}) %collective-permute-start.3) | collective-permute-done | bytes 786464 | tf_op jit(solution)/shard_map/ppermute | solution.py:321
  78.8 0.0 copy-done
  78.8 2.0 %backward_tiles.1 = bf16[8,384,128]{2,1,0:T(8,128)(2,1)S(1)} custom-call(s32[99]{0:T(128)S(1)} %compare_select_fusion.3.ids_any.ids, bf16[96,128,128]{2,1,0:T(8,128)(2,1)S(1)} %bitcast.9, bf16[8,384,128]{2,1,0:T(8,128)(2,1)S(1)} %all_to_all.33.mine, bf16[8,384,128]{2,1,0:T(8,128)(2,1)S(1)} %collective-permute-done.3.theirs), custom_call_target="tpu_custom_call" | custom-call | tf_op jit(solution)/shard_map/backward_tiles/pallas_call | solution.py:235
  80.8 31.7 %all_to_all.34.parts = bf16[8,384,128]{2,1,0:T(8,128)(2,1)S(1)} all-to-all(bf16[8,384,128]{2,1,0:T(8,128)(2,1)S(1)} %backward_tiles.1), channel_id=1, replica_groups=mesh['row'=8,'y'=8,'core'=2,'rep'=4] {'row'}, dimensions={0} | all-to-all | bytes 1572864 | tf_op jit(solution)/shard_map/all_to_all | solution.py:325
  112.5 1.0 finish.1
  113.4 3.5 %all-to-all-start.4 = ((bf16[8,256,128]{2,1,0:T(8,128)(2,1)}), bf16[8,256,128]{2,1,0:T(8,128)(2,1)S(1)}, u32[]{:S(2)}, u32[]{:S(2)}) async-start(bf16[8,256,128]{2,1,0:T(8,128)(2,1)} %bitcast.4), calls=%async_computation.4 | async-start | bytes 1048576 | tf_op jit(solution)/shard_map/all_to_all | solution.py:325
  116.9 1.9 %collective-permute-start.4 = (f32[32,512]{1,0:T(8,128)S(1)}, f32[32,512]{1,0:T(8,128)S(1)}, u32[]{:S(2)}, u32[]{:S(2)}) collective-permute-start(f32[32,512]{1,0:T(8,128)S(1)} %get-tuple-element.23.refs_0_), channel_id=1, source_target_pairs={{8,0},{16,8},{24,16},{32,24},{40,32},{48,40},{56,48},{0,56},{60,4}... | collective-permute-start | bytes 196616 | tf_op jit(solution)/shard_map/ppermute | solution.py:306
  118.9 3.0 %collective-permute-start.5 = (f32[32,512]{1,0:T(8,128)S(1)}, f32[32,512]{1,0:T(8,128)S(1)}, u32[]{:S(2)}, u32[]{:S(2)}) collective-permute-start(f32[32,512]{1,0:T(8,128)S(1)} %get-tuple-element.23.refs_0_), channel_id=1, source_target_pairs={{16,0},{24,8},{32,16},{40,24},{48,32},{56,40},{0,48},{8,56},{17,1}... | collective-permute-start | bytes 196616 | tf_op jit(solution)/shard_map/ppermute | solution.py:315
  121.9 1.2 collective-permute-done.4
  123.1 1.9 %all-gather.1 = f32[64,512]{1,0:T(8,128)S(1)} all-gather(f32[32,512]{1,0:T(8,128)S(1)} %collective-permute-done.4), channel_id=3, replica_groups=mesh['row'=8,'y'=8,'core'=2,'rep'=4] {'core'}, dimensions={0}, use_global_device_ids=true | all-gather | bytes 196608 | tf_op jit(solution)/shard_map/all_gather | solution.py:316
  125.0 1.0 collective-permute-done.5.refs_2_
  126.0 1.3 place.1
  127.3 6.2 %all-to-all-done.4 = bf16[8,256,128]{2,1,0:T(8,128)(2,1)S(1)} async-done(((bf16[8,256,128]{2,1,0:T(8,128)(2,1)}), bf16[8,256,128]{2,1,0:T(8,128)(2,1)S(1)}, u32[]{:S(2)}, u32[]{:S(2)}) %all-to-all-start.4) | async-done | bytes 524320 | tf_op jit(solution)/shard_map/all_to_all | solution.py:325
  133.5 0.8 copy.12
  (3 shorter events, 0.0 us)
Async XLA Ops:
  5.0 3.8 %collective-permute-start = (bf16[8,256,128]{2,1,0:T(8,128)(2,1)S(1)}, bf16[8,256,128]{2,1,0:T(8,128)(2,1)S(1)}, u32[]{:S(2)}, u32[]{:S(2)}) collective-permute-start(bf16[8,256,128]{2,1,0:T(8,128)(2,1)S(1)} %get-tuple-element.15), channel_id=1, source_target_pairs={{0,4},{4,0},{1,5},{5,1},{2,6},{6,2},{3,7},{7,3},{8,12},{12,8},{9,1... | collective-permute-start | bytes 1572872 | tf_op jit(solution)/shard_map/ppermute | solution.py:321
  9.7 69.1 %copy-start = (bf16[1,1,96,128,128]{4,3,2,1,0:T(8,128)(2,1)S(1)}, bf16[1,1,96,128,128]{4,3,2,1,0:T(8,128)(2,1)}, u32[]{:S(2)}) copy-start(bf16[1,1,96,128,128]{4,3,2,1,0:T(8,128)(2,1)} %param.7) | copy-start | bytes 9437188
  9.7 25.3 %all-to-all-start = ((bf16[8,256,128]{2,1,0:T(8,128)(2,1)}), bf16[8,256,128]{2,1,0:T(8,128)(2,1)}, u32[]{:S(2)}, u32[]{:S(2)}) async-start(bf16[8,256,128]{2,1,0:T(8,128)(2,1)} %add_convert_fusion), calls=%async_computation | async-start | bytes 1048576 | tf_op jit(solution)/shard_map/all_to_all | solution.py:325
  17.1 7.7 %collective-permute-start.1 = (bf16[128,512]{1,0:T(8,128)(2,1)}, bf16[128,512]{1,0:T(8,128)(2,1)S(1)}, u32[]{:S(2)}, u32[]{:S(2)}) collective-permute-start(bf16[128,512]{1,0:T(8,128)(2,1)} %weight_hbm.1), channel_id=1, source_target_pairs={{1,0},{2,1},{3,2},{0,3},{7,4},{4,5},{5,6},{6,7},{9,8},{10,9},{11,1... | collective-permute-start | bytes 393224 | tf_op jit(solution)/shard_map/ppermute | solution.py:306
  22.0 8.6 %collective-permute-start.2 = (bf16[128,512]{1,0:T(8,128)(2,1)}, bf16[128,512]{1,0:T(8,128)(2,1)S(1)}, u32[]{:S(2)}, u32[]{:S(2)}) collective-permute-start(bf16[128,512]{1,0:T(8,128)(2,1)} %weight_hbm.1), channel_id=1, source_target_pairs={{2,0},{3,1},{0,2},{1,3},{6,4},{7,5},{4,6},{5,7},{10,8},{11,9},{8,1... | collective-permute-start | bytes 393224 | tf_op jit(solution)/shard_map/ppermute | solution.py:315
  74.6 4.2 %collective-permute-start.3 = (bf16[8,384,128]{2,1,0:T(8,128)(2,1)S(1)}, bf16[8,384,128]{2,1,0:T(8,128)(2,1)S(1)}, u32[]{:S(2)}, u32[]{:S(2)}) collective-permute-start(bf16[8,384,128]{2,1,0:T(8,128)(2,1)S(1)} %all_to_all.33.mine), channel_id=1, source_target_pairs={{0,4},{4,0},{1,5},{5,1},{2,6},{6,2},{3,7},{7,3},{8,12},{12,8},{9,1... | collective-permute-start | bytes 2359304 | tf_op jit(solution)/shard_map/ppermute | solution.py:321
  113.4 20.1 %all-to-all-start.4 = ((bf16[8,256,128]{2,1,0:T(8,128)(2,1)}), bf16[8,256,128]{2,1,0:T(8,128)(2,1)S(1)}, u32[]{:S(2)}, u32[]{:S(2)}) async-start(bf16[8,256,128]{2,1,0:T(8,128)(2,1)} %bitcast.4), calls=%async_computation.4 | async-start | bytes 1048576 | tf_op jit(solution)/shard_map/all_to_all | solution.py:325
  116.9 6.2 %collective-permute-start.4 = (f32[32,512]{1,0:T(8,128)S(1)}, f32[32,512]{1,0:T(8,128)S(1)}, u32[]{:S(2)}, u32[]{:S(2)}) collective-permute-start(f32[32,512]{1,0:T(8,128)S(1)} %get-tuple-element.23.refs_0_), channel_id=1, source_target_pairs={{8,0},{16,8},{24,16},{32,24},{40,32},{48,40},{56,48},{0,56},{60,4}... | collective-permute-start | bytes 196616 | tf_op jit(solution)/shard_map/ppermute | solution.py:306
  118.9 7.2 %collective-permute-start.5 = (f32[32,512]{1,0:T(8,128)S(1)}, f32[32,512]{1,0:T(8,128)S(1)}, u32[]{:S(2)}, u32[]{:S(2)}) collective-permute-start(f32[32,512]{1,0:T(8,128)S(1)} %get-tuple-element.23.refs_0_), channel_id=1, source_target_pairs={{16,0},{24,8},{32,16},{40,24},{48,32},{56,40},{0,48},{8,56},{17,1}... | collective-permute-start | bytes 196616 | tf_op jit(solution)/shard_map/ppermute | solution.py:315

commit v5 on v4

--- a/solution.py
+++ b/solution.py
@@ -170,11 +170,12 @@
     for y in range(ys):
         for b in range(grains // side):
             payload[y, pl.ds(b * width, width), :] = back[:, b * side : (b + 1) * side]
-        chunk = y % holders
         for k in range(share.shape[1] // side):
-            payload[y, pl.ds(base + k * part, part), :] = share[
-                chunk * part : (chunk + 1) * part, k * side : (k + 1) * side
-            ]
+            for c in range(2):
+                rows = c * (width // 2) + y % holders * (part // 2)
+                payload[y, pl.ds(base + k * part + c * (part // 2), part // 2), :] = share[
+                    rows : rows + part // 2, k * side : (k + 1) * side
+                ]
     take_act.wait()
 
 
@@ -196,7 +197,7 @@
     )(ids, aggs, weight, *others, cot)
 
 
-def backward_kernel(ids, tiles, mine, theirs, payload, acc):
+def backward_kernel(parts, ids, tiles, mine, theirs, payload, acc):
     acc[...] = jnp.zeros_like(acc)
     side = tiles.shape[1]
     width = acc.shape[1]
@@ -218,22 +219,28 @@
         local = ((word >> core_shift) & 1) == me
         grad = jnp.where(local, mine[y, block], theirs[y, block])
         acc[word & (2 * col_blocks - 1)] += dot(grad, tiles[t])
-    share = jnp.zeros((payload.shape[1] - base, side), F4)
-    for grads in (mine, theirs):
-        for y in range(ys):
-            share += grads[y, base:, :].astype(F4)
-    share = share.astype(BF)
+    part = (payload.shape[1] - base) // parts
+    shares = []
+    for k in range(parts):
+        half = pl.ds(pl.multiple_of(base + 2 * k * part + me * part, part), part)
+        share = jnp.zeros((part, side), F4)
+        for grads in (mine, theirs):
+            for y in range(ys):
+                share += grads[y, half, :].astype(F4)
+        shares.append(share.astype(BF))
     for r in range(rows):
         for b in range(per_row):
             payload[r, pl.ds(b * width, width), :] = acc[r * per_row + b].astype(BF)
-        payload[r, base:, :] = share
-
-
-def backward_tiles(ids, values, mine, theirs, rows, col_blocks):
+        for k, share in enumerate(shares):
+            payload[r, pl.ds(base + k * part, part), :] = share
+
+
+def backward_tiles(ids, values, mine, theirs, rows, col_blocks, parts):
     side = values.shape[1]
-    length = mine.shape[1]
-    return pl.pallas_call(
-        backward_kernel,
+    base = col_blocks // rows * side
+    length = base + (mine.shape[1] - base) // 2
+    return pl.pallas_call(
+        functools.partial(backward_kernel, parts),
         out_shape=jax.ShapeDtypeStruct((rows, length, side), BF),
         in_specs=[SMEM] + [VMEM] * 3,
         out_specs=VMEM,
@@ -275,24 +282,30 @@
     )(parts)
 
 
-def place_kernel(chunk_at, ids, *refs):
+def place_kernel(chunk_at, steps, ids, *refs):
     pieces, out = refs[:-1], refs[-1]
     part = pieces[0].shape[0]
-    for k, piece in enumerate(pieces):
-        start = ((ids[chunk_at] + k) & (len(pieces) - 1)) * part
+    for step, piece in zip(steps, pieces):
+        start = ((ids[chunk_at] + step) & (len(steps) - 1)) * part
         out[pl.ds(pl.multiple_of(start, part), part), :] = piece[...]
 
 
-def place(ids, chunk_at, pieces):
-    part, total = pieces[0].shape
-    return pl.pallas_call(
-        functools.partial(place_kernel, chunk_at),
-        out_shape=jax.ShapeDtypeStruct((part * len(pieces), total), F4),
-        in_specs=[SMEM] + [VMEM] * len(pieces),
+def gather_chunks(ids, chunk_at, piece, holders):
+    steps = [0, 1, -1, 2][:holders]
+    n = lax.axis_size("y")
+    pieces = [piece] + [
+        lax.ppermute(piece, "y", [((i + k) % n, i) for i in range(n)]) for k in steps[1:]
+    ]
+    part, total = piece.shape
+    half = pl.pallas_call(
+        functools.partial(place_kernel, chunk_at, steps),
+        out_shape=jax.ShapeDtypeStruct((part * holders, total), F4),
+        in_specs=[SMEM] + [VMEM] * holders,
         out_specs=VMEM,
         compiler_params=pltpu.CompilerParams(vmem_limit_bytes=VMEM_LIMIT),
         name="place",
     )(ids, *pieces)
+    return lax.all_gather(half, "core", axis=0, tiled=True)
 
 
 def around(x, axis, count):
@@ -352,11 +365,11 @@
     activation, payload = dense(ids, aggs, near, others, cot, ys, side)
     mine = exchange(payload, "y")
     theirs = swap_cores(mine)
-    back = backward_tiles(ids, values, mine, theirs, rows, col_blocks)
+    back = backward_tiles(ids, values, mine, theirs, rows, col_blocks, total // side)
     sums = exchange(back, "row")
-    grad, share = finish(sums, 1.0 / math.sqrt(nodes), grains, width // holders, total)
+    grad, share = finish(sums, 1.0 / math.sqrt(nodes), grains, width // holders // 2, total)
     input_grad = exchange(grad, "row")
-    weight_grad = place(ids, slots + 1, [share, *around(share, "y", holders)])
+    weight_grad = gather_chunks(ids, slots + 1, share, holders)
     return (activation, weight_grad, input_grad)
 
 

time: 135 us -> 133 us (0.985)
  starting transfers between devices: 26.4 us -> 30.8 us
  waiting for transfers between devices: 21.3 us -> 17.5 us
  blocking collectives: 72.3 us -> 69.7 us
    ppermute x0 -> x3, starting transfers between devices: none -> 9.33 us  [gather_chunks(): lax.ppermute(piece, 'y', [((i + k) % n, i) for i in range(n)])]
    all_to_all x2, waiting for transfers between devices: 10.7 us -> 7.37 us  [exchange(): return lax.all_to_all(x, axis, 0, 0, tiled=True)]
    ppermute x2 -> x1, starting transfers between devices: 4.94 us -> 1.92 us  [around(): across = lax.ppermute(x, axis, [((i + 2) % n, i) for i in range(n)])]
    all_to_all x3, blocking collectives: 68.1 us -> 65.3 us  [exchange(): return lax.all_to_all(x, axis, 0, 0, tiled=True)]
    all_gather x0 -> x1, blocking collectives: none -> 1.99 us  [gather_chunks(): return lax.all_gather(half, 'core', axis=0, tiled=True)]
    ppermute x2 -> x1, starting transfers between devices: 6.8 us -> 4.88 us  [around(): lax.ppermute(x, names, [((i + k) % n * step + c * core, i * step + c * co...]
    all_gather x2 -> x1, blocking collectives: 4.28 us -> 2.39 us  [around(): sides = lax.all_gather(sides, 'core', axis=0)]
    ppermute x0 -> x3, waiting for transfers between devices: none -> 1.75 us  [gather_chunks(): lax.ppermute(piece, 'y', [((i + k) % n, i) for i in range(n)])]
  transfers between devices with their start and end apart: 8 -> 9, of which waited for: 8 -> 7; matrix products, arithmetic and copies ran while one was open for 0% -> 0% of each run, Pallas kernels for 1% -> 0%
where the time goes in v5:
time: 133 us; the launch traced here: 132 us
  blocking collectives  69.7 us (52%)
  starting transfers between devices  30.8 us (23%)
  waiting for transfers between devices  17.5 us (13%)
  Pallas kernels  9.75 us (7%)
  other arithmetic  1.58 us (1%)
  local copies, waits for them, and re-layouts  1.52 us (1%)
  between operations  1.41 us (1%)
    all_to_all x3, blocking collectives, exchange(): return lax.all_to_all(x, axis, 0, 0, tiled=True)  65.3 us
    all_to_all x2, starting transfers between devices, exchange(): return lax.all_to_all(x, axis, 0, 0, tiled=True)  10.8 us
    ppermute x3, starting transfers between devices, gather_chunks(): lax.ppermute(piece, 'y', [((i + k) % n, i) for i in range(n)])  9.33 us
    all_to_all x2, waiting for transfers between devices, exchange(): return lax.all_to_all(x, axis, 0, 0, tiled=True)  7.37 us
    ppermute x1, starting transfers between devices, around(): lax.ppermute(x, names, [((i + k) % n * step + c * core, i * step + c * co...  4.88 us
    ppermute x2, waiting for transfers between devices, swap_cores(): return lax.ppermute(x, 'core', [(0, 1), (1, 0)])  4.13 us
    ppermute x2, starting transfers between devices, swap_cores(): return lax.ppermute(x, 'core', [(0, 1), (1, 0)])  3.83 us
    ppermute x1, waiting for transfers between devices, around(): across = lax.ppermute(x, axis, [((i + 2) % n, i) for i in range(n)])  3.35 us
  transfers between devices with their start and end apart: 9, of which 7 were waited for; matrix products, arithmetic and copies ran while one was open for 0% of the time, Pallas kernels for 0%

profile of v5, /device:TPU:2, one launch (start us, length us, event | category | flops | bytes accessed | tf_op | source)
XLA Modules:
  0.0 132.2 jit_solution(12182163964922116057)
XLA Ops:
  1.3 0.7 compare_select_fusion
  2.0 3.1 %forward_tiles.1 = (f32[8,256,128]{2,1,0:T(8,128)S(1)}, bf16[8,256,128]{2,1,0:T(8,128)(2,1)S(1)}) custom-call(s32[99]{0:T(128)S(1)} %compare_select_fusion.3.ids_any.ids, bf16[96,128,128]{2,1,0:T(8,128)(2,1)} %bitcast.8, bf16[16,128,128]{2,1,0:T(8,128)(2,1)} %bitcast.11), custom_call_target="tpu_custom_call" | custom-call | tf_op jit(solution)/shard_map/forward_tiles/pallas_call | solution.py:85
  5.0 1.9 %collective-permute-start = (bf16[8,256,128]{2,1,0:T(8,128)(2,1)S(1)}, bf16[8,256,128]{2,1,0:T(8,128)(2,1)S(1)}, u32[]{:S(2)}, u32[]{:S(2)}) collective-permute-start(bf16[8,256,128]{2,1,0:T(8,128)(2,1)S(1)} %get-tuple-element.15), channel_id=1, source_target_pairs={{0,4},{4,0},{1,5},{5,1},{2,6},{6,2},{3,7},{7,3},{8,12},{12,8},{9,1... | collective-permute-start | bytes 1572872 | tf_op jit(solution)/shard_map/ppermute | solution.py:334
  7.0 1.9 %collective-permute-done = bf16[8,256,128]{2,1,0:T(8,128)(2,1)S(1)} collective-permute-done((bf16[8,256,128]{2,1,0:T(8,128)(2,1)S(1)}, bf16[8,256,128]{2,1,0:T(8,128)(2,1)S(1)}, u32[]{:S(2)}, u32[]{:S(2)}) %collective-permute-start) | collective-permute-done | bytes 524320 | tf_op jit(solution)/shard_map/ppermute | solution.py:334
  8.8 0.9 add_convert_fusion
  9.7 0.0 copy-start
  9.7 7.4 %all-to-all-start = ((bf16[8,256,128]{2,1,0:T(8,128)(2,1)}), bf16[8,256,128]{2,1,0:T(8,128)(2,1)}, u32[]{:S(2)}, u32[]{:S(2)}) async-start(bf16[8,256,128]{2,1,0:T(8,128)(2,1)} %add_convert_fusion), calls=%async_computation | async-start | bytes 1048576 | tf_op jit(solution)/shard_map/all_to_all | solution.py:338
  17.1 4.9 %collective-permute-start.1 = (bf16[128,512]{1,0:T(8,128)(2,1)}, bf16[128,512]{1,0:T(8,128)(2,1)S(1)}, u32[]{:S(2)}, u32[]{:S(2)}) collective-permute-start(bf16[128,512]{1,0:T(8,128)(2,1)} %weight_hbm.1), channel_id=1, source_target_pairs={{1,0},{2,1},{3,2},{0,3},{7,4},{4,5},{5,6},{6,7},{9,8},{10,9},{11,1... | collective-permute-start | bytes 393224 | tf_op jit(solution)/shard_map/ppermute | solution.py:319
  22.0 1.9 %collective-permute-start.2 = (bf16[128,512]{1,0:T(8,128)(2,1)}, bf16[128,512]{1,0:T(8,128)(2,1)S(1)}, u32[]{:S(2)}, u32[]{:S(2)}) collective-permute-start(bf16[128,512]{1,0:T(8,128)(2,1)} %weight_hbm.1), channel_id=1, source_target_pairs={{2,0},{3,1},{0,2},{1,3},{6,4},{7,5},{4,6},{5,7},{10,8},{11,9},{8,1... | collective-permute-start | bytes 393224 | tf_op jit(solution)/shard_map/ppermute | solution.py:328
  23.9 0.9 collective-permute-done.1
  24.8 2.4 %all-gather = bf16[256,512]{1,0:T(8,128)(2,1)S(1)} all-gather(bf16[128,512]{1,0:T(8,128)(2,1)S(1)} %collective-permute-done.1), channel_id=2, replica_groups=mesh['row'=8,'y'=8,'core'=2,'rep'=4] {'core'}, dimensions={0}, use_global_device_ids=true | all-gather | bytes 393216 | tf_op jit(solution)/shard_map/all_gather | solution.py:329
  27.2 3.4 %collective-permute-done.2.refs_1_ = bf16[128,512]{1,0:T(8,128)(2,1)S(1)} collective-permute-done((bf16[128,512]{1,0:T(8,128)(2,1)}, bf16[128,512]{1,0:T(8,128)(2,1)S(1)}, u32[]{:S(2)}, u32[]{:S(2)}) %collective-permute-start.2) | collective-permute-done | bytes 131104 | tf_op jit(solution)/shard_map/ppermute | solution.py:328
  30.6 4.4 %all-to-all-done.parts_hbm = bf16[8,256,128]{2,1,0:T(8,128)(2,1)} async-done(((bf16[8,256,128]{2,1,0:T(8,128)(2,1)}), bf16[8,256,128]{2,1,0:T(8,128)(2,1)}, u32[]{:S(2)}, u32[]{:S(2)}) %all-to-all-start) | async-done | bytes 524320 | tf_op jit(solution)/shard_map/all_to_all | solution.py:338
  35.0 1.4 %fold.1 = (bf16[4,256,128]{2,1,0:T(8,128)(2,1)S(1)}, bf16[128,512]{1,0:T(8,128)(2,1)S(1)}, bf16[256,512]{1,0:T(8,128)(2,1)S(1)}) custom-call(bf16[8,256,128]{2,1,0:T(8,128)(2,1)} %all-to-all-done.parts_hbm, bf16[128,512]{1,0:T(8,128)(2,1)} %weight_hbm.1, bf16[256,512]{1,0:T(8,128)(2,1)} %cot_hbm.1, bf16[128,512]{1,0:T(8,128)(2,1)S(1)} %get-tuple-element.26.refs_0_, ...), custom_call_target="tpu_custom_call" | custom-call | tf_op jit(solution)/shard_map/fold/pallas_call | solution.py:131
  36.4 11.3 %all_to_all.32.aggs = bf16[4,256,128]{2,1,0:T(8,128)(2,1)S(1)} all-to-all(bf16[4,256,128]{2,1,0:T(8,128)(2,1)S(1)} %get-tuple-element.18), channel_id=1, replica_groups=mesh['row'=8,'y'=8,'core'=2,'rep'=4] {'rep'}, dimensions={0} | all-to-all | bytes 524288 | tf_op jit(solution)/shard_map/all_to_all | solution.py:338
  47.6 1.8 %dense.1 = (bf16[256,512]{1,0:T(8,128)(2,1)}, bf16[8,384,128]{2,1,0:T(8,128)(2,1)S(1)}) custom-call(s32[99]{0:T(128)S(1)} %compare_select_fusion.3.ids_any.ids, bf16[4,256,128]{2,1,0:T(8,128)(2,1)S(1)} %all_to_all.32.aggs, bf16[128,512]{1,0:T(8,128)(2,1)S(1)} %get-tuple-element.19.own_weight, bf16[128,512]{1,0:T(8,128)(2,1)S(1)} %get-tuple-element.26.refs_0_, ...), custom_call_target="tpu_custom_call" | custom-call | tf_op jit(solution)/shard_map/dense/pallas_call | solution.py:186
  49.5 25.2 %all_to_all.33.mine = bf16[8,384,128]{2,1,0:T(8,128)(2,1)S(1)} all-to-all(bf16[8,384,128]{2,1,0:T(8,128)(2,1)S(1)} %get-tuple-element.22), channel_id=1, replica_groups=mesh['row'=8,'y'=8,'core'=2,'rep'=4] {'y'}, dimensions={0} | all-to-all | bytes 1572864 | tf_op jit(solution)/shard_map/all_to_all | solution.py:338
  74.6 1.9 %collective-permute-start.3 = (bf16[8,384,128]{2,1,0:T(8,128)(2,1)S(1)}, bf16[8,384,128]{2,1,0:T(8,128)(2,1)S(1)}, u32[]{:S(2)}, u32[]{:S(2)}) collective-permute-start(bf16[8,384,128]{2,1,0:T(8,128)(2,1)S(1)} %all_to_all.33.mine), channel_id=1, source_target_pairs={{0,4},{4,0},{1,5},{5,1},{2,6},{6,2},{3,7},{7,3},{8,12},{12,8},{9,1... | collective-permute-start | bytes 2359304 | tf_op jit(solution)/shard_map/ppermute | solution.py:334
  76.5 2.3 %collective-permute-done.3.theirs = bf16[8,384,128]{2,1,0:T(8,128)(2,1)S(1)} collective-permute-done((bf16[8,384,128]{2,1,0:T(8,128)(2,1)S(1)}, bf16[8,384,128]{2,1,0:T(8,128)(2,1)S(1)}, u32[]{:S(2)}, u32[]{:S(2)}) %collective-permute-start.3) | collective-permute-done | bytes 786464 | tf_op jit(solution)/shard_map/ppermute | solution.py:334
  78.8 0.0 copy-done
  78.8 2.0 %backward_tiles.1 = bf16[8,320,128]{2,1,0:T(8,128)(2,1)S(1)} custom-call(s32[99]{0:T(128)S(1)} %compare_select_fusion.3.ids_any.ids, bf16[96,128,128]{2,1,0:T(8,128)(2,1)S(1)} %bitcast.9, bf16[8,384,128]{2,1,0:T(8,128)(2,1)S(1)} %all_to_all.33.mine, bf16[8,384,128]{2,1,0:T(8,128)(2,1)S(1)} %collective-permute-done.3.theirs), custom_call_target="tpu_custom_call" | custom-call | tf_op jit(solution)/shard_map/backward_tiles/pallas_call | solution.py:242
  80.8 28.9 %all_to_all.34.parts = bf16[8,320,128]{2,1,0:T(8,128)(2,1)S(1)} all-to-all(bf16[8,320,128]{2,1,0:T(8,128)(2,1)S(1)} %backward_tiles.1), channel_id=1, replica_groups=mesh['row'=8,'y'=8,'core'=2,'rep'=4] {'row'}, dimensions={0} | all-to-all | bytes 1310720 | tf_op jit(solution)/shard_map/all_to_all | solution.py:338
  109.6 1.0 finish.1
  110.6 3.5 %all-to-all-start.4 = ((bf16[8,256,128]{2,1,0:T(8,128)(2,1)}), bf16[8,256,128]{2,1,0:T(8,128)(2,1)S(1)}, u32[]{:S(2)}, u32[]{:S(2)}) async-start(bf16[8,256,128]{2,1,0:T(8,128)(2,1)} %bitcast.4), calls=%async_computation.4 | async-start | bytes 1048576 | tf_op jit(solution)/shard_map/all_to_all | solution.py:338
  114.1 2.3 %collective-permute-start.6 = (f32[16,512]{1,0:T(8,128)S(1)}, f32[16,512]{1,0:T(8,128)S(1)}, u32[]{:S(2)}, u32[]{:S(2)}) collective-permute-start(f32[16,512]{1,0:T(8,128)S(1)} %get-tuple-element.23.refs_0_), channel_id=1, source_target_pairs={{16,0},{24,8},{32,16},{40,24},{48,32},{56,40},{0,48},{8,56},{17,1}... | collective-permute-start | bytes 98312 | tf_op jit(solution)/shard_map/ppermute | solution.py:297
  116.4 2.1 %collective-permute-start.5 = (f32[16,512]{1,0:T(8,128)S(1)}, f32[16,512]{1,0:T(8,128)S(1)}, u32[]{:S(2)}, u32[]{:S(2)}) collective-permute-start(f32[16,512]{1,0:T(8,128)S(1)} %get-tuple-element.23.refs_0_), channel_id=1, source_target_pairs={{56,0},{0,8},{8,16},{16,24},{24,32},{32,40},{40,48},{48,56},{57,1}... | collective-permute-start | bytes 98312 | tf_op jit(solution)/shard_map/ppermute | solution.py:297
  118.5 4.9 %collective-permute-start.4 = (f32[16,512]{1,0:T(8,128)S(1)}, f32[16,512]{1,0:T(8,128)S(1)}, u32[]{:S(2)}, u32[]{:S(2)}) collective-permute-start(f32[16,512]{1,0:T(8,128)S(1)} %get-tuple-element.23.refs_0_), channel_id=1, source_target_pairs={{8,0},{16,8},{24,16},{32,24},{40,32},{48,40},{56,48},{0,56},{9,1},... | collective-permute-start | bytes 98312 | tf_op jit(solution)/shard_map/ppermute | solution.py:297
  123.5 0.0 collective-permute-done.6.refs_3_
  123.5 0.0 collective-permute-done.5.refs_2_
  123.5 1.7 %collective-permute-done.4.refs_1_ = f32[16,512]{1,0:T(8,128)S(1)} collective-permute-done((f32[16,512]{1,0:T(8,128)S(1)}, f32[16,512]{1,0:T(8,128)S(1)}, u32[]{:S(2)}, u32[]{:S(2)}) %collective-permute-start.4) | collective-permute-done | bytes 32800 | tf_op jit(solution)/shard_map/ppermute | solution.py:297
  125.2 0.6 place.1
  125.8 2.0 %all_gather.11 = f32[128,512]{1,0:T(8,128)S(1)} all-gather(f32[64,512]{1,0:T(8,128)S(1)} %place.1), channel_id=1, replica_groups=mesh['row'=8,'y'=8,'core'=2,'rep'=4] {'core'}, dimensions={0}, use_global_device_ids=true | all-gather | bytes 393216 | tf_op jit(solution)/shard_map/all_gather | solution.py:308
  127.8 2.9 %all-to-all-done.4 = bf16[8,256,128]{2,1,0:T(8,128)(2,1)S(1)} async-done(((bf16[8,256,128]{2,1,0:T(8,128)(2,1)}), bf16[8,256,128]{2,1,0:T(8,128)(2,1)S(1)}, u32[]{:S(2)}, u32[]{:S(2)}) %all-to-all-start.4) | async-done | bytes 524320 | tf_op jit(solution)/shard_map/all_to_all | solution.py:338
  130.7 0.7 copy.13
  131.4 0.8 copy.14
  (2 shorter events, 0.0 us)
Async XLA Ops:
  5.0 3.8 %collective-permute-start = (bf16[8,256,128]{2,1,0:T(8,128)(2,1)S(1)}, bf16[8,256,128]{2,1,0:T(8,128)(2,1)S(1)}, u32[]{:S(2)}, u32[]{:S(2)}) collective-permute-start(bf16[8,256,128]{2,1,0:T(8,128)(2,1)S(1)} %get-tuple-element.15), channel_id=1, source_target_pairs={{0,4},{4,0},{1,5},{5,1},{2,6},{6,2},{3,7},{7,3},{8,12},{12,8},{9,1... | collective-permute-start | bytes 1572872 | tf_op jit(solution)/shard_map/ppermute | solution.py:334
  9.7 69.1 %copy-start = (bf16[1,1,96,128,128]{4,3,2,1,0:T(8,128)(2,1)S(1)}, bf16[1,1,96,128,128]{4,3,2,1,0:T(8,128)(2,1)}, u32[]{:S(2)}) copy-start(bf16[1,1,96,128,128]{4,3,2,1,0:T(8,128)(2,1)} %param.7) | copy-start | bytes 9437188
  9.7 25.3 %all-to-all-start = ((bf16[8,256,128]{2,1,0:T(8,128)(2,1)}), bf16[8,256,128]{2,1,0:T(8,128)(2,1)}, u32[]{:S(2)}, u32[]{:S(2)}) async-start(bf16[8,256,128]{2,1,0:T(8,128)(2,1)} %add_convert_fusion), calls=%async_computation | async-start | bytes 1048576 | tf_op jit(solution)/shard_map/all_to_all | solution.py:338
  17.1 7.7 %collective-permute-start.1 = (bf16[128,512]{1,0:T(8,128)(2,1)}, bf16[128,512]{1,0:T(8,128)(2,1)S(1)}, u32[]{:S(2)}, u32[]{:S(2)}) collective-permute-start(bf16[128,512]{1,0:T(8,128)(2,1)} %weight_hbm.1), channel_id=1, source_target_pairs={{1,0},{2,1},{3,2},{0,3},{7,4},{4,5},{5,6},{6,7},{9,8},{10,9},{11,1... | collective-permute-start | bytes 393224 | tf_op jit(solution)/shard_map/ppermute | solution.py:319
  22.0 8.6 %collective-permute-start.2 = (bf16[128,512]{1,0:T(8,128)(2,1)}, bf16[128,512]{1,0:T(8,128)(2,1)S(1)}, u32[]{:S(2)}, u32[]{:S(2)}) collective-permute-start(bf16[128,512]{1,0:T(8,128)(2,1)} %weight_hbm.1), channel_id=1, source_target_pairs={{2,0},{3,1},{0,2},{1,3},{6,4},{7,5},{4,6},{5,7},{10,8},{11,9},{8,1... | collective-permute-start | bytes 393224 | tf_op jit(solution)/shard_map/ppermute | solution.py:328
  74.6 4.2 %collective-permute-start.3 = (bf16[8,384,128]{2,1,0:T(8,128)(2,1)S(1)}, bf16[8,384,128]{2,1,0:T(8,128)(2,1)S(1)}, u32[]{:S(2)}, u32[]{:S(2)}) collective-permute-start(bf16[8,384,128]{2,1,0:T(8,128)(2,1)S(1)} %all_to_all.33.mine), channel_id=1, source_target_pairs={{0,4},{4,0},{1,5},{5,1},{2,6},{6,2},{3,7},{7,3},{8,12},{12,8},{9,1... | collective-permute-start | bytes 2359304 | tf_op jit(solution)/shard_map/ppermute | solution.py:334
  110.6 20.1 %all-to-all-start.4 = ((bf16[8,256,128]{2,1,0:T(8,128)(2,1)}), bf16[8,256,128]{2,1,0:T(8,128)(2,1)S(1)}, u32[]{:S(2)}, u32[]{:S(2)}) async-start(bf16[8,256,128]{2,1,0:T(8,128)(2,1)} %bitcast.4), calls=%async_computation.4 | async-start | bytes 1048576 | tf_op jit(solution)/shard_map/all_to_all | solution.py:338
  114.1 9.4 %collective-permute-start.6 = (f32[16,512]{1,0:T(8,128)S(1)}, f32[16,512]{1,0:T(8,128)S(1)}, u32[]{:S(2)}, u32[]{:S(2)}) collective-permute-start(f32[16,512]{1,0:T(8,128)S(1)} %get-tuple-element.23.refs_0_), channel_id=1, source_target_pairs={{16,0},{24,8},{32,16},{40,24},{48,32},{56,40},{0,48},{8,56},{17,1}... | collective-permute-start | bytes 98312 | tf_op jit(solution)/shard_map/ppermute | solution.py:297
  116.4 7.1 %collective-permute-start.5 = (f32[16,512]{1,0:T(8,128)S(1)}, f32[16,512]{1,0:T(8,128)S(1)}, u32[]{:S(2)}, u32[]{:S(2)}) collective-permute-start(f32[16,512]{1,0:T(8,128)S(1)} %get-tuple-element.23.refs_0_), channel_id=1, source_target_pairs={{56,0},{0,8},{8,16},{16,24},{24,32},{32,40},{40,48},{48,56},{57,1}... | collective-permute-start | bytes 98312 | tf_op jit(solution)/shard_map/ppermute | solution.py:297
  118.5 6.7 %collective-permute-start.4 = (f32[16,512]{1,0:T(8,128)S(1)}, f32[16,512]{1,0:T(8,128)S(1)}, u32[]{:S(2)}, u32[]{:S(2)}) collective-permute-start(f32[16,512]{1,0:T(8,128)S(1)} %get-tuple-element.23.refs_0_), channel_id=1, source_target_pairs={{8,0},{16,8},{24,16},{32,24},{40,32},{48,40},{56,48},{0,56},{9,1},... | collective-permute-start | bytes 98312 | tf_op jit(solution)/shard_map/ppermute | solution.py:297

commit v6 on v5

--- a/solution.py
+++ b/solution.py
@@ -170,12 +170,11 @@
     for y in range(ys):
         for b in range(grains // side):
             payload[y, pl.ds(b * width, width), :] = back[:, b * side : (b + 1) * side]
+        chunk = y % holders
         for k in range(share.shape[1] // side):
-            for c in range(2):
-                rows = c * (width // 2) + y % holders * (part // 2)
-                payload[y, pl.ds(base + k * part + c * (part // 2), part // 2), :] = share[
-                    rows : rows + part // 2, k * side : (k + 1) * side
-                ]
+            payload[y, pl.ds(base + k * part, part), :] = share[
+                chunk * part : (chunk + 1) * part, k * side : (k + 1) * side
+            ]
     take_act.wait()
 
 
@@ -282,30 +281,10 @@
     )(parts)
 
 
-def place_kernel(chunk_at, steps, ids, *refs):
-    pieces, out = refs[:-1], refs[-1]
-    part = pieces[0].shape[0]
-    for step, piece in zip(steps, pieces):
-        start = ((ids[chunk_at] + step) & (len(steps) - 1)) * part
-        out[pl.ds(pl.multiple_of(start, part), part), :] = piece[...]
-
-
-def gather_chunks(ids, chunk_at, piece, holders):
-    steps = [0, 1, -1, 2][:holders]
-    n = lax.axis_size("y")
-    pieces = [piece] + [
-        lax.ppermute(piece, "y", [((i + k) % n, i) for i in range(n)]) for k in steps[1:]
-    ]
-    part, total = piece.shape
-    half = pl.pallas_call(
-        functools.partial(place_kernel, chunk_at, steps),
-        out_shape=jax.ShapeDtypeStruct((part * holders, total), F4),
-        in_specs=[SMEM] + [VMEM] * holders,
-        out_specs=VMEM,
-        compiler_params=pltpu.CompilerParams(vmem_limit_bytes=VMEM_LIMIT),
-        name="place",
-    )(ids, *pieces)
-    return lax.all_gather(half, "core", axis=0, tiled=True)
+def gather_chunks(half, holders):
+    groups = [list(range(y, y + holders)) for y in range(0, lax.axis_size("y"), holders)]
+    chunk = lax.all_gather(half, "core", axis=0, tiled=True)
+    return lax.all_gather(chunk, "y", axis=0, axis_index_groups=groups, tiled=True)
 
 
 def around(x, axis, count):
@@ -369,7 +348,7 @@
     sums = exchange(back, "row")
     grad, share = finish(sums, 1.0 / math.sqrt(nodes), grains, width // holders // 2, total)
     input_grad = exchange(grad, "row")
-    weight_grad = gather_chunks(ids, slots + 1, share, holders)
+    weight_grad = gather_chunks(share, holders)
     return (activation, weight_grad, input_grad)
 
 

time: 133 us -> 133 us (level)
  blocking collectives: 69.7 us -> 83.8 us
  starting transfers between devices: 30.8 us -> 21.5 us
  waiting for transfers between devices: 17.5 us -> 13.2 us
    all_gather x1 -> x2, blocking collectives: 1.99 us -> 16.2 us  [the longest x1 14.3 us: gather_chunks(): lax.all_gather(chunk, 'y', axis=0, axis_index_groups=groups, tiled=True)]
    ppermute x3 -> x0, starting transfers between devices: 9.33 us -> none  [gather_chunks(): lax.ppermute(piece, 'y', [((i + k) % n, i) for i in range(n)])]
    all_to_all x2, waiting for transfers between devices: 7.37 us -> 4.89 us  [exchange(): return lax.all_to_all(x, axis, 0, 0, tiled=True)]
    ppermute x3 -> x0, waiting for transfers between devices: 1.75 us -> none  [gather_chunks(): lax.ppermute(piece, 'y', [((i + k) % n, i) for i in range(n)])]
  transfers between devices with their start and end apart: 9 -> 6, of which waited for: 7 -> 6; matrix products, arithmetic and copies ran while one was open for 0% -> 0% of each run, Pallas kernels for 0% -> 0%
where the time goes in v6:
time: 133 us; the launch traced here: 132 us
  blocking collectives  83.8 us (63%)
  starting transfers between devices  21.5 us (16%)
  waiting for transfers between devices  13.2 us (10%)
  Pallas kernels  9.22 us (7%)
  other arithmetic  1.58 us (1%)
  local copies, waits for them, and re-layouts  1.52 us (1%)
  between operations  1.37 us (1%)
    all_to_all x3, blocking collectives, exchange(): return lax.all_to_all(x, axis, 0, 0, tiled=True)  65.3 us
    all_gather x1, blocking collectives, gather_chunks(): lax.all_gather(chunk, 'y', axis=0, axis_index_groups=groups, tiled=True)  14.3 us
    all_to_all x2, starting transfers between devices, exchange(): return lax.all_to_all(x, axis, 0, 0, tiled=True)  10.9 us
    all_to_all x2, waiting for transfers between devices, exchange(): return lax.all_to_all(x, axis, 0, 0, tiled=True)  4.89 us
    ppermute x1, starting transfers between devices, around(): lax.ppermute(x, names, [((i + k) % n * step + c * core, i * step + c * co...  4.86 us
    ppermute x2, waiting for transfers between devices, swap_cores(): return lax.ppermute(x, 'core', [(0, 1), (1, 0)])  4.13 us
    ppermute x2, starting transfers between devices, swap_cores(): return lax.ppermute(x, 'core', [(0, 1), (1, 0)])  3.83 us
    ppermute x1, waiting for transfers between devices, around(): across = lax.ppermute(x, axis, [((i + 2) % n, i) for i in range(n)])  3.35 us
  transfers between devices with their start and end apart: 6, of which 6 were waited for; matrix products, arithmetic and copies ran while one was open for 0% of the time, Pallas kernels for 0%

profile of v6, /device:TPU:2, one launch (start us, length us, event | category | flops | bytes accessed | tf_op | source)
XLA Modules:
  0.0 132.2 jit_solution(13609492925752098089)
XLA Ops:
  1.3 0.7 compare_select_fusion
  2.0 3.0 %forward_tiles.1 = (f32[8,256,128]{2,1,0:T(8,128)S(1)}, bf16[8,256,128]{2,1,0:T(8,128)(2,1)S(1)}) custom-call(s32[99]{0:T(128)S(1)} %compare_select_fusion.3.ids_any.ids, bf16[96,128,128]{2,1,0:T(8,128)(2,1)} %bitcast.8, bf16[16,128,128]{2,1,0:T(8,128)(2,1)} %bitcast.11), custom_call_target="tpu_custom_call" | custom-call | tf_op jit(solution)/shard_map/forward_tiles/pallas_call | solution.py:85
  5.0 1.9 %collective-permute-start = (bf16[8,256,128]{2,1,0:T(8,128)(2,1)S(1)}, bf16[8,256,128]{2,1,0:T(8,128)(2,1)S(1)}, u32[]{:S(2)}, u32[]{:S(2)}) collective-permute-start(bf16[8,256,128]{2,1,0:T(8,128)(2,1)S(1)} %get-tuple-element.15), channel_id=1, source_target_pairs={{0,4},{4,0},{1,5},{5,1},{2,6},{6,2},{3,7},{7,3},{8,12},{12,8},{9,1... | collective-permute-start | bytes 1572872 | tf_op jit(solution)/shard_map/ppermute | solution.py:313
  6.9 1.9 %collective-permute-done = bf16[8,256,128]{2,1,0:T(8,128)(2,1)S(1)} collective-permute-done((bf16[8,256,128]{2,1,0:T(8,128)(2,1)S(1)}, bf16[8,256,128]{2,1,0:T(8,128)(2,1)S(1)}, u32[]{:S(2)}, u32[]{:S(2)}) %collective-permute-start) | collective-permute-done | bytes 524320 | tf_op jit(solution)/shard_map/ppermute | solution.py:313
  8.8 0.9 add_convert_fusion
  9.7 0.0 copy-start
  9.7 7.4 %all-to-all-start = ((bf16[8,256,128]{2,1,0:T(8,128)(2,1)}), bf16[8,256,128]{2,1,0:T(8,128)(2,1)}, u32[]{:S(2)}, u32[]{:S(2)}) async-start(bf16[8,256,128]{2,1,0:T(8,128)(2,1)} %add_convert_fusion), calls=%async_computation | async-start | bytes 1048576 | tf_op jit(solution)/shard_map/all_to_all | solution.py:317
  17.0 4.9 %collective-permute-start.1 = (bf16[128,512]{1,0:T(8,128)(2,1)}, bf16[128,512]{1,0:T(8,128)(2,1)S(1)}, u32[]{:S(2)}, u32[]{:S(2)}) collective-permute-start(bf16[128,512]{1,0:T(8,128)(2,1)} %weight_hbm.1), channel_id=1, source_target_pairs={{1,0},{2,1},{3,2},{0,3},{7,4},{4,5},{5,6},{6,7},{9,8},{10,9},{11,1... | collective-permute-start | bytes 393224 | tf_op jit(solution)/shard_map/ppermute | solution.py:298
  21.9 1.9 %collective-permute-start.2 = (bf16[128,512]{1,0:T(8,128)(2,1)}, bf16[128,512]{1,0:T(8,128)(2,1)S(1)}, u32[]{:S(2)}, u32[]{:S(2)}) collective-permute-start(bf16[128,512]{1,0:T(8,128)(2,1)} %weight_hbm.1), channel_id=1, source_target_pairs={{2,0},{3,1},{0,2},{1,3},{6,4},{7,5},{4,6},{5,7},{10,8},{11,9},{8,1... | collective-permute-start | bytes 393224 | tf_op jit(solution)/shard_map/ppermute | solution.py:307
  23.8 0.9 collective-permute-done.1
  24.7 2.4 %all-gather = bf16[256,512]{1,0:T(8,128)(2,1)S(1)} all-gather(bf16[128,512]{1,0:T(8,128)(2,1)S(1)} %collective-permute-done.1), channel_id=2, replica_groups=mesh['row'=8,'y'=8,'core'=2,'rep'=4] {'core'}, dimensions={0}, use_global_device_ids=true | all-gather | bytes 393216 | tf_op jit(solution)/shard_map/all_gather | solution.py:308
  27.1 3.4 %collective-permute-done.2.refs_1_ = bf16[128,512]{1,0:T(8,128)(2,1)S(1)} collective-permute-done((bf16[128,512]{1,0:T(8,128)(2,1)}, bf16[128,512]{1,0:T(8,128)(2,1)S(1)}, u32[]{:S(2)}, u32[]{:S(2)}) %collective-permute-start.2) | collective-permute-done | bytes 131104 | tf_op jit(solution)/shard_map/ppermute | solution.py:307
  30.5 4.5 %all-to-all-done.parts_hbm = bf16[8,256,128]{2,1,0:T(8,128)(2,1)} async-done(((bf16[8,256,128]{2,1,0:T(8,128)(2,1)}), bf16[8,256,128]{2,1,0:T(8,128)(2,1)}, u32[]{:S(2)}, u32[]{:S(2)}) %all-to-all-start) | async-done | bytes 524320 | tf_op jit(solution)/shard_map/all_to_all | solution.py:317
  34.9 1.4 %fold.1 = (bf16[4,256,128]{2,1,0:T(8,128)(2,1)S(1)}, bf16[128,512]{1,0:T(8,128)(2,1)S(1)}, bf16[256,512]{1,0:T(8,128)(2,1)S(1)}) custom-call(bf16[8,256,128]{2,1,0:T(8,128)(2,1)} %all-to-all-done.parts_hbm, bf16[128,512]{1,0:T(8,128)(2,1)} %weight_hbm.1, bf16[256,512]{1,0:T(8,128)(2,1)} %cot_hbm.1, bf16[128,512]{1,0:T(8,128)(2,1)S(1)} %get-tuple-element.26.refs_0_, ...), custom_call_target="tpu_custom_call" | custom-call | tf_op jit(solution)/shard_map/fold/pallas_call | solution.py:131
  36.3 11.2 %all_to_all.32.aggs = bf16[4,256,128]{2,1,0:T(8,128)(2,1)S(1)} all-to-all(bf16[4,256,128]{2,1,0:T(8,128)(2,1)S(1)} %get-tuple-element.18), channel_id=1, replica_groups=mesh['row'=8,'y'=8,'core'=2,'rep'=4] {'rep'}, dimensions={0} | all-to-all | bytes 524288 | tf_op jit(solution)/shard_map/all_to_all | solution.py:317
  47.5 1.8 %dense.1 = (bf16[256,512]{1,0:T(8,128)(2,1)}, bf16[8,384,128]{2,1,0:T(8,128)(2,1)S(1)}) custom-call(s32[99]{0:T(128)S(1)} %compare_select_fusion.3.ids_any.ids, bf16[4,256,128]{2,1,0:T(8,128)(2,1)S(1)} %all_to_all.32.aggs, bf16[128,512]{1,0:T(8,128)(2,1)S(1)} %get-tuple-element.19.own_weight, bf16[128,512]{1,0:T(8,128)(2,1)S(1)} %get-tuple-element.26.refs_0_, ...), custom_call_target="tpu_custom_call" | custom-call | tf_op jit(solution)/shard_map/dense/pallas_call | solution.py:185
  49.4 25.2 %all_to_all.33.mine = bf16[8,384,128]{2,1,0:T(8,128)(2,1)S(1)} all-to-all(bf16[8,384,128]{2,1,0:T(8,128)(2,1)S(1)} %get-tuple-element.22), channel_id=1, replica_groups=mesh['row'=8,'y'=8,'core'=2,'rep'=4] {'y'}, dimensions={0} | all-to-all | bytes 1572864 | tf_op jit(solution)/shard_map/all_to_all | solution.py:317
  74.5 1.9 %collective-permute-start.3 = (bf16[8,384,128]{2,1,0:T(8,128)(2,1)S(1)}, bf16[8,384,128]{2,1,0:T(8,128)(2,1)S(1)}, u32[]{:S(2)}, u32[]{:S(2)}) collective-permute-start(bf16[8,384,128]{2,1,0:T(8,128)(2,1)S(1)} %all_to_all.33.mine), channel_id=1, source_target_pairs={{0,4},{4,0},{1,5},{5,1},{2,6},{6,2},{3,7},{7,3},{8,12},{12,8},{9,1... | collective-permute-start | bytes 2359304 | tf_op jit(solution)/shard_map/ppermute | solution.py:313
  76.5 2.3 %collective-permute-done.3.theirs = bf16[8,384,128]{2,1,0:T(8,128)(2,1)S(1)} collective-permute-done((bf16[8,384,128]{2,1,0:T(8,128)(2,1)S(1)}, bf16[8,384,128]{2,1,0:T(8,128)(2,1)S(1)}, u32[]{:S(2)}, u32[]{:S(2)}) %collective-permute-start.3) | collective-permute-done | bytes 786464 | tf_op jit(solution)/shard_map/ppermute | solution.py:313
  78.7 0.0 copy-done
  78.7 2.1 %backward_tiles.1 = bf16[8,320,128]{2,1,0:T(8,128)(2,1)S(1)} custom-call(s32[99]{0:T(128)S(1)} %compare_select_fusion.3.ids_any.ids, bf16[96,128,128]{2,1,0:T(8,128)(2,1)S(1)} %bitcast.9, bf16[8,384,128]{2,1,0:T(8,128)(2,1)S(1)} %all_to_all.33.mine, bf16[8,384,128]{2,1,0:T(8,128)(2,1)S(1)} %collective-permute-done.3.theirs), custom_call_target="tpu_custom_call" | custom-call | tf_op jit(solution)/shard_map/backward_tiles/pallas_call | solution.py:241
  80.8 28.9 %all_to_all.34.parts = bf16[8,320,128]{2,1,0:T(8,128)(2,1)S(1)} all-to-all(bf16[8,320,128]{2,1,0:T(8,128)(2,1)S(1)} %backward_tiles.1), channel_id=1, replica_groups=mesh['row'=8,'y'=8,'core'=2,'rep'=4] {'row'}, dimensions={0} | all-to-all | bytes 1310720 | tf_op jit(solution)/shard_map/all_to_all | solution.py:317
  109.7 1.0 finish.1
  110.6 3.5 %all-to-all-start.4 = ((bf16[8,256,128]{2,1,0:T(8,128)(2,1)}), bf16[8,256,128]{2,1,0:T(8,128)(2,1)S(1)}, u32[]{:S(2)}, u32[]{:S(2)}) async-start(bf16[8,256,128]{2,1,0:T(8,128)(2,1)} %bitcast.4), calls=%async_computation.4 | async-start | bytes 1048576 | tf_op jit(solution)/shard_map/all_to_all | solution.py:317
  114.1 1.9 %all_gather.14 = f32[32,512]{1,0:T(8,128)S(1)} all-gather(f32[16,512]{1,0:T(8,128)S(1)} %get-tuple-element.23), channel_id=1, replica_groups=mesh['row'=8,'y'=8,'core'=2,'rep'=4] {'core'}, dimensions={0}, use_global_device_ids=true | all-gather | bytes 98304 | tf_op jit(solution)/shard_map/all_gather | solution.py:286
  116.0 14.3 %all_gather.15 = f32[128,512]{1,0:T(8,128)S(1)} all-gather(f32[32,512]{1,0:T(8,128)S(1)} %all_gather.14), channel_id=1, replica_groups={{0,8,16,24},{32,40,48,56},{1,9,17,25},{33,41,49,57},{2,10,18,26},{34,42..., dimensions={0}, use_global_device_ids=true | all-gather | bytes 327680 | tf_op jit(solution)/shard_map/all_gather | solution.py:287
  130.3 0.4 all-to-all-done.4
  130.7 0.7 copy.13
  131.4 0.8 copy.14
  (2 shorter events, 0.0 us)
Async XLA Ops:
  5.0 3.8 %collective-permute-start = (bf16[8,256,128]{2,1,0:T(8,128)(2,1)S(1)}, bf16[8,256,128]{2,1,0:T(8,128)(2,1)S(1)}, u32[]{:S(2)}, u32[]{:S(2)}) collective-permute-start(bf16[8,256,128]{2,1,0:T(8,128)(2,1)S(1)} %get-tuple-element.15), channel_id=1, source_target_pairs={{0,4},{4,0},{1,5},{5,1},{2,6},{6,2},{3,7},{7,3},{8,12},{12,8},{9,1... | collective-permute-start | bytes 1572872 | tf_op jit(solution)/shard_map/ppermute | solution.py:313
  9.7 69.0 %copy-start = (bf16[1,1,96,128,128]{4,3,2,1,0:T(8,128)(2,1)S(1)}, bf16[1,1,96,128,128]{4,3,2,1,0:T(8,128)(2,1)}, u32[]{:S(2)}) copy-start(bf16[1,1,96,128,128]{4,3,2,1,0:T(8,128)(2,1)} %param.7) | copy-start | bytes 9437188
  9.7 25.3 %all-to-all-start = ((bf16[8,256,128]{2,1,0:T(8,128)(2,1)}), bf16[8,256,128]{2,1,0:T(8,128)(2,1)}, u32[]{:S(2)}, u32[]{:S(2)}) async-start(bf16[8,256,128]{2,1,0:T(8,128)(2,1)} %add_convert_fusion), calls=%async_computation | async-start | bytes 1048576 | tf_op jit(solution)/shard_map/all_to_all | solution.py:317
  17.0 7.7 %collective-permute-start.1 = (bf16[128,512]{1,0:T(8,128)(2,1)}, bf16[128,512]{1,0:T(8,128)(2,1)S(1)}, u32[]{:S(2)}, u32[]{:S(2)}) collective-permute-start(bf16[128,512]{1,0:T(8,128)(2,1)} %weight_hbm.1), channel_id=1, source_target_pairs={{1,0},{2,1},{3,2},{0,3},{7,4},{4,5},{5,6},{6,7},{9,8},{10,9},{11,1... | collective-permute-start | bytes 393224 | tf_op jit(solution)/shard_map/ppermute | solution.py:298
  21.9 8.6 %collective-permute-start.2 = (bf16[128,512]{1,0:T(8,128)(2,1)}, bf16[128,512]{1,0:T(8,128)(2,1)S(1)}, u32[]{:S(2)}, u32[]{:S(2)}) collective-permute-start(bf16[128,512]{1,0:T(8,128)(2,1)} %weight_hbm.1), channel_id=1, source_target_pairs={{2,0},{3,1},{0,2},{1,3},{6,4},{7,5},{4,6},{5,7},{10,8},{11,9},{8,1... | collective-permute-start | bytes 393224 | tf_op jit(solution)/shard_map/ppermute | solution.py:307
  74.5 4.2 %collective-permute-start.3 = (bf16[8,384,128]{2,1,0:T(8,128)(2,1)S(1)}, bf16[8,384,128]{2,1,0:T(8,128)(2,1)S(1)}, u32[]{:S(2)}, u32[]{:S(2)}) collective-permute-start(bf16[8,384,128]{2,1,0:T(8,128)(2,1)S(1)} %all_to_all.33.mine), channel_id=1, source_target_pairs={{0,4},{4,0},{1,5},{5,1},{2,6},{6,2},{3,7},{7,3},{8,12},{12,8},{9,1... | collective-permute-start | bytes 2359304 | tf_op jit(solution)/shard_map/ppermute | solution.py:313
  110.6 20.1 %all-to-all-start.4 = ((bf16[8,256,128]{2,1,0:T(8,128)(2,1)}), bf16[8,256,128]{2,1,0:T(8,128)(2,1)S(1)}, u32[]{:S(2)}, u32[]{:S(2)}) async-start(bf16[8,256,128]{2,1,0:T(8,128)(2,1)} %bitcast.4), calls=%async_computation.4 | async-start | bytes 1048576 | tf_op jit(solution)/shard_map/all_to_all | solution.py:317

commit v7 on v6

--- a/solution.py
+++ b/solution.py
@@ -149,17 +149,15 @@
 
 def dense_kernel(rep_at, ids, aggs, own_weight, *refs):
     reps, grains, width = aggs.shape
-    others, (cot, act_hbm, payload, act, sem) = refs[: reps - 1], refs[reps - 1 :]
-    take_act = pltpu.make_async_copy(act, act_hbm, sem)
+    others, (cot, act, payload) = refs[: reps - 1], refs[reps - 1 :]
     me = ids[rep_at]
     ys, _, side = payload.shape
     own_agg = aggs[me]
-    hidden = dot(own_agg, own_weight[...])
-    for k, weight in enumerate(others):
-        hidden += dot(aggs[(me + k + 1) % reps], weight[...])
+    near = [own_agg] + [aggs[(me + k) % reps] for k in range(1, reps)]
+    weights = [own_weight[...]] + [weight[...] for weight in others]
+    hidden = dot(jnp.concatenate(near, axis=1), jnp.concatenate(weights, axis=0))
     sigma = jax.nn.sigmoid(hidden)
     act[...] = (hidden * sigma).astype(BF)
-    take_act.start()
     slope = sigma * (1.0 + hidden * (1.0 - sigma))
     grad_hidden = (cot[...].astype(F4) * slope).astype(BF)
     back = dot(own_weight[...], grad_hidden, (((1,), (1,)), ((), ()))).astype(BF)
@@ -175,7 +173,6 @@
             payload[y, pl.ds(base + k * part, part), :] = share[
                 chunk * part : (chunk + 1) * part, k * side : (k + 1) * side
             ]
-    take_act.wait()
 
 
 def dense(ids, aggs, weight, others, cot, ys, side):
@@ -185,18 +182,19 @@
     return pl.pallas_call(
         functools.partial(dense_kernel, ids.shape[0] - 1),
         out_shape=(
-            jax.ShapeDtypeStruct((grains, total), BF),
+            pltpu.VMEM((grains, total), BF),
             jax.ShapeDtypeStruct((ys, rows, side), BF),
         ),
         in_specs=[SMEM] + [VMEM] * (2 + reps),
-        out_specs=(ANY, VMEM),
-        scratch_shapes=[pltpu.VMEM((grains, total), BF), pltpu.SemaphoreType.DMA],
+        out_specs=(VMEM, VMEM),
         compiler_params=pltpu.CompilerParams(vmem_limit_bytes=VMEM_LIMIT),
         name="dense",
     )(ids, aggs, weight, *others, cot)
 
 
-def backward_kernel(parts, ids, tiles, mine, theirs, payload, acc):
+def backward_kernel(parts, ids, tiles, mine, theirs, act, payload, act_hbm, acc, sem):
+    take_act = pltpu.make_async_copy(act, act_hbm, sem)
+    take_act.start()
     acc[...] = jnp.zeros_like(acc)
     side = tiles.shape[1]
     width = acc.shape[1]
@@ -232,21 +230,28 @@
             payload[r, pl.ds(b * width, width), :] = acc[r * per_row + b].astype(BF)
         for k, share in enumerate(shares):
             payload[r, pl.ds(base + k * part, part), :] = share
-
-
-def backward_tiles(ids, values, mine, theirs, rows, col_blocks, parts):
+    take_act.wait()
+
+
+def backward_tiles(ids, values, mine, theirs, act, rows, col_blocks, parts):
     side = values.shape[1]
     base = col_blocks // rows * side
     length = base + (mine.shape[1] - base) // 2
     return pl.pallas_call(
         functools.partial(backward_kernel, parts),
-        out_shape=jax.ShapeDtypeStruct((rows, length, side), BF),
-        in_specs=[SMEM] + [VMEM] * 3,
-        out_specs=VMEM,
-        scratch_shapes=[pltpu.VMEM((col_blocks + 1, side, side), F4)],
+        out_shape=(
+            jax.ShapeDtypeStruct((rows, length, side), BF),
+            jax.ShapeDtypeStruct(act.shape, BF),
+        ),
+        in_specs=[SMEM] + [VMEM] * 3 + [ANY],
+        out_specs=(VMEM, ANY),
+        scratch_shapes=[
+            pltpu.VMEM((col_blocks + 1, side, side), F4),
+            pltpu.SemaphoreType.DMA,
+        ],
         compiler_params=pltpu.CompilerParams(vmem_limit_bytes=VMEM_LIMIT),
         name="backward_tiles",
-    )(ids, values, mine, theirs)
+    )(ids, values, mine, theirs, act)
 
 
 def finish_kernel(scale, parts, grad, share):
@@ -341,10 +346,12 @@
     others = around(lent, "rep", reps)
     copies, near, cot = fold(parts, weight, cotangent, reps, others)
     aggs = exchange(copies, "rep")
-    activation, payload = dense(ids, aggs, near, others, cot, ys, side)
+    act, payload = dense(ids, aggs, near, others, cot, ys, side)
     mine = exchange(payload, "y")
     theirs = swap_cores(mine)
-    back = backward_tiles(ids, values, mine, theirs, rows, col_blocks, total // side)
+    back, activation = backward_tiles(
+        ids, values, mine, theirs, act, rows, col_blocks, total // side
+    )
     sums = exchange(back, "row")
     grad, share = finish(sums, 1.0 / math.sqrt(nodes), grains, width // holders // 2, total)
     input_grad = exchange(grad, "row")

time: 133 us -> 133 us (level)
  no operation moved by 1% of the time
where the time goes in v7:
time: 133 us; the launch traced here: 132 us
  blocking collectives  83.8 us (63%)
  starting transfers between devices  21.5 us (16%)
  waiting for transfers between devices  13.2 us (10%)
  Pallas kernels  9.19 us (7%)
  other arithmetic  1.58 us (1%)
  local copies, waits for them, and re-layouts  1.52 us (1%)
  between operations  1.37 us (1%)
    all_to_all x3, blocking collectives, exchange(): return lax.all_to_all(x, axis, 0, 0, tiled=True)  65.3 us
    all_gather x1, blocking collectives, gather_chunks(): lax.all_gather(chunk, 'y', axis=0, axis_index_groups=groups, tiled=True)  14.3 us
    all_to_all x2, starting transfers between devices, exchange(): return lax.all_to_all(x, axis, 0, 0, tiled=True)  10.9 us
    all_to_all x2, waiting for transfers between devices, exchange(): return lax.all_to_all(x, axis, 0, 0, tiled=True)  4.88 us
    ppermute x1, starting transfers between devices, around(): lax.ppermute(x, names, [((i + k) % n * step + c * core, i * step + c * co...  4.86 us
    ppermute x2, waiting for transfers between devices, swap_cores(): return lax.ppermute(x, 'core', [(0, 1), (1, 0)])  4.13 us
    ppermute x2, starting transfers between devices, swap_cores(): return lax.ppermute(x, 'core', [(0, 1), (1, 0)])  3.83 us
    ppermute x1, waiting for transfers between devices, around(): across = lax.ppermute(x, axis, [((i + 2) % n, i) for i in range(n)])  3.35 us
  transfers between devices with their start and end apart: 6, of which 6 were waited for; matrix products, arithmetic and copies ran while one was open for 0% of the time, Pallas kernels for 0%

profile of v7, /device:TPU:2, one launch (start us, length us, event | category | flops | bytes accessed | tf_op | source)
XLA Modules:
  0.0 132.2 jit_solution(10531195717391487400)
XLA Ops:
  1.3 0.7 compare_select_fusion
  2.0 3.0 %forward_tiles.1 = (f32[8,256,128]{2,1,0:T(8,128)S(1)}, bf16[8,256,128]{2,1,0:T(8,128)(2,1)S(1)}) custom-call(s32[99]{0:T(128)S(1)} %compare_select_fusion.3.ids_any.ids, bf16[96,128,128]{2,1,0:T(8,128)(2,1)} %bitcast.8, bf16[16,128,128]{2,1,0:T(8,128)(2,1)} %bitcast.11), custom_call_target="tpu_custom_call" | custom-call | tf_op jit(solution)/shard_map/forward_tiles/pallas_call | solution.py:85
  5.0 1.9 %collective-permute-start = (bf16[8,256,128]{2,1,0:T(8,128)(2,1)S(1)}, bf16[8,256,128]{2,1,0:T(8,128)(2,1)S(1)}, u32[]{:S(2)}, u32[]{:S(2)}) collective-permute-start(bf16[8,256,128]{2,1,0:T(8,128)(2,1)S(1)} %get-tuple-element.17), channel_id=1, source_target_pairs={{0,4},{4,0},{1,5},{5,1},{2,6},{6,2},{3,7},{7,3},{8,12},{12,8},{9,1... | collective-permute-start | bytes 1572872 | tf_op jit(solution)/shard_map/ppermute | solution.py:318
  6.9 1.9 %collective-permute-done = bf16[8,256,128]{2,1,0:T(8,128)(2,1)S(1)} collective-permute-done((bf16[8,256,128]{2,1,0:T(8,128)(2,1)S(1)}, bf16[8,256,128]{2,1,0:T(8,128)(2,1)S(1)}, u32[]{:S(2)}, u32[]{:S(2)}) %collective-permute-start) | collective-permute-done | bytes 524320 | tf_op jit(solution)/shard_map/ppermute | solution.py:318
  8.8 0.9 add_convert_fusion
  9.7 0.0 copy-start
  9.7 7.4 %all-to-all-start = ((bf16[8,256,128]{2,1,0:T(8,128)(2,1)}), bf16[8,256,128]{2,1,0:T(8,128)(2,1)}, u32[]{:S(2)}, u32[]{:S(2)}) async-start(bf16[8,256,128]{2,1,0:T(8,128)(2,1)} %add_convert_fusion), calls=%async_computation | async-start | bytes 1048576 | tf_op jit(solution)/shard_map/all_to_all | solution.py:322
  17.0 4.9 %collective-permute-start.1 = (bf16[128,512]{1,0:T(8,128)(2,1)}, bf16[128,512]{1,0:T(8,128)(2,1)S(1)}, u32[]{:S(2)}, u32[]{:S(2)}) collective-permute-start(bf16[128,512]{1,0:T(8,128)(2,1)} %weight_hbm.1), channel_id=1, source_target_pairs={{1,0},{2,1},{3,2},{0,3},{7,4},{4,5},{5,6},{6,7},{9,8},{10,9},{11,1... | collective-permute-start | bytes 393224 | tf_op jit(solution)/shard_map/ppermute | solution.py:303
  21.9 1.9 %collective-permute-start.2 = (bf16[128,512]{1,0:T(8,128)(2,1)}, bf16[128,512]{1,0:T(8,128)(2,1)S(1)}, u32[]{:S(2)}, u32[]{:S(2)}) collective-permute-start(bf16[128,512]{1,0:T(8,128)(2,1)} %weight_hbm.1), channel_id=1, source_target_pairs={{2,0},{3,1},{0,2},{1,3},{6,4},{7,5},{4,6},{5,7},{10,8},{11,9},{8,1... | collective-permute-start | bytes 393224 | tf_op jit(solution)/shard_map/ppermute | solution.py:312
  23.8 0.9 collective-permute-done.1
  24.7 2.4 %all-gather = bf16[256,512]{1,0:T(8,128)(2,1)S(1)} all-gather(bf16[128,512]{1,0:T(8,128)(2,1)S(1)} %collective-permute-done.1), channel_id=2, replica_groups=mesh['row'=8,'y'=8,'core'=2,'rep'=4] {'core'}, dimensions={0}, use_global_device_ids=true | all-gather | bytes 393216 | tf_op jit(solution)/shard_map/all_gather | solution.py:313
  27.1 3.4 %collective-permute-done.2.refs_1_ = bf16[128,512]{1,0:T(8,128)(2,1)S(1)} collective-permute-done((bf16[128,512]{1,0:T(8,128)(2,1)}, bf16[128,512]{1,0:T(8,128)(2,1)S(1)}, u32[]{:S(2)}, u32[]{:S(2)}) %collective-permute-start.2) | collective-permute-done | bytes 131104 | tf_op jit(solution)/shard_map/ppermute | solution.py:312
  30.5 4.5 %all-to-all-done.parts_hbm = bf16[8,256,128]{2,1,0:T(8,128)(2,1)} async-done(((bf16[8,256,128]{2,1,0:T(8,128)(2,1)}), bf16[8,256,128]{2,1,0:T(8,128)(2,1)}, u32[]{:S(2)}, u32[]{:S(2)}) %all-to-all-start) | async-done | bytes 524320 | tf_op jit(solution)/shard_map/all_to_all | solution.py:322
  34.9 1.4 %fold.1 = (bf16[4,256,128]{2,1,0:T(8,128)(2,1)S(1)}, bf16[128,512]{1,0:T(8,128)(2,1)S(1)}, bf16[256,512]{1,0:T(8,128)(2,1)S(1)}) custom-call(bf16[8,256,128]{2,1,0:T(8,128)(2,1)} %all-to-all-done.parts_hbm, bf16[128,512]{1,0:T(8,128)(2,1)} %weight_hbm.1, bf16[256,512]{1,0:T(8,128)(2,1)} %cot_hbm.1, bf16[128,512]{1,0:T(8,128)(2,1)S(1)} %get-tuple-element.30.refs_0_, ...), custom_call_target="tpu_custom_call" | custom-call | tf_op jit(solution)/shard_map/fold/pallas_call | solution.py:131
  36.3 11.2 %all_to_all.32.aggs = bf16[4,256,128]{2,1,0:T(8,128)(2,1)S(1)} all-to-all(bf16[4,256,128]{2,1,0:T(8,128)(2,1)S(1)} %get-tuple-element.20), channel_id=1, replica_groups=mesh['row'=8,'y'=8,'core'=2,'rep'=4] {'rep'}, dimensions={0} | all-to-all | bytes 524288 | tf_op jit(solution)/shard_map/all_to_all | solution.py:322
  47.5 1.2 dense.1
  48.8 25.2 %all_to_all.33.mine = bf16[8,384,128]{2,1,0:T(8,128)(2,1)S(1)} all-to-all(bf16[8,384,128]{2,1,0:T(8,128)(2,1)S(1)} %get-tuple-element.23), channel_id=1, replica_groups=mesh['row'=8,'y'=8,'core'=2,'rep'=4] {'y'}, dimensions={0} | all-to-all | bytes 1572864 | tf_op jit(solution)/shard_map/all_to_all | solution.py:322
  73.9 1.9 %collective-permute-start.3 = (bf16[8,384,128]{2,1,0:T(8,128)(2,1)S(1)}, bf16[8,384,128]{2,1,0:T(8,128)(2,1)S(1)}, u32[]{:S(2)}, u32[]{:S(2)}) collective-permute-start(bf16[8,384,128]{2,1,0:T(8,128)(2,1)S(1)} %all_to_all.33.mine), channel_id=1, source_target_pairs={{0,4},{4,0},{1,5},{5,1},{2,6},{6,2},{3,7},{7,3},{8,12},{12,8},{9,1... | collective-permute-start | bytes 2359304 | tf_op jit(solution)/shard_map/ppermute | solution.py:318
  75.8 2.3 %collective-permute-done.3.theirs = bf16[8,384,128]{2,1,0:T(8,128)(2,1)S(1)} collective-permute-done((bf16[8,384,128]{2,1,0:T(8,128)(2,1)S(1)}, bf16[8,384,128]{2,1,0:T(8,128)(2,1)S(1)}, u32[]{:S(2)}, u32[]{:S(2)}) %collective-permute-start.3) | collective-permute-done | bytes 786464 | tf_op jit(solution)/shard_map/ppermute | solution.py:318
  78.1 0.0 copy-done
  78.1 2.7 %backward_tiles.1 = (bf16[8,320,128]{2,1,0:T(8,128)(2,1)S(1)}, bf16[256,512]{1,0:T(8,128)(2,1)}) custom-call(s32[99]{0:T(128)S(1)} %compare_select_fusion.3.ids_any.ids, bf16[96,128,128]{2,1,0:T(8,128)(2,1)S(1)} %bitcast.9, bf16[8,384,128]{2,1,0:T(8,128)(2,1)S(1)} %all_to_all.33.mine, bf16[8,384,128]{2,1,0:T(8,128)(2,1)S(1)} %collective-permute-done.3.theirs, ...), custom_call_target="tpu_custom_call" | custom-call | tf_op jit(solution)/shard_map/backward_tiles/pallas_call | solution.py:240
  80.8 28.9 %all_to_all.34.parts = bf16[8,320,128]{2,1,0:T(8,128)(2,1)S(1)} all-to-all(bf16[8,320,128]{2,1,0:T(8,128)(2,1)S(1)} %get-tuple-element.26), channel_id=1, replica_groups=mesh['row'=8,'y'=8,'core'=2,'rep'=4] {'row'}, dimensions={0} | all-to-all | bytes 1310720 | tf_op jit(solution)/shard_map/all_to_all | solution.py:322
  109.6 1.0 finish.1
  110.6 3.5 %all-to-all-start.4 = ((bf16[8,256,128]{2,1,0:T(8,128)(2,1)}), bf16[8,256,128]{2,1,0:T(8,128)(2,1)S(1)}, u32[]{:S(2)}, u32[]{:S(2)}) async-start(bf16[8,256,128]{2,1,0:T(8,128)(2,1)} %bitcast.4), calls=%async_computation.4 | async-start | bytes 1048576 | tf_op jit(solution)/shard_map/all_to_all | solution.py:322
  114.1 1.9 %all_gather.14 = f32[32,512]{1,0:T(8,128)S(1)} all-gather(f32[16,512]{1,0:T(8,128)S(1)} %get-tuple-element.27), channel_id=1, replica_groups=mesh['row'=8,'y'=8,'core'=2,'rep'=4] {'core'}, dimensions={0}, use_global_device_ids=true | all-gather | bytes 98304 | tf_op jit(solution)/shard_map/all_gather | solution.py:291
  116.0 14.3 %all_gather.15 = f32[128,512]{1,0:T(8,128)S(1)} all-gather(f32[32,512]{1,0:T(8,128)S(1)} %all_gather.14), channel_id=1, replica_groups={{0,8,16,24},{32,40,48,56},{1,9,17,25},{33,41,49,57},{2,10,18,26},{34,42..., dimensions={0}, use_global_device_ids=true | all-gather | bytes 327680 | tf_op jit(solution)/shard_map/all_gather | solution.py:292
  130.3 0.4 all-to-all-done.4
  130.7 0.7 copy.13
  131.4 0.8 copy.14
  (2 shorter events, 0.0 us)
Async XLA Ops:
  5.0 3.8 %collective-permute-start = (bf16[8,256,128]{2,1,0:T(8,128)(2,1)S(1)}, bf16[8,256,128]{2,1,0:T(8,128)(2,1)S(1)}, u32[]{:S(2)}, u32[]{:S(2)}) collective-permute-start(bf16[8,256,128]{2,1,0:T(8,128)(2,1)S(1)} %get-tuple-element.17), channel_id=1, source_target_pairs={{0,4},{4,0},{1,5},{5,1},{2,6},{6,2},{3,7},{7,3},{8,12},{12,8},{9,1... | collective-permute-start | bytes 1572872 | tf_op jit(solution)/shard_map/ppermute | solution.py:318
  9.7 68.4 %copy-start = (bf16[1,1,96,128,128]{4,3,2,1,0:T(8,128)(2,1)S(1)}, bf16[1,1,96,128,128]{4,3,2,1,0:T(8,128)(2,1)}, u32[]{:S(2)}) copy-start(bf16[1,1,96,128,128]{4,3,2,1,0:T(8,128)(2,1)} %param.7) | copy-start | bytes 9437188
  9.7 25.3 %all-to-all-start = ((bf16[8,256,128]{2,1,0:T(8,128)(2,1)}), bf16[8,256,128]{2,1,0:T(8,128)(2,1)}, u32[]{:S(2)}, u32[]{:S(2)}) async-start(bf16[8,256,128]{2,1,0:T(8,128)(2,1)} %add_convert_fusion), calls=%async_computation | async-start | bytes 1048576 | tf_op jit(solution)/shard_map/all_to_all | solution.py:322
  17.0 7.7 %collective-permute-start.1 = (bf16[128,512]{1,0:T(8,128)(2,1)}, bf16[128,512]{1,0:T(8,128)(2,1)S(1)}, u32[]{:S(2)}, u32[]{:S(2)}) collective-permute-start(bf16[128,512]{1,0:T(8,128)(2,1)} %weight_hbm.1), channel_id=1, source_target_pairs={{1,0},{2,1},{3,2},{0,3},{7,4},{4,5},{5,6},{6,7},{9,8},{10,9},{11,1... | collective-permute-start | bytes 393224 | tf_op jit(solution)/shard_map/ppermute | solution.py:303
  21.9 8.6 %collective-permute-start.2 = (bf16[128,512]{1,0:T(8,128)(2,1)}, bf16[128,512]{1,0:T(8,128)(2,1)S(1)}, u32[]{:S(2)}, u32[]{:S(2)}) collective-permute-start(bf16[128,512]{1,0:T(8,128)(2,1)} %weight_hbm.1), channel_id=1, source_target_pairs={{2,0},{3,1},{0,2},{1,3},{6,4},{7,5},{4,6},{5,7},{10,8},{11,9},{8,1... | collective-permute-start | bytes 393224 | tf_op jit(solution)/shard_map/ppermute | solution.py:312
  73.9 4.2 %collective-permute-start.3 = (bf16[8,384,128]{2,1,0:T(8,128)(2,1)S(1)}, bf16[8,384,128]{2,1,0:T(8,128)(2,1)S(1)}, u32[]{:S(2)}, u32[]{:S(2)}) collective-permute-start(bf16[8,384,128]{2,1,0:T(8,128)(2,1)S(1)} %all_to_all.33.mine), channel_id=1, source_target_pairs={{0,4},{4,0},{1,5},{5,1},{2,6},{6,2},{3,7},{7,3},{8,12},{12,8},{9,1... | collective-permute-start | bytes 2359304 | tf_op jit(solution)/shard_map/ppermute | solution.py:318
  110.6 20.1 %all-to-all-start.4 = ((bf16[8,256,128]{2,1,0:T(8,128)(2,1)}), bf16[8,256,128]{2,1,0:T(8,128)(2,1)S(1)}, u32[]{:S(2)}, u32[]{:S(2)}) async-start(bf16[8,256,128]{2,1,0:T(8,128)(2,1)} %bitcast.4), calls=%async_computation.4 | async-start | bytes 1048576 | tf_op jit(solution)/shard_map/all_to_all | solution.py:322

commit v8 on v6

--- a/solution.py
+++ b/solution.py
@@ -154,9 +154,9 @@
     me = ids[rep_at]
     ys, _, side = payload.shape
     own_agg = aggs[me]
-    hidden = dot(own_agg, own_weight[...])
-    for k, weight in enumerate(others):
-        hidden += dot(aggs[(me + k + 1) % reps], weight[...])
+    near = [own_agg] + [aggs[(me + k) % reps] for k in range(1, reps)]
+    weights = [own_weight[...]] + [weight[...] for weight in others]
+    hidden = dot(jnp.concatenate(near, axis=1), jnp.concatenate(weights, axis=0))
     sigma = jax.nn.sigmoid(hidden)
     act[...] = (hidden * sigma).astype(BF)
     take_act.start()

time: 133 us -> 133 us (level)
  no operation moved by 1% of the time
where the time goes in v8:
time: 133 us; the launch traced here: 132 us
  blocking collectives  83.8 us (63%)
  starting transfers between devices  21.5 us (16%)
  waiting for transfers between devices  13.2 us (10%)
  Pallas kernels  9.14 us (7%)
  other arithmetic  1.58 us (1%)
  local copies, waits for them, and re-layouts  1.52 us (1%)
  between operations  1.37 us (1%)
    all_to_all x3, blocking collectives, exchange(): return lax.all_to_all(x, axis, 0, 0, tiled=True)  65.3 us
    all_gather x1, blocking collectives, gather_chunks(): lax.all_gather(chunk, 'y', axis=0, axis_index_groups=groups, tiled=True)  14.3 us
    all_to_all x2, starting transfers between devices, exchange(): return lax.all_to_all(x, axis, 0, 0, tiled=True)  10.9 us
    all_to_all x2, waiting for transfers between devices, exchange(): return lax.all_to_all(x, axis, 0, 0, tiled=True)  4.87 us
    ppermute x1, starting transfers between devices, around(): lax.ppermute(x, names, [((i + k) % n * step + c * core, i * step + c * co...  4.87 us
    ppermute x2, waiting for transfers between devices, swap_cores(): return lax.ppermute(x, 'core', [(0, 1), (1, 0)])  4.13 us
    ppermute x2, starting transfers between devices, swap_cores(): return lax.ppermute(x, 'core', [(0, 1), (1, 0)])  3.83 us
    ppermute x1, waiting for transfers between devices, around(): across = lax.ppermute(x, axis, [((i + 2) % n, i) for i in range(n)])  3.35 us
  transfers between devices with their start and end apart: 6, of which 6 were waited for; matrix products, arithmetic and copies ran while one was open for 0% of the time, Pallas kernels for 0%

profile of v8, /device:TPU:2, one launch (start us, length us, event | category | flops | bytes accessed | tf_op | source)
XLA Modules:
  0.0 132.1 jit_solution(5448369545462056616)
XLA Ops:
  1.3 0.7 compare_select_fusion
  2.0 3.0 %forward_tiles.1 = (f32[8,256,128]{2,1,0:T(8,128)S(1)}, bf16[8,256,128]{2,1,0:T(8,128)(2,1)S(1)}) custom-call(s32[99]{0:T(128)S(1)} %compare_select_fusion.3.ids_any.ids, bf16[96,128,128]{2,1,0:T(8,128)(2,1)} %bitcast.8, bf16[16,128,128]{2,1,0:T(8,128)(2,1)} %bitcast.11), custom_call_target="tpu_custom_call" | custom-call | tf_op jit(solution)/shard_map/forward_tiles/pallas_call | solution.py:85
  5.0 1.9 %collective-permute-start = (bf16[8,256,128]{2,1,0:T(8,128)(2,1)S(1)}, bf16[8,256,128]{2,1,0:T(8,128)(2,1)S(1)}, u32[]{:S(2)}, u32[]{:S(2)}) collective-permute-start(bf16[8,256,128]{2,1,0:T(8,128)(2,1)S(1)} %get-tuple-element.15), channel_id=1, source_target_pairs={{0,4},{4,0},{1,5},{5,1},{2,6},{6,2},{3,7},{7,3},{8,12},{12,8},{9,1... | collective-permute-start | bytes 1572872 | tf_op jit(solution)/shard_map/ppermute | solution.py:313
  6.9 1.9 %collective-permute-done = bf16[8,256,128]{2,1,0:T(8,128)(2,1)S(1)} collective-permute-done((bf16[8,256,128]{2,1,0:T(8,128)(2,1)S(1)}, bf16[8,256,128]{2,1,0:T(8,128)(2,1)S(1)}, u32[]{:S(2)}, u32[]{:S(2)}) %collective-permute-start) | collective-permute-done | bytes 524320 | tf_op jit(solution)/shard_map/ppermute | solution.py:313
  8.8 0.9 add_convert_fusion
  9.7 0.0 copy-start
  9.7 7.4 %all-to-all-start = ((bf16[8,256,128]{2,1,0:T(8,128)(2,1)}), bf16[8,256,128]{2,1,0:T(8,128)(2,1)}, u32[]{:S(2)}, u32[]{:S(2)}) async-start(bf16[8,256,128]{2,1,0:T(8,128)(2,1)} %add_convert_fusion), calls=%async_computation | async-start | bytes 1048576 | tf_op jit(solution)/shard_map/all_to_all | solution.py:317
  17.0 4.9 %collective-permute-start.1 = (bf16[128,512]{1,0:T(8,128)(2,1)}, bf16[128,512]{1,0:T(8,128)(2,1)S(1)}, u32[]{:S(2)}, u32[]{:S(2)}) collective-permute-start(bf16[128,512]{1,0:T(8,128)(2,1)} %weight_hbm.1), channel_id=1, source_target_pairs={{1,0},{2,1},{3,2},{0,3},{7,4},{4,5},{5,6},{6,7},{9,8},{10,9},{11,1... | collective-permute-start | bytes 393224 | tf_op jit(solution)/shard_map/ppermute | solution.py:298
  21.9 1.9 %collective-permute-start.2 = (bf16[128,512]{1,0:T(8,128)(2,1)}, bf16[128,512]{1,0:T(8,128)(2,1)S(1)}, u32[]{:S(2)}, u32[]{:S(2)}) collective-permute-start(bf16[128,512]{1,0:T(8,128)(2,1)} %weight_hbm.1), channel_id=1, source_target_pairs={{2,0},{3,1},{0,2},{1,3},{6,4},{7,5},{4,6},{5,7},{10,8},{11,9},{8,1... | collective-permute-start | bytes 393224 | tf_op jit(solution)/shard_map/ppermute | solution.py:307
  23.8 0.9 collective-permute-done.1
  24.7 2.4 %all-gather = bf16[256,512]{1,0:T(8,128)(2,1)S(1)} all-gather(bf16[128,512]{1,0:T(8,128)(2,1)S(1)} %collective-permute-done.1), channel_id=2, replica_groups=mesh['row'=8,'y'=8,'core'=2,'rep'=4] {'core'}, dimensions={0}, use_global_device_ids=true | all-gather | bytes 393216 | tf_op jit(solution)/shard_map/all_gather | solution.py:308
  27.1 3.4 %collective-permute-done.2.refs_1_ = bf16[128,512]{1,0:T(8,128)(2,1)S(1)} collective-permute-done((bf16[128,512]{1,0:T(8,128)(2,1)}, bf16[128,512]{1,0:T(8,128)(2,1)S(1)}, u32[]{:S(2)}, u32[]{:S(2)}) %collective-permute-start.2) | collective-permute-done | bytes 131104 | tf_op jit(solution)/shard_map/ppermute | solution.py:307
  30.5 4.4 %all-to-all-done.parts_hbm = bf16[8,256,128]{2,1,0:T(8,128)(2,1)} async-done(((bf16[8,256,128]{2,1,0:T(8,128)(2,1)}), bf16[8,256,128]{2,1,0:T(8,128)(2,1)}, u32[]{:S(2)}, u32[]{:S(2)}) %all-to-all-start) | async-done | bytes 524320 | tf_op jit(solution)/shard_map/all_to_all | solution.py:317
  34.9 1.4 %fold.1 = (bf16[4,256,128]{2,1,0:T(8,128)(2,1)S(1)}, bf16[128,512]{1,0:T(8,128)(2,1)S(1)}, bf16[256,512]{1,0:T(8,128)(2,1)S(1)}) custom-call(bf16[8,256,128]{2,1,0:T(8,128)(2,1)} %all-to-all-done.parts_hbm, bf16[128,512]{1,0:T(8,128)(2,1)} %weight_hbm.1, bf16[256,512]{1,0:T(8,128)(2,1)} %cot_hbm.1, bf16[128,512]{1,0:T(8,128)(2,1)S(1)} %get-tuple-element.26.refs_0_, ...), custom_call_target="tpu_custom_call" | custom-call | tf_op jit(solution)/shard_map/fold/pallas_call | solution.py:131
  36.3 11.2 %all_to_all.32.aggs = bf16[4,256,128]{2,1,0:T(8,128)(2,1)S(1)} all-to-all(bf16[4,256,128]{2,1,0:T(8,128)(2,1)S(1)} %get-tuple-element.18), channel_id=1, replica_groups=mesh['row'=8,'y'=8,'core'=2,'rep'=4] {'rep'}, dimensions={0} | all-to-all | bytes 524288 | tf_op jit(solution)/shard_map/all_to_all | solution.py:317
  47.5 1.8 %dense.1 = (bf16[256,512]{1,0:T(8,128)(2,1)}, bf16[8,384,128]{2,1,0:T(8,128)(2,1)S(1)}) custom-call(s32[99]{0:T(128)S(1)} %compare_select_fusion.3.ids_any.ids, bf16[4,256,128]{2,1,0:T(8,128)(2,1)S(1)} %all_to_all.32.aggs, bf16[128,512]{1,0:T(8,128)(2,1)S(1)} %get-tuple-element.19.own_weight, bf16[128,512]{1,0:T(8,128)(2,1)S(1)} %get-tuple-element.26.refs_0_, ...), custom_call_target="tpu_custom_call" | custom-call | tf_op jit(solution)/shard_map/dense/pallas_call | solution.py:185
  49.3 25.2 %all_to_all.33.mine = bf16[8,384,128]{2,1,0:T(8,128)(2,1)S(1)} all-to-all(bf16[8,384,128]{2,1,0:T(8,128)(2,1)S(1)} %get-tuple-element.22), channel_id=1, replica_groups=mesh['row'=8,'y'=8,'core'=2,'rep'=4] {'y'}, dimensions={0} | all-to-all | bytes 1572864 | tf_op jit(solution)/shard_map/all_to_all | solution.py:317
  74.5 1.9 %collective-permute-start.3 = (bf16[8,384,128]{2,1,0:T(8,128)(2,1)S(1)}, bf16[8,384,128]{2,1,0:T(8,128)(2,1)S(1)}, u32[]{:S(2)}, u32[]{:S(2)}) collective-permute-start(bf16[8,384,128]{2,1,0:T(8,128)(2,1)S(1)} %all_to_all.33.mine), channel_id=1, source_target_pairs={{0,4},{4,0},{1,5},{5,1},{2,6},{6,2},{3,7},{7,3},{8,12},{12,8},{9,1... | collective-permute-start | bytes 2359304 | tf_op jit(solution)/shard_map/ppermute | solution.py:313
  76.4 2.3 %collective-permute-done.3.theirs = bf16[8,384,128]{2,1,0:T(8,128)(2,1)S(1)} collective-permute-done((bf16[8,384,128]{2,1,0:T(8,128)(2,1)S(1)}, bf16[8,384,128]{2,1,0:T(8,128)(2,1)S(1)}, u32[]{:S(2)}, u32[]{:S(2)}) %collective-permute-start.3) | collective-permute-done | bytes 786464 | tf_op jit(solution)/shard_map/ppermute | solution.py:313
  78.6 0.0 copy-done
  78.6 2.1 %backward_tiles.1 = bf16[8,320,128]{2,1,0:T(8,128)(2,1)S(1)} custom-call(s32[99]{0:T(128)S(1)} %compare_select_fusion.3.ids_any.ids, bf16[96,128,128]{2,1,0:T(8,128)(2,1)S(1)} %bitcast.9, bf16[8,384,128]{2,1,0:T(8,128)(2,1)S(1)} %all_to_all.33.mine, bf16[8,384,128]{2,1,0:T(8,128)(2,1)S(1)} %collective-permute-done.3.theirs), custom_call_target="tpu_custom_call" | custom-call | tf_op jit(solution)/shard_map/backward_tiles/pallas_call | solution.py:241
  80.7 28.9 %all_to_all.34.parts = bf16[8,320,128]{2,1,0:T(8,128)(2,1)S(1)} all-to-all(bf16[8,320,128]{2,1,0:T(8,128)(2,1)S(1)} %backward_tiles.1), channel_id=1, replica_groups=mesh['row'=8,'y'=8,'core'=2,'rep'=4] {'row'}, dimensions={0} | all-to-all | bytes 1310720 | tf_op jit(solution)/shard_map/all_to_all | solution.py:317
  109.6 1.0 finish.1
  110.5 3.5 %all-to-all-start.4 = ((bf16[8,256,128]{2,1,0:T(8,128)(2,1)}), bf16[8,256,128]{2,1,0:T(8,128)(2,1)S(1)}, u32[]{:S(2)}, u32[]{:S(2)}) async-start(bf16[8,256,128]{2,1,0:T(8,128)(2,1)} %bitcast.4), calls=%async_computation.4 | async-start | bytes 1048576 | tf_op jit(solution)/shard_map/all_to_all | solution.py:317
  114.0 1.9 %all_gather.14 = f32[32,512]{1,0:T(8,128)S(1)} all-gather(f32[16,512]{1,0:T(8,128)S(1)} %get-tuple-element.23), channel_id=1, replica_groups=mesh['row'=8,'y'=8,'core'=2,'rep'=4] {'core'}, dimensions={0}, use_global_device_ids=true | all-gather | bytes 98304 | tf_op jit(solution)/shard_map/all_gather | solution.py:286
  115.9 14.3 %all_gather.15 = f32[128,512]{1,0:T(8,128)S(1)} all-gather(f32[32,512]{1,0:T(8,128)S(1)} %all_gather.14), channel_id=1, replica_groups={{0,8,16,24},{32,40,48,56},{1,9,17,25},{33,41,49,57},{2,10,18,26},{34,42..., dimensions={0}, use_global_device_ids=true | all-gather | bytes 327680 | tf_op jit(solution)/shard_map/all_gather | solution.py:287
  130.2 0.4 all-to-all-done.4
  130.6 0.7 copy.13
  131.4 0.8 copy.14
  (2 shorter events, 0.0 us)
Async XLA Ops:
  5.0 3.8 %collective-permute-start = (bf16[8,256,128]{2,1,0:T(8,128)(2,1)S(1)}, bf16[8,256,128]{2,1,0:T(8,128)(2,1)S(1)}, u32[]{:S(2)}, u32[]{:S(2)}) collective-permute-start(bf16[8,256,128]{2,1,0:T(8,128)(2,1)S(1)} %get-tuple-element.15), channel_id=1, source_target_pairs={{0,4},{4,0},{1,5},{5,1},{2,6},{6,2},{3,7},{7,3},{8,12},{12,8},{9,1... | collective-permute-start | bytes 1572872 | tf_op jit(solution)/shard_map/ppermute | solution.py:313
  9.7 69.0 %copy-start = (bf16[1,1,96,128,128]{4,3,2,1,0:T(8,128)(2,1)S(1)}, bf16[1,1,96,128,128]{4,3,2,1,0:T(8,128)(2,1)}, u32[]{:S(2)}) copy-start(bf16[1,1,96,128,128]{4,3,2,1,0:T(8,128)(2,1)} %param.7) | copy-start | bytes 9437188
  9.7 25.3 %all-to-all-start = ((bf16[8,256,128]{2,1,0:T(8,128)(2,1)}), bf16[8,256,128]{2,1,0:T(8,128)(2,1)}, u32[]{:S(2)}, u32[]{:S(2)}) async-start(bf16[8,256,128]{2,1,0:T(8,128)(2,1)} %add_convert_fusion), calls=%async_computation | async-start | bytes 1048576 | tf_op jit(solution)/shard_map/all_to_all | solution.py:317
  17.0 7.7 %collective-permute-start.1 = (bf16[128,512]{1,0:T(8,128)(2,1)}, bf16[128,512]{1,0:T(8,128)(2,1)S(1)}, u32[]{:S(2)}, u32[]{:S(2)}) collective-permute-start(bf16[128,512]{1,0:T(8,128)(2,1)} %weight_hbm.1), channel_id=1, source_target_pairs={{1,0},{2,1},{3,2},{0,3},{7,4},{4,5},{5,6},{6,7},{9,8},{10,9},{11,1... | collective-permute-start | bytes 393224 | tf_op jit(solution)/shard_map/ppermute | solution.py:298
  21.9 8.6 %collective-permute-start.2 = (bf16[128,512]{1,0:T(8,128)(2,1)}, bf16[128,512]{1,0:T(8,128)(2,1)S(1)}, u32[]{:S(2)}, u32[]{:S(2)}) collective-permute-start(bf16[128,512]{1,0:T(8,128)(2,1)} %weight_hbm.1), channel_id=1, source_target_pairs={{2,0},{3,1},{0,2},{1,3},{6,4},{7,5},{4,6},{5,7},{10,8},{11,9},{8,1... | collective-permute-start | bytes 393224 | tf_op jit(solution)/shard_map/ppermute | solution.py:307
  74.5 4.2 %collective-permute-start.3 = (bf16[8,384,128]{2,1,0:T(8,128)(2,1)S(1)}, bf16[8,384,128]{2,1,0:T(8,128)(2,1)S(1)}, u32[]{:S(2)}, u32[]{:S(2)}) collective-permute-start(bf16[8,384,128]{2,1,0:T(8,128)(2,1)S(1)} %all_to_all.33.mine), channel_id=1, source_target_pairs={{0,4},{4,0},{1,5},{5,1},{2,6},{6,2},{3,7},{7,3},{8,12},{12,8},{9,1... | collective-permute-start | bytes 2359304 | tf_op jit(solution)/shard_map/ppermute | solution.py:313
  110.5 20.1 %all-to-all-start.4 = ((bf16[8,256,128]{2,1,0:T(8,128)(2,1)}), bf16[8,256,128]{2,1,0:T(8,128)(2,1)S(1)}, u32[]{:S(2)}, u32[]{:S(2)}) async-start(bf16[8,256,128]{2,1,0:T(8,128)(2,1)} %bitcast.4), calls=%async_computation.4 | async-start | bytes 1048576 | tf_op jit(solution)/shard_map/all_to_all | solution.py:317
